TPU v7x, 32 devices: a whole 2x2x4 slice. The times are simulated.
32 devices in a mesh: wide: 8 (over y, x, core), narrow: 4 (over z).
Axes of the slice: x: 2, y: 2, z: 4, core: 2. Of those that a mesh axis runs over, the one named last changes fastest.
Arguments:
- features: bfloat16 [16384, 512], P(('wide', 'narrow')), may hold values from -6 to 6
- stripe_owner: int32 [4, 2], replicated, may hold values from 0 to 7
- dense_weight: int32 [16384, 1024], P(('wide', 'narrow')), may hold values from 0 to 3
- sparse_weight: int32 [32, 4, 128, 128], P(('wide', 'narrow')), may hold values from 0 to 3
- send_blocks: int32 [32, 4, 2], P(('wide', 'narrow')), may hold values from -1 to 3, as said below
- target_block: int32 [32, 4, 2], P(('wide', 'narrow')), may hold values from 0 to 3
- first_weight: bfloat16 [512, 2048], P('wide'), may hold values from -0.25 to 0.25
- second_weight: bfloat16 [2048, 512], P('wide'), may hold values from -0.125 to 0.125
Outputs:
- updated: bfloat16 [16384, 512], P(('wide', 'narrow'))
Inputs may be any that keep to these rules, and one draw needn't show every extreme that they name: `send_blocks`: entry [d, p, s] names a local row block of device d for slot s to partition p of d's wide group, -1 marks an empty slot, filled slots come first; in every wide group one partition receives 2 blocks from every member.
All inputs are finite; a program needn't handle non-finite values.
Results may differ from a plain program's by a relative error of at most 0.0057.
Values may be sent and summed in bfloat16 or wider, within the bound.
No kernel may reach another device: no remote copies, remote signals or barrier semaphores. Data moves between devices by JAX's collectives and lax.ppermute only.
A program may use at most 128 MiB of HBM per device.

v0:
```python
import jax
import jax.numpy as jnp
from jax import lax
from jax.sharding import PartitionSpec as P


def spread(block, axis, holder):
    block = jnp.where(lax.axis_index(axis) == holder, block, jnp.zeros_like(block))
    return lax.psum(block, axis)


def tile_products(tile_weights, received):
    carried, present = received
    products = jnp.einsum(
        "pij,pcjd->pcid", tile_weights, carried, preferred_element_type=jnp.float32
    )
    return (products, present)


def add_rows(left, portion):
    return jnp.dot(left, portion, preferred_element_type=jnp.float32)


def shards(
    features,
    stripe_owner,
    dense_weight,
    sparse_weight,
    send_blocks,
    target_block,
    first_weight,
    second_weight,
):
    row_count, feature_width = features.shape
    part_count = sparse_weight.shape[1]
    block_rows = sparse_weight.shape[2]
    blocks_dev = row_count // block_rows
    stripe_count = stripe_owner.shape[1]
    narrow_index = lax.axis_index("narrow")
    owners = lax.dynamic_index_in_dim(stripe_owner, narrow_index, 0, keepdims=False)
    pieces = []
    for stripe_index in range(stripe_count):
        pieces.append(spread(features, "wide", owners[stripe_index]))
    stripes = jnp.concatenate(pieces, 0)
    dense_sum = jnp.dot(
        dense_weight.astype(jnp.bfloat16), stripes, preferred_element_type=jnp.float32
    )
    tile_weights = sparse_weight[0].astype(jnp.bfloat16)
    lists_sent = send_blocks.astype(jnp.bfloat16)
    every_rows, every_lists = (
        lax.all_gather(features, "narrow", axis=0, tiled=True),
        lax.all_gather(lists_sent, "narrow", axis=0, tiled=True),
    )
    mine = lax.dynamic_index_in_dim(every_lists, narrow_index, 1, keepdims=False).astype(jnp.int32)
    present = mine >= 0
    block_grid = every_rows.reshape(part_count, blocks_dev, block_rows, feature_width)
    chosen = block_grid[jnp.arange(part_count)[:, None], jnp.maximum(mine, 0)]
    chosen = jnp.where(present[:, :, None, None], chosen, jnp.zeros((), jnp.bfloat16))
    products, arrived = tile_products(tile_weights, (chosen, present.astype(jnp.bfloat16)))
    highest = lax.Precision.HIGHEST
    routed = (target_block[0][:, :, None] == jnp.arange(blocks_dev)[None, None, :]) & (
        arrived[:, :, None] > 0.5
    )
    routed = routed.astype(jnp.float32)
    sparse_sum = jnp.einsum("pcb,pcid->bid", routed, products, precision=highest).reshape(
        row_count, feature_width
    )
    row_weight = jnp.sum(sparse_weight[0], axis=2).astype(jnp.float32)
    sparse_degree = jnp.einsum("pcb,pi->bi", routed, row_weight, precision=highest).reshape(
        row_count
    )
    degree = 1.0 + jnp.sum(dense_weight, axis=1).astype(jnp.float32) + sparse_degree
    combined = (
        features.astype(jnp.float32) + (dense_sum + sparse_sum) / jnp.sqrt(degree)[:, None]
    ).astype(jnp.bfloat16)
    gated = add_rows(combined, lax.all_gather(first_weight, "wide", axis=0, tiled=True))
    hidden = jax.nn.relu(gated).astype(jnp.bfloat16)
    updated = add_rows(hidden, lax.all_gather(second_weight, "wide", axis=0, tiled=True))
    return updated.astype(jnp.bfloat16)


def solution(mesh):
    placed = (
        P(("wide", "narrow"), None),
        P(),
        P(("wide", "narrow"), None),
        P(("wide", "narrow"), None, None, None),
        P(("wide", "narrow"), None, None),
        P(("wide", "narrow"), None, None),
        P("wide", None),
        P("wide", None),
    )
    return jax.shard_map(
        shards, mesh=mesh, in_specs=placed, out_specs=P(("wide", "narrow"), None), check_vma=False
    )
```

profile of v0, /device:TPU:0, one launch (start us, length us, event | category | flops | bytes accessed | tf_op | source)
XLA Modules:
  0.0 128.5 jit_solution(2431664640445505962)
XLA Ops:
  7.4 0.7 all-gather.4.cloned.1.call-update
  8.1 0.0 all-reduce.3.cloned.1.call-start
  8.2 0.1 constant_dynamic-slice_fusion.1
  8.2 0.6 fusion.33
  10.1 2.3 %broadcast_select_fusion.1 = (bf16[512,512]{1,0:T(8,128)(2,1)}, bf16[512,512]{1,0:T(8,128)(2,1)}) fusion(bf16[512,512]{1,0:T(8,128)(2,1)} %param.8, pred[]{:T(512)S(6)} %eq.21, pred[]{:T(512)S(6)} %eq.22), kind=kLoop, calls=%fused_computation.22 | loop fusion | flops 524288 | bytes 1572866 | tf_op jit(solution)/shard_map/jit(_where)/select_n | solution.py:8
  12.4 0.0 all-gather.6.cloned.1.call-start
  12.5 0.7 all-gather.6.cloned.1.call-update
  13.2 0.7 all-gather.8.cloned.1.call-update
  13.9 12.7 %all_gather.12 = bf16[4,4,2]{1,2,0:T(2,128)(2,1)S(1)} all-gather(bf16[1,4,2]{1,2,0:T(2,128)(2,1)S(1)} %convert_element_type.65), channel_id=1, replica_groups=mesh['wide'=8,'narrow'=4] {'narrow'}, dimensions={0}, use_global_device_ids=true | all-gather | bytes 80 | tf_op jit(solution)/shard_map/all_gather | solution.py:52
  26.6 1.0 copy.24
  27.6 0.1 constant_dynamic-slice_fusion
  27.7 0.1 copy.35
  27.8 0.1 copy.26
  28.0 0.1 copy.28
  28.0 0.1 reshape.62
  28.1 0.1 copy.27
  28.3 0.2 reduce_sum.27
  28.4 0.1 reduce_sum.29
  28.6 0.1 fusion.5
  28.7 29.7 %all-gather.4.cloned.1.call-done = bf16[2048,512]{1,0:T(8,128)(2,1)} async-done(((bf16[512,512]{1,0:T(8,128)(2,1)}), bf16[2048,512]{1,0:T(8,128)(2,1)}) %all-gather.4.cloned.1.call-update) | async-done | bytes 2097168 | tf_op jit(solution)/shard_map/all_gather | solution.py:51
  58.4 2.3 %gather_fusion = bf16[8,128,512]{2,1,0:T(8,128)(2,1)S(1)} fusion(bf16[4,4,128,512]{3,2,1,0:T(8,128)(2,1)} %bitcast.53, s32[8]{0:T(128)S(1)} %reshape.62), kind=kCustom, calls=%fused_computation | custom fusion | bytes 2097216 | tf_op jit(solution)/shard_map/gather | solution.py:57
  60.7 0.7 copy.29
  61.4 0.5 convolution_bitcast_fusion
  61.9 2.1 %copy.30 = f32[4,2,128,512]{3,0,1,2:T(4,128)} copy(f32[4,2,128,512]{2,3,1,0:T(8,128)S(1)} %convolution_bitcast_fusion) | data formatting | bytes 4194304 | tf_op jit(solution)/shard_map/pij,pcjd->pcid/transpose | solution.py:14
  64.0 3.4 %convolution_bitcast_fusion.2 = f32[4,128,512]{2,0,1:T(4,128)S(1)} fusion(f32[4,2,128,512]{3,0,1,2:T(4,128)} %copy.30, s32[4,2]{0,1:T(2,128)S(1)} %bitcast.55, pred[4,2]{0,1:T(4,128)(4,1)S(1)} %copy.27), kind=kOutput, calls=%fused_computation.6 | convolution fusion | flops 25165888 | bytes 3145768 | tf_op jit(solution)/shard_map/pcb,pcid->bid/dot_general | solution.py:65
  67.4 0.3 copy.31
  67.7 1.3 %copy.32 = f32[512,512]{0,1:T(8,128)} copy(f32[512,512]{1,0:T(8,128)S(1)} %bitcast.52) | data formatting | bytes 2097152 | tf_op jit(solution)/shard_map/reshape | solution.py:65
  69.1 3.9 %all-reduce.3.cloned.1.call-done = (bf16[512,512]{1,0:T(8,128)(2,1)}, bf16[512,512]{1,0:T(8,128)(2,1)}) async-done(((bf16[512,512]{1,0:T(8,128)(2,1)}, bf16[512,512]{1,0:T(8,128)(2,1)}), (bf16[512,512]{1,0:T(8,128)(2,1)}, bf16[512,512]{1,0:T(8,128)(2,1)})) %all-reduce.3.cloned.1.call-update) | async-done | bytes 1048592 | tf_op jit(solution)/shard_map/psum | solution.py:9
  73.0 14.2 %all-gather.6.cloned.1.call-done = bf16[512,2048]{1,0:T(8,128)(2,1)} async-done(((bf16[64,2048]{1,0:T(8,128)(2,1)}), bf16[512,2048]{1,0:T(8,128)(2,1)}) %all-gather.6.cloned.1.call-update) | async-done | bytes 2097168 | tf_op jit(solution)/shard_map/all_gather | solution.py:76
  87.2 5.7 %maximum_convert_fusion = bf16[512,2048]{1,0:T(8,128)(2,1)} fusion(bf16[512,2048]{1,0:T(8,128)(2,1)} %all-gather.6.cloned.1.call-done, f32[512,512]{0,1:T(8,128)} %copy.32, bf16[512,512]{1,0:T(8,128)(2,1)} %get-tuple-element.5, bf16[512,512]{1,0:T(8,128)(2,1)} %get-tuple-element.6, s32[512,1024]{1,0:T(8,128)S(1)} %copy-done.3, bf16[512,512]{0,1:T(8,128)(2,1)} %copy.24, ...), kind=kOutput, calls=%fused_computation.1 | convolution fusion | flops 1616642048 | bytes 8914944 | tf_op jit(solution)/shard_map/dot_general | solution.py:21
  93.0 24.1 %all-gather.8.cloned.1.call-done = bf16[2048,512]{1,0:T(8,128)(2,1)} async-done(((bf16[256,512]{1,0:T(8,128)(2,1)}), bf16[2048,512]{1,0:T(8,128)(2,1)}) %all-gather.8.cloned.1.call-update) | async-done | bytes 2097168 | tf_op jit(solution)/shard_map/all_gather | solution.py:78
  117.1 4.3 %convolution_convert_fusion = bf16[512,512]{1,0:T(8,128)(2,1)} fusion(bf16[512,2048]{1,0:T(8,128)(2,1)} %maximum_convert_fusion, bf16[2048,512]{1,0:T(8,128)(2,1)} %all-gather.8.cloned.1.call-done), kind=kOutput, calls=%fused_computation.8 | convolution fusion | flops 1074003968 | bytes 4718592 | tf_op jit(solution)/shard_map/dot_general | solution.py:21
  (22 shorter events, 0.1 us)
Async XLA Ops:
  7.4 0.8 copy-start
  7.4 19.2 %copy-start.1 = (bf16[512,512]{1,0:T(8,128)(2,1)S(1)}, bf16[512,512]{1,0:T(8,128)(2,1)}, u32[]{:S(2)}) copy-start(bf16[512,512]{1,0:T(8,128)(2,1)} %param.8) | copy-start | bytes 1572868
  7.4 6.5 %copy-start.6 = (s32[1,4,2]{1,2,0:T(2,128)S(1)}, s32[1,4,2]{1,2,0:T(2,128)}, u32[]{:S(2)}) copy-start(s32[1,4,2]{1,2,0:T(2,128)} %param.12) | copy-start | bytes 100
  7.4 51.1 %all-gather.4.cloned.1.call-start = ((), (), s32[]{:S(2)}) async-start(), calls=%async_computation | async-start | bytes 2621440 | tf_op jit(solution)/shard_map/all_gather | solution.py:51
  8.1 64.9 %all-reduce.3.cloned.1.call-start = ((), (), s32[]{:S(2)}) async-start(), calls=%async_computation.3 | async-start | bytes 2097152 | tf_op jit(solution)/shard_map/psum | solution.py:9
  10.1 18.2 %copy-start.2 = (s32[512,1024]{1,0:T(8,128)S(1)}, s32[512,1024]{1,0:T(8,128)}, u32[]{:S(2)}) copy-start(s32[512,1024]{1,0:T(8,128)} %param.10) | copy-start | bytes 6291460
  12.4 16.0 %copy-start.4 = (s32[1,4,128,128]{3,2,1,0:T(8,128)S(1)}, s32[1,4,128,128]{3,2,1,0:T(8,128)}, u32[]{:S(2)}) copy-start(s32[1,4,128,128]{3,2,1,0:T(8,128)} %param.11) | copy-start | bytes 786436
  12.4 16.2 %copy-start.5 = (s32[1,4,2]{1,2,0:T(2,128)S(1)}, s32[1,4,2]{1,2,0:T(2,128)}, u32[]{:S(2)}) copy-start(s32[1,4,2]{1,2,0:T(2,128)} %param.13) | copy-start | bytes 100
  12.4 74.8 %all-gather.6.cloned.1.call-start = ((), (), s32[]{:S(2)}) async-start(), calls=%async_computation.1 | async-start | bytes 2359296 | tf_op jit(solution)/shard_map/all_gather | solution.py:76
  13.2 103.9 %all-gather.8.cloned.1.call-start = ((), (), s32[]{:S(2)}) async-start(), calls=%async_computation.2 | async-start | bytes 2359296 | tf_op jit(solution)/shard_map/all_gather | solution.py:78
  67.4 19.9 %copy-start.3 = (s32[512,1024]{1,0:T(8,128)S(1)}, s32[512,1024]{1,0:T(8,128)}, u32[]{:S(2)}) copy-start(s32[512,1024]{1,0:T(8,128)} %param.10) | copy-start | bytes 6291460
Sparse Core Ops, SparseCore 0:
  9.8 48.6 all-gather.3
  60.3 26.8 all-gather.5
  89.1 27.8 all-gather.7
Sparse Core Ops, SparseCore 1:
  12.5 60.5 all-reduce.2
where the time goes:
time: 129 us; the launch traced here: 128 us
  waiting for transfers between devices  74 us (57%)
  between operations  16 us (12%)
  matrix products  14 us (11%)
  blocking collectives  12.7 us (10%)
  local copies, waits for them, and re-layouts  9.02 us (7%)
  other arithmetic  2.63 us (2%)
    all_gather x1, waiting for transfers between devices, shards(): lax.all_gather(features, 'narrow', axis=0, tiled=True)  29.7 us
    all_gather x1, waiting for transfers between devices, shards(): lax.all_gather(second_weight, 'wide', axis=0, tiled=True)  24.1 us
    all_gather x1, waiting for transfers between devices, shards(): lax.all_gather(first_weight, 'wide', axis=0, tiled=True)  14.2 us
    all_gather x1, blocking collectives, shards(): lax.all_gather(lists_sent, 'narrow', axis=0, tiled=True)  12.7 us
    dot_general x2, matrix products, add_rows(): return jnp.dot(left, portion, preferred_element_type=jnp.float32)  10 us
    psum x1, waiting for transfers between devices, spread(): return lax.psum(block, axis)  3.93 us
    dot_general x1, matrix products, shards(): jnp.einsum('pcb,pcid->bid', routed, products, precision=highest)  3.42 us
    gather x2, local copies, waits for them, and re-layouts, shards(): chosen = block_grid[jnp.arange(part_count)[:, None], jnp.maximum(mine, 0)]  2.93 us
  transfers between devices with their start and end apart: 4, of which 4 were waited for; matrix products, arithmetic and copies ran while one was open for 17% of the time, Pallas kernels for 0%

commit v1 on v0

v1 whole, which is shorter than its diff:
```python
import functools

import jax
import jax.numpy as jnp
from jax import lax
from jax.experimental import pallas as pl
from jax.experimental.pallas import tpu as pltpu
from jax.sharding import PartitionSpec as P

ABSENT = 64.0
VMEM_LIMIT = 48 * 1024 * 1024


def params():
    return pltpu.CompilerParams(vmem_limit_bytes=VMEM_LIMIT)


def vmem():
    return pl.BlockSpec(memory_space=pltpu.VMEM)


def smem():
    return pl.BlockSpec(memory_space=pltpu.SMEM)


def anywhere():
    return pl.BlockSpec(memory_space=pl.ANY)


def swap(block, count, bit):
    return lax.ppermute(block, "wide", [(i, i ^ bit) for i in range(count)])


def turn(block, count, step):
    return lax.ppermute(block, "narrow", [(i, (i + step) % count) for i in range(count)])


def pick_kernel(parts, cap, block_rows, where_ref, lists_ref, features_ref, *rest):
    outs = rest[: parts - 1]
    empty_ref, sems = rest[parts - 1 :]
    empty_ref[...] = jnp.full(empty_ref.shape, ABSENT, empty_ref.dtype)
    me = where_ref[1]
    copies = []
    for step in range(1, parts):
        to = lax.rem(me + step, parts)
        for slot in range(cap):
            listed = lists_ref[0, to, slot]
            target = outs[step - 1].at[pl.ds(slot * block_rows, block_rows)]
            sem = sems.at[(step - 1) * cap + slot]
            start = pl.multiple_of(jnp.maximum(listed, 0) * block_rows, block_rows)
            real = pltpu.make_async_copy(features_ref.at[pl.ds(start, block_rows)], target, sem)
            blank = pltpu.make_async_copy(empty_ref, target, sem)

            @pl.when(listed >= 0)
            def _():
                real.start()

            @pl.when(listed < 0)
            def _():
                blank.start()

            copies.append(blank)
    for copy in copies:
        copy.wait()


def pick(where, lists, features, block_rows):
    _, parts, cap = lists.shape
    width = features.shape[1]
    shape = jax.ShapeDtypeStruct((cap * block_rows, width), features.dtype)
    return pl.pallas_call(
        functools.partial(pick_kernel, parts, cap, block_rows),
        out_shape=[shape] * (parts - 1),
        in_specs=[smem(), smem(), anywhere()],
        out_specs=[anywhere()] * (parts - 1),
        scratch_shapes=[
            pltpu.VMEM((block_rows, width), features.dtype),
            pltpu.SemaphoreType.DMA(((parts - 1) * cap,)),
        ],
        compiler_params=params(),
        name="pick_blocks",
    )(where, lists, features)


def prepare_kernel(dense_ref, out_ref, degree_ref):
    values = dense_ref[...]
    out_ref[...] = values.astype(jnp.float32).astype(jnp.bfloat16)
    degree_ref[...] = 1.0 + jnp.sum(values, axis=1, keepdims=True).astype(jnp.float32)


def prepare(dense_weight):
    rows, columns = dense_weight.shape
    step = rows // 4
    return pl.pallas_call(
        prepare_kernel,
        grid=(rows // step,),
        out_shape=[
            jax.ShapeDtypeStruct((rows, columns), jnp.bfloat16),
            jax.ShapeDtypeStruct((rows, 1), jnp.float32),
        ],
        in_specs=[pl.BlockSpec((step, columns), lambda i: (i, 0))],
        out_specs=[
            pl.BlockSpec((step, columns), lambda i: (i, 0)),
            pl.BlockSpec((step, 1), lambda i: (i, 0)),
        ],
        compiler_params=params(),
        cost_estimate=pl.CostEstimate(
            flops=2 * rows * columns, bytes_accessed=6 * rows * columns, transcendentals=0
        ),
        name="dense_rows",
    )(dense_weight)


def dense_kernel(where_ref, dense_ref, mine_ref, other_ref, out_ref):
    stripes, half, _ = mine_ref.shape
    core = lax.rem(where_ref[0], 2)
    total = None
    for stripe in range(stripes):
        for ref, side in ((mine_ref, core), (other_ref, 1 - core)):
            start = pl.multiple_of((2 * stripe + side) * half, half)
            part = jnp.dot(
                dense_ref[:, pl.ds(start, half)], ref[stripe], preferred_element_type=jnp.float32
            )
            total = part if total is None else total + part
    out_ref[...] = total


def dense_sum(where, dense, mine, other):
    rows = dense.shape[0]
    stripes, half, width = mine.shape
    return pl.pallas_call(
        dense_kernel,
        out_shape=jax.ShapeDtypeStruct((rows, width), jnp.float32),
        in_specs=[smem(), vmem(), vmem(), vmem()],
        out_specs=vmem(),
        compiler_params=params(),
        cost_estimate=pl.CostEstimate(
            flops=4 * rows * stripes * half * width,
            bytes_accessed=4 * rows * width * 4,
            transcendentals=0,
        ),
        name="dense_product",
    )(where, dense, mine, other)


def load_pieces(me, groups, target_ref, sems):
    copies = []
    for ref, masks in groups:
        rows = ref.shape[1]
        for at, mask in enumerate(masks):
            start = pl.multiple_of((me ^ mask) * rows, rows)
            copy = pltpu.make_async_copy(
                ref.at[at], target_ref.at[pl.ds(start, rows)], sems.at[len(copies)]
            )
            copy.start()
            copies.append(copy)
    return copies


def hidden_kernel(
    parts, cap, masks, where_ref, lists_ref, targets_ref, features_ref, dense_ref, degree_ref,
    tiles_ref, first_a, first_b, *rest
):
    received = rest[: parts - 1]
    out_ref, first_ref, total_ref, count_ref, combined_ref, sems = rest[parts - 1 :]
    me, part = where_ref[0], where_ref[1]
    copies = load_pieces(
        me, ((first_a, masks), (first_b, tuple(mask ^ 1 for mask in masks))), first_ref, sems
    )
    block_rows = tiles_ref.shape[2]
    lanes = count_ref.shape[1]
    total_ref[...] = dense_ref[...]
    count_ref[...] = jnp.broadcast_to(degree_ref[...], count_ref.shape)
    for step in range(parts):
        source = lax.rem(part + parts - step, parts)
        tile = tiles_ref[0, source]
        weight = jnp.sum(tile, axis=1, keepdims=True).astype(jnp.float32)
        tile = tile.astype(jnp.float32).astype(jnp.bfloat16)
        for slot in range(cap):
            if step == 0:
                listed = lists_ref[0, source, slot]
                start = pl.multiple_of(jnp.maximum(listed, 0) * block_rows, block_rows)
                block = features_ref[pl.ds(start, block_rows), :]
                present = jnp.broadcast_to(listed, (1, block.shape[1])) >= 0
            else:
                block = received[step - 1][pl.ds(slot * block_rows, block_rows), :]
                present = block[0:1, :].astype(jnp.float32) < ABSENT / 2
            product = jnp.dot(tile, block, preferred_element_type=jnp.float32)
            product = jnp.where(present, product, 0.0)
            start = pl.multiple_of(targets_ref[0, source, slot] * block_rows, block_rows)
            total_ref[pl.ds(start, block_rows), :] += product
            count_ref[pl.ds(start, block_rows), :] += jnp.where(present[:, :lanes], weight, 0.0)
    scale = lax.rsqrt(count_ref[...])
    for at in range(0, total_ref.shape[1], lanes):
        columns = pl.ds(at, lanes)
        combined_ref[:, columns] = (
            features_ref[:, columns].astype(jnp.float32) + total_ref[:, columns] * scale
        ).astype(jnp.bfloat16)
    for copy in copies:
        copy.wait()
    hidden = out_ref.shape[1]
    step = min(hidden, 512)

    @pl.loop(0, hidden // step)
    def _(at):
        columns = pl.ds(pl.multiple_of(at * step, step), step)
        gated = jnp.dot(
            combined_ref[...], first_ref[:, columns], preferred_element_type=jnp.float32
        )
        out_ref[:, columns] = jnp.maximum(gated, 0.0).astype(jnp.bfloat16)


def hidden_rows(where, lists, targets, features, dense, degree, tiles, first, masks, received):
    rows, width = features.shape
    hidden = first[0].shape[2]
    _, parts, cap = lists.shape
    pieces = 2 * first[0].shape[0]
    return pl.pallas_call(
        functools.partial(hidden_kernel, parts, cap, masks),
        out_shape=jax.ShapeDtypeStruct((rows, hidden), jnp.bfloat16),
        in_specs=[smem(), smem(), smem(), vmem(), vmem(), vmem(), vmem(), anywhere(), anywhere()]
        + [vmem()] * (parts - 1),
        out_specs=vmem(),
        scratch_shapes=[
            pltpu.VMEM((width, hidden), jnp.bfloat16),
            pltpu.VMEM((rows, width), jnp.float32),
            pltpu.VMEM((rows, 128), jnp.float32),
            pltpu.VMEM((rows, width), jnp.bfloat16),
            pltpu.SemaphoreType.DMA((pieces,)),
        ],
        compiler_params=params(),
        cost_estimate=pl.CostEstimate(
            flops=2 * rows * width * hidden, bytes_accessed=8 * rows * hidden, transcendentals=0
        ),
        name="hidden",
    )(where, lists, targets, features, dense, degree, tiles, *first, *received)


def update_kernel(masks, where_ref, hidden_ref, a, b, c, d, out_ref, second_ref, sems):
    me = where_ref[0]
    low, high = masks
    groups = (
        (a, low),
        (b, high),
        (c, tuple(mask ^ 1 for mask in low)),
        (d, tuple(mask ^ 1 for mask in high)),
    )
    for copy in load_pieces(me, groups, second_ref, sems):
        copy.wait()
    width = out_ref.shape[1]
    step = min(width, 256)

    @pl.loop(0, width // step)
    def _(at):
        columns = pl.ds(pl.multiple_of(at * step, step), step)
        out_ref[:, columns] = jnp.dot(
            hidden_ref[...], second_ref[:, columns], preferred_element_type=jnp.float32
        ).astype(jnp.bfloat16)


def update(where, hidden, second, masks):
    rows, depth = hidden.shape
    width = second[0].shape[2]
    pieces = 2 * (len(masks[0]) + len(masks[1]))
    return pl.pallas_call(
        functools.partial(update_kernel, masks),
        out_shape=jax.ShapeDtypeStruct((rows, width), jnp.bfloat16),
        in_specs=[smem(), vmem()] + [anywhere()] * 4,
        out_specs=vmem(),
        scratch_shapes=[
            pltpu.VMEM((depth, width), jnp.bfloat16),
            pltpu.SemaphoreType.DMA((pieces,)),
        ],
        compiler_params=params(),
        cost_estimate=pl.CostEstimate(
            flops=2 * rows * width * depth, bytes_accessed=4 * depth * width, transcendentals=0
        ),
        name="update",
    )(where, hidden, *second)


def shards(
    features,
    stripe_owner,
    dense_weight,
    sparse_weight,
    send_blocks,
    target_block,
    first_weight,
    second_weight,
    wide,
    narrow,
):
    rows = features.shape[0]
    block_rows = sparse_weight.shape[2]
    stripes = stripe_owner.shape[1]
    bits = [1 << at for at in range(1, wide.bit_length() - 1)]
    me, part = lax.axis_index("wide"), lax.axis_index("narrow")
    where = jnp.stack([me, part]).astype(jnp.int32)
    owners = lax.dynamic_index_in_dim(stripe_owner, part, 0, keepdims=False)
    core = me & 1
    half = rows // 2

    first, second = first_weight[None], second_weight[None]
    first_masks, second_masks = (0,), (0,)
    first_new = swap(first, wide, bits[0])
    second_new = swap(second, wide, bits[-1])

    picked = pick(where, send_blocks, features, block_rows)
    received = [turn(block, narrow, step + 1) for step, block in enumerate(picked)]

    kept = lax.dynamic_slice_in_dim(features, core * half, half)
    given = swap(lax.dynamic_slice_in_dim(features, (1 - core) * half, half), wide, 1)
    carried = [jnp.where((owners[k] & 1) == core, kept, given) for k in range(stripes)]
    hops = len(bits)
    for hop in range(hops):
        for k in range(stripes):
            bit = bits[hop] if k % 2 == 0 else bits[hops - 1 - hop]
            came = swap(carried[k], wide, bit)
            carried[k] = jnp.where(((owners[k] ^ me) & bit) == 0, carried[k], came)
    mine = jnp.stack(carried)
    other = swap(mine, wide, 1)

    for hop in range(hops):
        if hop > 0:
            first_new = swap(first, wide, bits[hop])
            second_new = swap(second, wide, bits[hops - 1 - hop])
        first_more = tuple(mask ^ bits[hop] for mask in first_masks)
        second_more = tuple(mask ^ bits[hops - 1 - hop] for mask in second_masks)
        first = jnp.concatenate([first, first_new])
        first_masks += first_more
        if hop < hops - 1:
            second = jnp.concatenate([second, second_new])
            second_masks += second_more
    first_pair = (first, swap(first, wide, 1))
    second_all = (second, second_new, swap(second, wide, 1), swap(second_new, wide, 1))

    dense, degree = prepare(dense_weight)
    dense_total = dense_sum(where, dense, mine, other)
    hidden = hidden_rows(
        where, send_blocks, target_block, features, dense_total, degree, sparse_weight,
        first_pair, first_masks, received,
    )
    return update(where, hidden, second_all, (second_masks, second_more))


def solution(mesh):
    placed = (
        P(("wide", "narrow"), None),
        P(),
        P(("wide", "narrow"), None),
        P(("wide", "narrow"), None, None, None),
        P(("wide", "narrow"), None, None),
        P(("wide", "narrow"), None, None),
        P("wide", None),
        P("wide", None),
    )
    local = functools.partial(shards, wide=mesh.shape["wide"], narrow=mesh.shape["narrow"])
    return jax.shard_map(
        local, mesh=mesh, in_specs=placed, out_specs=P(("wide", "narrow"), None), check_vma=False
    )
```

time: 129 us -> 80.8 us (0.63)
  waiting for transfers between devices: 74 us -> 37.8 us
  starting transfers between devices: 0.13 us -> 18 us
  Pallas kernels: 0 us -> 14.2 us
  matrix products: 14 us -> 0 us
  between operations: 16 us -> 2.86 us
  blocking collectives: 12.7 us -> 0 us
  local copies, waits for them, and re-layouts: 9.02 us -> 5.08 us
    all_gather x3 -> x0, waiting for transfers between devices: 68 us -> none  [the longest x1 29.7 us: shards(): lax.all_gather(features, 'narrow', axis=0, tiled=True)]
    ppermute x0 -> x16, waiting for transfers between devices: none -> 37.8 us  [the longest x3 20.4 us: turn(): lax.ppermute(block, 'narrow', [(i, (i + step) % count) for i in range(cou...]
    ppermute x0 -> x16, starting transfers between devices: none -> 18 us  [the longest x13 11.9 us: swap(): return lax.ppermute(block, 'wide', [(i, i ^ bit) for i in range(count)])]
    pallas_call x0 -> x5, Pallas kernels: none -> 14.2 us  [the longest x1 5.98 us: hidden_rows(): pl.pallas_call(functools.partial(hidden_kernel, parts, cap, masks), out_s...]
    dot_general x5 -> x0, matrix products: 14 us -> none  [the longest x2 10 us: add_rows(): return jnp.dot(left, portion, preferred_element_type=jnp.float32)]
    all_gather x1 -> x0, blocking collectives: 12.7 us -> none  [shards(): lax.all_gather(lists_sent, 'narrow', axis=0, tiled=True)]
    psum x1 -> x0, waiting for transfers between devices: 3.93 us -> none  [spread(): return lax.psum(block, axis)]
    gather x2 -> x0, local copies, waits for them, and re-layouts: 2.93 us -> none  [shards(): chosen = block_grid[jnp.arange(part_count)[:, None], jnp.maximum(mine, 0)]]
  transfers between devices with their start and end apart: 4 -> 16, of which waited for: 4 -> 7; matrix products, arithmetic and copies ran while one was open for 17% -> 4% of each run, Pallas kernels for 0% -> 13%
where the time goes in v1:
time: 80.8 us; the launch traced here: 80.4 us
  waiting for transfers between devices  37.8 us (47%)
  starting transfers between devices  18 us (22%)
  Pallas kernels  14.2 us (18%)
  local copies, waits for them, and re-layouts  5.08 us (6%)
  between operations  2.86 us (4%)
  other arithmetic  2.45 us (3%)
    ppermute x3, waiting for transfers between devices, turn(): lax.ppermute(block, 'narrow', [(i, (i + step) % count) for i in range(cou...  20.4 us
    ppermute x13, waiting for transfers between devices, swap(): return lax.ppermute(block, 'wide', [(i, i ^ bit) for i in range(count)])  17.3 us
    ppermute x13, starting transfers between devices, swap(): return lax.ppermute(block, 'wide', [(i, i ^ bit) for i in range(count)])  11.9 us
    ppermute x3, starting transfers between devices, turn(): lax.ppermute(block, 'narrow', [(i, (i + step) % count) for i in range(cou...  6.14 us
    pallas_call x1, Pallas kernels, hidden_rows(): pl.pallas_call(functools.partial(hidden_kernel, parts, cap, masks), out_s...  5.98 us
    pallas_call x1, Pallas kernels, update(): pl.pallas_call(functools.partial(update_kernel, masks), out_shape=jax.Sha...  4.12 us
    unnamed x20, local copies, waits for them, and re-layouts  3.4 us
    pallas_call x1, Pallas kernels, dense_sum(): pl.pallas_call(dense_kernel, out_shape=jax.ShapeDtypeStruct((rows, width)...  1.8 us
  transfers between devices with their start and end apart: 16, of which 7 were waited for; matrix products, arithmetic and copies ran while one was open for 4% of the time, Pallas kernels for 13%

profile of v1, /device:TPU:0, one launch (start us, length us, event | category | flops | bytes accessed | tf_op | source)
XLA Modules:
  0.0 80.4 jit_solution(849077229077288997)
XLA Ops:
  0.0 1.0 %constant_dynamic-slice_fusion = bf16[256,512]{1,0:T(8,128)(2,1)S(1)} fusion(bf16[512,512]{1,0:T(8,128)(2,1)} %features_ref.3, s32[]{:T(128)S(6)} %select_n.53), kind=kLoop, calls=%fused_computation.10 | loop fusion | bytes 524292 | tf_op jit(solution)/shard_map/dynamic_slice | solution.py:313
  1.0 0.5 collective-permute-start
  1.5 2.6 %collective-permute-start.6 = (bf16[1,64,2048]{2,1,0:T(8,128)(2,1)}, bf16[1,64,2048]{2,1,0:T(8,128)(2,1)S(1)}, u32[]{:S(2)}, u32[]{:S(2)}) collective-permute-start(bf16[1,64,2048]{2,1,0:T(8,128)(2,1)} %bitcast.10), channel_id=1, source_target_pairs={{0,8},{4,12},{8,0},{12,4},{16,24},{20,28},{24,16},{28,20},{1,9},{5... | collective-permute-start | bytes 786440 | tf_op jit(solution)/shard_map/ppermute | solution.py:31
  4.1 1.5 %collective-permute-start.12 = (bf16[1,256,512]{2,1,0:T(8,128)(2,1)}, bf16[1,256,512]{2,1,0:T(8,128)(2,1)S(1)}, u32[]{:S(2)}, u32[]{:S(2)}) collective-permute-start(bf16[1,256,512]{2,1,0:T(8,128)(2,1)} %bitcast.13), channel_id=1, source_target_pairs={{0,16},{4,20},{8,24},{12,28},{16,0},{20,4},{24,8},{28,12},{1,17},{... | collective-permute-start | bytes 786440 | tf_op jit(solution)/shard_map/ppermute | solution.py:31
  5.7 0.6 fusion
  9.0 1.0 %broadcast_select_fusion.2 = (bf16[256,512]{1,0:T(8,128)(2,1)S(1)}, bf16[256,512]{1,0:T(8,128)(2,1)S(1)}) fusion(bf16[256,512]{1,0:T(8,128)(2,1)S(1)} %collective-permute-done, pred[]{:T(512)S(6)} %eq.20, bf16[512,512]{1,0:T(8,128)(2,1)} %features_ref.3, s32[]{:T(128)S(6)} %select_n.52, pred[]{:T(512)S(6)} %eq.23), kind=kLoop, calls=%fused_computation.8 | loop fusion | flops 262144 | bytes 1048582 | tf_op jit(solution)/shard_map/jit(_where)/select_n | solution.py:314
  10.0 0.6 collective-permute-start.1
  10.7 0.5 collective-permute-done.6
  11.2 1.0 %pad_maximum_fusion.2 = bf16[2,64,2048]{2,1,0:T(8,128)(2,1)S(1)} fusion(bf16[1,64,2048]{2,1,0:T(8,128)(2,1)S(1)} %collective-permute-done.6, bf16[1,64,2048]{2,1,0:T(8,128)(2,1)} %bitcast.11), kind=kLoop, calls=%fused_computation.2 | loop fusion | flops 262144 | bytes 1048576 | tf_op jit(solution)/shard_map/concatenate | solution.py:330
  12.2 1.9 %collective-permute-start.7 = (bf16[2,64,2048]{2,1,0:T(8,128)(2,1)S(1)}, bf16[2,64,2048]{2,1,0:T(8,128)(2,1)S(1)}, u32[]{:S(2)}, u32[]{:S(2)}) collective-permute-start(bf16[2,64,2048]{2,1,0:T(8,128)(2,1)S(1)} %pad_maximum_fusion.2), channel_id=1, source_target_pairs={{0,16},{4,20},{8,24},{12,28},{16,0},{20,4},{24,8},{28,12},{1,17},{... | collective-permute-start | bytes 1572872 | tf_op jit(solution)/shard_map/ppermute | solution.py:31
  14.1 2.0 %collective-permute-start.13 = (bf16[2,256,512]{2,1,0:T(8,128)(2,1)S(1)}, bf16[2,256,512]{2,1,0:T(8,128)(2,1)S(1)}, u32[]{:S(2)}, u32[]{:S(2)}) collective-permute-start(bf16[2,256,512]{2,1,0:T(8,128)(2,1)S(1)} %pad_maximum_fusion.3.a), channel_id=1, source_target_pairs={{0,8},{4,12},{8,0},{12,4},{16,24},{20,28},{24,16},{28,20},{1,9},{5... | collective-permute-start | bytes 1572872 | tf_op jit(solution)/shard_map/ppermute | solution.py:31
  16.1 3.1 %collective-permute-done.1 = bf16[256,512]{1,0:T(8,128)(2,1)S(1)} collective-permute-done((bf16[256,512]{1,0:T(8,128)(2,1)S(1)}, bf16[256,512]{1,0:T(8,128)(2,1)S(1)}, u32[]{:S(2)}, u32[]{:S(2)}) %collective-permute-start.1) | collective-permute-done | bytes 262176 | tf_op jit(solution)/shard_map/ppermute | solution.py:31
  19.3 0.6 collective-permute-start.2
  19.9 1.5 %collective-permute-start.4 = (bf16[256,512]{1,0:T(8,128)(2,1)S(1)}, bf16[256,512]{1,0:T(8,128)(2,1)S(1)}, u32[]{:S(2)}, u32[]{:S(2)}) collective-permute-start(bf16[256,512]{1,0:T(8,128)(2,1)S(1)} %broadcast_select_fusion.1), channel_id=1, source_target_pairs={{0,8},{4,12},{8,0},{12,4},{16,24},{20,28},{24,16},{28,20},{1,9},{5... | collective-permute-start | bytes 786440 | tf_op jit(solution)/shard_map/ppermute | solution.py:31
  21.5 9.6 %collective-permute-done.7 = bf16[2,64,2048]{2,1,0:T(8,128)(2,1)S(1)} collective-permute-done((bf16[2,64,2048]{2,1,0:T(8,128)(2,1)S(1)}, bf16[2,64,2048]{2,1,0:T(8,128)(2,1)S(1)}, u32[]{:S(2)}, u32[]{:S(2)}) %collective-permute-start.7) | collective-permute-done | bytes 524320 | tf_op jit(solution)/shard_map/ppermute | solution.py:31
  31.1 0.1 pad_maximum_fusion.first_a
  31.3 4.0 %collective-permute-done.2 = bf16[256,512]{1,0:T(8,128)(2,1)S(1)} collective-permute-done((bf16[256,512]{1,0:T(8,128)(2,1)S(1)}, bf16[256,512]{1,0:T(8,128)(2,1)S(1)}, u32[]{:S(2)}, u32[]{:S(2)}) %collective-permute-start.2) | collective-permute-done | bytes 262176 | tf_op jit(solution)/shard_map/ppermute | solution.py:31
  35.5 0.1 copy.10.lists_ref
  35.7 1.7 %pick_blocks.1 = (bf16[256,512]{1,0:T(8,128)(2,1)}, bf16[256,512]{1,0:T(8,128)(2,1)S(1)}, bf16[256,512]{1,0:T(8,128)(2,1)}) custom-call(s32[2]{0:T(128)S(1)} %pad_add_fusion.where_ref, s32[1,4,2]{2,1,0:T(4,128)S(1)} %copy.10.lists_ref, bf16[512,512]{1,0:T(8,128)(2,1)S(1)} %copy-done.2), custom_call_target="tpu_custom_call" | custom-call | tf_op jit(solution)/shard_map/pick_blocks/pallas_call | solution.py:71
  37.4 2.7 %collective-permute-start.10 = (bf16[256,512]{1,0:T(8,128)(2,1)S(1)}, bf16[256,512]{1,0:T(8,128)(2,1)S(1)}, u32[]{:S(2)}, u32[]{:S(2)}) collective-permute-start(bf16[256,512]{1,0:T(8,128)(2,1)S(1)} %get-tuple-element.13), channel_id=1, source_target_pairs={{0,2},{1,3},{2,0},{3,1},{4,6},{5,7},{6,4},{7,5},{8,10},{9,11},{10,... | collective-permute-start | bytes 786440 | tf_op jit(solution)/shard_map/ppermute | solution.py:35
  40.1 0.2 collective-permute-start.14
  40.3 0.3 collective-permute-start.15
  40.6 12.1 %collective-permute-done.10.rest_1_ = bf16[256,512]{1,0:T(8,128)(2,1)S(1)} collective-permute-done((bf16[256,512]{1,0:T(8,128)(2,1)S(1)}, bf16[256,512]{1,0:T(8,128)(2,1)S(1)}, u32[]{:S(2)}, u32[]{:S(2)}) %collective-permute-start.10) | collective-permute-done | bytes 262176 | tf_op jit(solution)/shard_map/ppermute | solution.py:35
  52.7 3.5 %collective-permute-start.11 = (bf16[256,512]{1,0:T(8,128)(2,1)}, bf16[256,512]{1,0:T(8,128)(2,1)}, u32[]{:S(2)}, u32[]{:S(2)}) collective-permute-start(bf16[256,512]{1,0:T(8,128)(2,1)} %get-tuple-element.14), channel_id=1, source_target_pairs={{0,3},{1,0},{2,1},{3,2},{4,7},{5,4},{6,5},{7,6},{8,11},{9,8},{10,9... | collective-permute-start | bytes 786440 | tf_op jit(solution)/shard_map/ppermute | solution.py:35
  56.3 1.6 %copy-done.3 = s32[512,1024]{1,0:T(8,128)S(1)} copy-done((s32[512,1024]{1,0:T(8,128)S(1)}, s32[512,1024]{1,0:T(8,128)}, u32[]{:S(2)}) %copy-start.3) | copy-done | bytes 2097176
  57.9 0.6 dense_rows.1
  58.5 1.8 %dense_product.1.dense_ref = f32[512,512]{1,0:T(8,128)S(1)} custom-call(s32[2]{0:T(128)S(1)} %pad_add_fusion.where_ref, bf16[512,1024]{1,0:T(8,128)(2,1)S(1)} %get-tuple-element.10.dense_ref, bf16[2,256,512]{2,1,0:T(8,128)(2,1)S(1)} %pad_maximum_fusion.1.mine_ref, bf16[2,256,512]{2,1,0:T(8,128)(2,1)} %collective-permute-done.5.other_ref), custom_call_target="tpu_custom_call" | custom-call | flops 536870912 | bytes 4194304 | tf_op jit(solution)/shard_map/dense_product/pallas_call | solution.py:131
  60.3 2.9 %collective-permute-done.11.rest_2_ = bf16[256,512]{1,0:T(8,128)(2,1)} collective-permute-done((bf16[256,512]{1,0:T(8,128)(2,1)}, bf16[256,512]{1,0:T(8,128)(2,1)}, u32[]{:S(2)}, u32[]{:S(2)}) %collective-permute-start.11) | collective-permute-done | bytes 262176 | tf_op jit(solution)/shard_map/ppermute | solution.py:35
  63.2 5.4 %collective-permute-done.9.rest_0_ = bf16[256,512]{1,0:T(8,128)(2,1)} collective-permute-done((bf16[256,512]{1,0:T(8,128)(2,1)}, bf16[256,512]{1,0:T(8,128)(2,1)}, u32[]{:S(2)}, u32[]{:S(2)}) %collective-permute-start.9) | collective-permute-done | bytes 262176 | tf_op jit(solution)/shard_map/ppermute | solution.py:35
  68.7 6.0 %hidden.1.hidden_ref = bf16[512,2048]{1,0:T(8,128)(2,1)} custom-call(s32[2]{0:T(128)S(1)} %pad_add_fusion.where_ref, s32[1,4,2]{2,1,0:T(4,128)S(1)} %copy.10.lists_ref, s32[1,4,2]{2,1,0:T(4,128)S(1)} %copy.11.targets_ref, bf16[512,512]{1,0:T(8,128)(2,1)S(1)} %copy-done.2, f32[512,512]{1,0:T(8,128)S(1)} %dense_product.1.dense_ref, ...), custom_call_target="tpu_custom_call" | custom-call | flops 1073741824 | bytes 8388608 | tf_op jit(solution)/shard_map/hidden/pallas_call | solution.py:218
  74.7 1.6 %copy-done.1 = bf16[512,2048]{1,0:T(8,128)(2,1)S(1)} copy-done((bf16[512,2048]{1,0:T(8,128)(2,1)S(1)}, bf16[512,2048]{1,0:T(8,128)(2,1)}, u32[]{:S(2)}) %copy-start.1) | copy-done | bytes 2097176
  76.3 4.1 %update.1 = bf16[512,512]{1,0:T(8,128)(2,1)} custom-call(s32[2]{0:T(128)S(1)} %pad_add_fusion.where_ref, bf16[512,2048]{1,0:T(8,128)(2,1)S(1)} %copy-done.1, bf16[2,256,512]{2,1,0:T(8,128)(2,1)S(1)} %pad_maximum_fusion.3.a, bf16[2,256,512]{2,1,0:T(8,128)(2,1)S(1)} %collective-permute-done.13.b, bf16[2,256,512]{2,1,0:T(8,128)(2,1)} %collective-permute-done.14.c, ...), custom_call_target="tpu_custom_call" | custom-call | flops 1073741824 | bytes 4194304 | tf_op jit(solution)/shard_map/update/pallas_call | solution.py:265
  (38 shorter events, 0.7 us)
Async XLA Ops:
  0.0 5.6 %copy-start = (s32[4,2]{0,1:T(2,128)S(1)}, s32[4,2]{0,1:T(2,128)}, u32[]{:S(2)}) copy-start(s32[4,2]{0,1:T(2,128)} %param.9) | copy-start | bytes 100
  0.0 14.1 %copy-start.6 = (bf16[256,512]{1,0:T(8,128)(2,1)S(1)}, bf16[256,512]{1,0:T(8,128)(2,1)}, u32[]{:S(2)}) copy-start(bf16[256,512]{1,0:T(8,128)(2,1)} %param.15) | copy-start | bytes 786436
  1.0 7.9 %collective-permute-start = (bf16[256,512]{1,0:T(8,128)(2,1)S(1)}, bf16[256,512]{1,0:T(8,128)(2,1)S(1)}, u32[]{:S(2)}, u32[]{:S(2)}) collective-permute-start(bf16[256,512]{1,0:T(8,128)(2,1)S(1)} %constant_dynamic-slice_fusion), channel_id=1, source_target_pairs={{0,4},{4,0},{8,12},{12,8},{16,20},{20,16},{24,28},{28,24},{1,5},{5... | collective-permute-start | bytes 786440 | tf_op jit(solution)/shard_map/ppermute | solution.py:31
  1.5 9.7 %collective-permute-start.6 = (bf16[1,64,2048]{2,1,0:T(8,128)(2,1)}, bf16[1,64,2048]{2,1,0:T(8,128)(2,1)S(1)}, u32[]{:S(2)}, u32[]{:S(2)}) collective-permute-start(bf16[1,64,2048]{2,1,0:T(8,128)(2,1)} %bitcast.10), channel_id=1, source_target_pairs={{0,8},{4,12},{8,0},{12,4},{16,24},{20,28},{24,16},{28,20},{1,9},{5... | collective-permute-start | bytes 786440 | tf_op jit(solution)/shard_map/ppermute | solution.py:31
  4.1 10.0 %collective-permute-start.12 = (bf16[1,256,512]{2,1,0:T(8,128)(2,1)}, bf16[1,256,512]{2,1,0:T(8,128)(2,1)S(1)}, u32[]{:S(2)}, u32[]{:S(2)}) collective-permute-start(bf16[1,256,512]{2,1,0:T(8,128)(2,1)} %bitcast.13), channel_id=1, source_target_pairs={{0,16},{4,20},{8,24},{12,28},{16,0},{20,4},{24,8},{28,12},{1,17},{... | collective-permute-start | bytes 786440 | tf_op jit(solution)/shard_map/ppermute | solution.py:31
  10.0 21.1 %copy-start.5 = (bf16[64,2048]{1,0:T(8,128)(2,1)S(1)}, bf16[64,2048]{1,0:T(8,128)(2,1)}, u32[]{:S(2)}) copy-start(bf16[64,2048]{1,0:T(8,128)(2,1)} %param.14) | copy-start | bytes 786436
  10.0 9.3 %collective-permute-start.1 = (bf16[256,512]{1,0:T(8,128)(2,1)S(1)}, bf16[256,512]{1,0:T(8,128)(2,1)S(1)}, u32[]{:S(2)}, u32[]{:S(2)}) collective-permute-start(bf16[256,512]{1,0:T(8,128)(2,1)S(1)} %get-tuple-element.15), channel_id=1, source_target_pairs={{0,8},{4,12},{8,0},{12,4},{16,24},{20,28},{24,16},{28,20},{1,9},{5... | collective-permute-start | bytes 786440 | tf_op jit(solution)/shard_map/ppermute | solution.py:31
  10.6 9.3 %collective-permute-start.3 = (bf16[256,512]{1,0:T(8,128)(2,1)S(1)}, bf16[256,512]{1,0:T(8,128)(2,1)S(1)}, u32[]{:S(2)}, u32[]{:S(2)}) collective-permute-start(bf16[256,512]{1,0:T(8,128)(2,1)S(1)} %get-tuple-element.16), channel_id=1, source_target_pairs={{0,16},{4,20},{8,24},{12,28},{16,0},{20,4},{24,8},{28,12},{1,17},{... | collective-permute-start | bytes 786440 | tf_op jit(solution)/shard_map/ppermute | solution.py:31
  12.2 18.9 %collective-permute-start.7 = (bf16[2,64,2048]{2,1,0:T(8,128)(2,1)S(1)}, bf16[2,64,2048]{2,1,0:T(8,128)(2,1)S(1)}, u32[]{:S(2)}, u32[]{:S(2)}) collective-permute-start(bf16[2,64,2048]{2,1,0:T(8,128)(2,1)S(1)} %pad_maximum_fusion.2), channel_id=1, source_target_pairs={{0,16},{4,20},{8,24},{12,28},{16,0},{20,4},{24,8},{28,12},{1,17},{... | collective-permute-start | bytes 1572872 | tf_op jit(solution)/shard_map/ppermute | solution.py:31
  14.1 26.1 %collective-permute-start.13 = (bf16[2,256,512]{2,1,0:T(8,128)(2,1)S(1)}, bf16[2,256,512]{2,1,0:T(8,128)(2,1)S(1)}, u32[]{:S(2)}, u32[]{:S(2)}) collective-permute-start(bf16[2,256,512]{2,1,0:T(8,128)(2,1)S(1)} %pad_maximum_fusion.3.a), channel_id=1, source_target_pairs={{0,8},{4,12},{8,0},{12,4},{16,24},{20,28},{24,16},{28,20},{1,9},{5... | collective-permute-start | bytes 1572872 | tf_op jit(solution)/shard_map/ppermute | solution.py:31
  19.3 16.0 %collective-permute-start.2 = (bf16[256,512]{1,0:T(8,128)(2,1)S(1)}, bf16[256,512]{1,0:T(8,128)(2,1)S(1)}, u32[]{:S(2)}, u32[]{:S(2)}) collective-permute-start(bf16[256,512]{1,0:T(8,128)(2,1)S(1)} %broadcast_select_fusion.3), channel_id=1, source_target_pairs={{0,16},{4,20},{8,24},{12,28},{16,0},{20,4},{24,8},{28,12},{1,17},{... | collective-permute-start | bytes 786440 | tf_op jit(solution)/shard_map/ppermute | solution.py:31
  19.9 15.6 %copy-start.7 = (s32[1,4,2]{1,2,0:T(2,128)S(1)}, s32[1,4,2]{1,2,0:T(2,128)}, u32[]{:S(2)}) copy-start(s32[1,4,2]{1,2,0:T(2,128)} %param.12) | copy-start | bytes 100
  19.9 15.8 %copy-start.2 = (bf16[512,512]{1,0:T(8,128)(2,1)S(1)}, bf16[512,512]{1,0:T(8,128)(2,1)}, u32[]{:S(2)}) copy-start(bf16[512,512]{1,0:T(8,128)(2,1)} %features_ref.3) | copy-start | bytes 1572868
  19.9 15.4 %collective-permute-start.4 = (bf16[256,512]{1,0:T(8,128)(2,1)S(1)}, bf16[256,512]{1,0:T(8,128)(2,1)S(1)}, u32[]{:S(2)}, u32[]{:S(2)}) collective-permute-start(bf16[256,512]{1,0:T(8,128)(2,1)S(1)} %broadcast_select_fusion.1), channel_id=1, source_target_pairs={{0,8},{4,12},{8,0},{12,4},{16,24},{20,28},{24,16},{28,20},{1,9},{5... | collective-permute-start | bytes 786440 | tf_op jit(solution)/shard_map/ppermute | solution.py:31
  31.2 25.0 %copy-start.8 = (s32[1,4,2]{1,2,0:T(2,128)S(1)}, s32[1,4,2]{1,2,0:T(2,128)}, u32[]{:S(2)}) copy-start(s32[1,4,2]{1,2,0:T(2,128)} %param.13) | copy-start | bytes 100
  31.2 37.4 %collective-permute-start.8 = (bf16[4,64,2048]{2,1,0:T(8,128)(2,1)S(1)}, bf16[4,64,2048]{2,1,0:T(8,128)(2,1)}, u32[]{:S(2)}, u32[]{:S(2)}) collective-permute-start(bf16[4,64,2048]{2,1,0:T(8,128)(2,1)S(1)} %pad_maximum_fusion.first_a), channel_id=1, source_target_pairs={{0,4},{4,0},{8,12},{12,8},{16,20},{20,16},{24,28},{28,24},{1,5},{5... | collective-permute-start | bytes 3145736 | tf_op jit(solution)/shard_map/ppermute | solution.py:31
  35.4 20.7 %collective-permute-start.5 = (bf16[2,256,512]{2,1,0:T(8,128)(2,1)S(1)}, bf16[2,256,512]{2,1,0:T(8,128)(2,1)}, u32[]{:S(2)}, u32[]{:S(2)}) collective-permute-start(bf16[2,256,512]{2,1,0:T(8,128)(2,1)S(1)} %pad_maximum_fusion.1.mine_ref), channel_id=1, source_target_pairs={{0,4},{4,0},{8,12},{12,8},{16,20},{20,16},{24,28},{28,24},{1,5},{5... | collective-permute-start | bytes 1572872 | tf_op jit(solution)/shard_map/ppermute | solution.py:31
  37.4 15.3 %collective-permute-start.10 = (bf16[256,512]{1,0:T(8,128)(2,1)S(1)}, bf16[256,512]{1,0:T(8,128)(2,1)S(1)}, u32[]{:S(2)}, u32[]{:S(2)}) collective-permute-start(bf16[256,512]{1,0:T(8,128)(2,1)S(1)} %get-tuple-element.13), channel_id=1, source_target_pairs={{0,2},{1,3},{2,0},{3,1},{4,6},{5,7},{6,4},{7,5},{8,10},{9,11},{10,... | collective-permute-start | bytes 786440 | tf_op jit(solution)/shard_map/ppermute | solution.py:35
  40.1 34.6 %collective-permute-start.14 = (bf16[2,256,512]{2,1,0:T(8,128)(2,1)S(1)}, bf16[2,256,512]{2,1,0:T(8,128)(2,1)}, u32[]{:S(2)}, u32[]{:S(2)}) collective-permute-start(bf16[2,256,512]{2,1,0:T(8,128)(2,1)S(1)} %pad_maximum_fusion.3.a), channel_id=1, source_target_pairs={{0,4},{4,0},{8,12},{12,8},{16,20},{20,16},{24,28},{28,24},{1,5},{5... | collective-permute-start | bytes 1572872 | tf_op jit(solution)/shard_map/ppermute | solution.py:31
  40.3 34.4 %collective-permute-start.15 = (bf16[2,256,512]{2,1,0:T(8,128)(2,1)S(1)}, bf16[2,256,512]{2,1,0:T(8,128)(2,1)}, u32[]{:S(2)}, u32[]{:S(2)}) collective-permute-start(bf16[2,256,512]{2,1,0:T(8,128)(2,1)S(1)} %collective-permute-done.13.b), channel_id=1, source_target_pairs={{0,4},{4,0},{8,12},{12,8},{16,20},{20,16},{24,28},{28,24},{1,5},{5... | collective-permute-start | bytes 1572872 | tf_op jit(solution)/shard_map/ppermute | solution.py:31
  52.7 10.5 %collective-permute-start.11 = (bf16[256,512]{1,0:T(8,128)(2,1)}, bf16[256,512]{1,0:T(8,128)(2,1)}, u32[]{:S(2)}, u32[]{:S(2)}) collective-permute-start(bf16[256,512]{1,0:T(8,128)(2,1)} %get-tuple-element.14), channel_id=1, source_target_pairs={{0,3},{1,0},{2,1},{3,2},{4,7},{5,4},{6,5},{7,6},{8,11},{9,8},{10,9... | collective-permute-start | bytes 786440 | tf_op jit(solution)/shard_map/ppermute | solution.py:35
  56.2 12.5 %collective-permute-start.9 = (bf16[256,512]{1,0:T(8,128)(2,1)}, bf16[256,512]{1,0:T(8,128)(2,1)}, u32[]{:S(2)}, u32[]{:S(2)}) collective-permute-start(bf16[256,512]{1,0:T(8,128)(2,1)} %get-tuple-element.12), channel_id=1, source_target_pairs={{0,1},{1,2},{2,3},{3,0},{4,5},{5,6},{6,7},{7,4},{8,9},{9,10},{10,1... | collective-permute-start | bytes 786440 | tf_op jit(solution)/shard_map/ppermute | solution.py:35
  56.3 1.6 %copy-start.3 = (s32[512,1024]{1,0:T(8,128)S(1)}, s32[512,1024]{1,0:T(8,128)}, u32[]{:S(2)}) copy-start(s32[512,1024]{1,0:T(8,128)} %dense_ref.1) | copy-start | bytes 6291460
  58.5 10.2 %copy-start.4 = (s32[1,4,128,128]{3,2,1,0:T(8,128)S(1)}, s32[1,4,128,128]{3,2,1,0:T(8,128)}, u32[]{:S(2)}) copy-start(s32[1,4,128,128]{3,2,1,0:T(8,128)} %tiles_ref.1) | copy-start | bytes 786436
  74.7 1.6 %copy-start.1 = (bf16[512,2048]{1,0:T(8,128)(2,1)S(1)}, bf16[512,2048]{1,0:T(8,128)(2,1)}, u32[]{:S(2)}) copy-start(bf16[512,2048]{1,0:T(8,128)(2,1)} %hidden.1.hidden_ref) | copy-start | bytes 6291460

commit v2 on v1

v2 whole, which is shorter than its diff:
```python
import functools

import jax
import jax.numpy as jnp
from jax import lax
from jax.experimental import pallas as pl
from jax.experimental.pallas import tpu as pltpu
from jax.sharding import PartitionSpec as P

ABSENT = 64.0
VMEM_LIMIT = 48 * 1024 * 1024


def params():
    return pltpu.CompilerParams(vmem_limit_bytes=VMEM_LIMIT)


def vmem():
    return pl.BlockSpec(memory_space=pltpu.VMEM)


def smem():
    return pl.BlockSpec(memory_space=pltpu.SMEM)


def anywhere():
    return pl.BlockSpec(memory_space=pl.ANY)


def hbm():
    return pl.BlockSpec(memory_space=pltpu.HBM)


def swap(block, count, bit):
    return lax.ppermute(block, "wide", [(i, i ^ bit) for i in range(count)])


def pick_kernel(parts, cap, block_rows, lists_ref, features_ref, out_ref, kept_ref, given_ref, empty_ref, sems):
    empty_ref[...] = jnp.full(empty_ref.shape, ABSENT, empty_ref.dtype)
    core = lax.rem(lax.axis_index("wide"), 2)
    half = kept_ref.shape[0]
    copies = []
    for ref, side in ((given_ref, 1 - core), (kept_ref, core)):
        start = pl.multiple_of(side * half, half)
        copy = pltpu.make_async_copy(
            features_ref.at[pl.ds(start, half)], ref, sems.at[len(copies)]
        )
        copy.start()
        copies.append(copy)
    for to in range(parts):
        for slot in range(cap):
            listed = lists_ref[0, slot, to]
            target = out_ref.at[to, pl.ds(slot * block_rows, block_rows)]
            sem = sems.at[len(copies)]
            start = pl.multiple_of(jnp.maximum(listed, 0) * block_rows, block_rows)
            real = pltpu.make_async_copy(features_ref.at[pl.ds(start, block_rows)], target, sem)
            blank = pltpu.make_async_copy(empty_ref, target, sem)

            @pl.when(listed >= 0)
            def _():
                real.start()

            @pl.when(listed < 0)
            def _():
                blank.start()

            copies.append(blank)
    for copy in copies:
        copy.wait()


def pick(lists, features, block_rows):
    _, cap, parts = lists.shape
    rows, width = features.shape
    half = jax.ShapeDtypeStruct((rows // 2, width), features.dtype)
    return pl.pallas_call(
        functools.partial(pick_kernel, parts, cap, block_rows),
        out_shape=[
            jax.ShapeDtypeStruct((parts, cap * block_rows, width), features.dtype), half, half
        ],
        in_specs=[smem(), hbm()],
        out_specs=[hbm()] * 3,
        scratch_shapes=[
            pltpu.VMEM((block_rows, width), features.dtype),
            pltpu.SemaphoreType.DMA((parts * cap + 2,)),
        ],
        compiler_params=params(),
        name="pick_blocks",
    )(lists, features)


def join_kernel(sizes, *refs):
    sems = refs[-1]
    outs = refs[-1 - len(sizes) : -1]
    copies, at = [], 0
    for stack, size in enumerate(sizes):
        for place in range(size):
            copy = pltpu.make_async_copy(refs[at], outs[stack].at[place], sems.at[at])
            copy.start()
            copies.append(copy)
            at += 1
    for copy in copies:
        copy.wait()


def join(stacks, after):
    flat = [piece for stack in stacks for piece in stack]
    sizes = tuple(len(stack) for stack in stacks)
    return pl.pallas_call(
        functools.partial(join_kernel, sizes),
        out_shape=[
            jax.ShapeDtypeStruct((len(stack),) + stack[0].shape, stack[0].dtype) for stack in stacks
        ],
        in_specs=[hbm()] * len(flat) + [anywhere()] * len(after),
        out_specs=[hbm()] * len(stacks),
        scratch_shapes=[pltpu.SemaphoreType.DMA((len(flat),))],
        compiler_params=params(),
        name="join_pieces",
    )(*flat, *after)


def tie_kernel(*refs):
    pass


def tie(blocks, after):
    return pl.pallas_call(
        tie_kernel,
        out_shape=[jax.ShapeDtypeStruct(block.shape, block.dtype) for block in blocks],
        in_specs=[anywhere()] * (len(blocks) + len(after)),
        out_specs=[anywhere()] * len(blocks),
        input_output_aliases={at: at for at in range(len(blocks))},
        compiler_params=params(),
        name="tie",
    )(*blocks, *after)


def prepare_kernel(dense_ref, out_ref, degree_ref):
    values = dense_ref[...]
    out_ref[...] = values.astype(jnp.float32).astype(jnp.bfloat16)
    degree_ref[...] = 1.0 + jnp.sum(values, axis=1, keepdims=True).astype(jnp.float32)


def prepare(dense_weight):
    rows, columns = dense_weight.shape
    step = rows // 4
    return pl.pallas_call(
        prepare_kernel,
        grid=(rows // step,),
        out_shape=[
            jax.ShapeDtypeStruct((rows, columns), jnp.bfloat16),
            jax.ShapeDtypeStruct((rows, 1), jnp.float32),
        ],
        in_specs=[pl.BlockSpec((step, columns), lambda i: (i, 0))],
        out_specs=[
            pl.BlockSpec((step, columns), lambda i: (i, 0)),
            pl.BlockSpec((step, 1), lambda i: (i, 0)),
        ],
        compiler_params=params(),
        cost_estimate=pl.CostEstimate(
            flops=2 * rows * columns, bytes_accessed=6 * rows * columns, transcendentals=0
        ),
        name="dense_rows",
    )(dense_weight)


def dense_kernel(dense_ref, mine_ref, other_ref, out_ref):
    stripes, half, _ = mine_ref.shape
    core = lax.rem(lax.axis_index("wide"), 2)
    total = None
    for stripe in range(stripes):
        for ref, side in ((mine_ref, core), (other_ref, 1 - core)):
            start = pl.multiple_of((2 * stripe + side) * half, half)
            part = jnp.dot(
                dense_ref[:, pl.ds(start, half)], ref[stripe], preferred_element_type=jnp.float32
            )
            total = part if total is None else total + part
    out_ref[...] = total


def dense_sum(dense, mine, other):
    rows = dense.shape[0]
    stripes, half, width = mine.shape
    return pl.pallas_call(
        dense_kernel,
        out_shape=jax.ShapeDtypeStruct((rows, width), jnp.float32),
        in_specs=[vmem(), vmem(), vmem()],
        out_specs=vmem(),
        compiler_params=params(),
        cost_estimate=pl.CostEstimate(
            flops=4 * rows * stripes * half * width,
            bytes_accessed=4 * rows * width * 4,
            transcendentals=0,
        ),
        name="dense_product",
    )(dense, mine, other)


def load_pieces(refs, masks, target_ref, sems):
    me = lax.axis_index("wide")
    copies = []
    for ref, group in zip(refs, masks):
        for at, mask in enumerate(group):
            source = ref if len(ref.shape) == 2 else ref.at[at]
            rows = source.shape[0]
            start = pl.multiple_of((me ^ mask) * rows, rows)
            copy = pltpu.make_async_copy(
                source, target_ref.at[pl.ds(start, rows)], sems.at[len(copies)]
            )
            copy.start()
            copies.append(copy)
    return copies


def combine_kernel(
    parts, cap, targets_ref, features_ref, dense_ref, degree_ref, tiles_ref, received_ref, out_ref,
    total_ref, count_ref
):
    block_rows = tiles_ref.shape[2]
    lanes = count_ref.shape[1]
    total_ref[...] = dense_ref[...]
    count_ref[...] = jnp.broadcast_to(degree_ref[...], count_ref.shape)
    for source in range(parts):
        tile = tiles_ref[0, source]
        weight = jnp.sum(tile, axis=1, keepdims=True).astype(jnp.float32)
        tile = tile.astype(jnp.float32).astype(jnp.bfloat16)
        for slot in range(cap):
            block = received_ref[source, pl.ds(slot * block_rows, block_rows), :]
            present = block[0:1, :].astype(jnp.float32) < ABSENT / 2
            product = jnp.dot(tile, block, preferred_element_type=jnp.float32)
            product = jnp.where(present, product, 0.0)
            start = pl.multiple_of(targets_ref[0, slot, source] * block_rows, block_rows)
            total_ref[pl.ds(start, block_rows), :] += product
            count_ref[pl.ds(start, block_rows), :] += jnp.where(present[:, :lanes], weight, 0.0)
    scale = lax.rsqrt(count_ref[...])
    for at in range(0, total_ref.shape[1], lanes):
        columns = pl.ds(at, lanes)
        out_ref[:, columns] = (
            features_ref[:, columns].astype(jnp.float32) + total_ref[:, columns] * scale
        ).astype(jnp.bfloat16)


def combine(targets, features, dense, degree, tiles, received):
    rows, width = features.shape
    _, cap, parts = targets.shape
    return pl.pallas_call(
        functools.partial(combine_kernel, parts, cap),
        out_shape=jax.ShapeDtypeStruct((rows, width), jnp.bfloat16),
        in_specs=[smem()] + [vmem()] * 5,
        out_specs=vmem(),
        scratch_shapes=[
            pltpu.VMEM((rows, width), jnp.float32),
            pltpu.VMEM((rows, 128), jnp.float32),
        ],
        compiler_params=params(),
        cost_estimate=pl.CostEstimate(
            flops=4 * rows * width * tiles.shape[2], bytes_accessed=8 * rows * width,
            transcendentals=0,
        ),
        name="combine",
    )(targets, features, dense, degree, tiles, received)


def perceptron_kernel(first_masks, second_masks, combined_ref, *refs):
    out_ref, first_ref, second_ref, hidden_ref, first_sems, second_sems = refs[-6:]
    count = len(first_masks)
    first_copies = load_pieces(refs[:count], first_masks, first_ref, first_sems)
    second_copies = load_pieces(refs[count:-6], second_masks, second_ref, second_sems)
    for copy in first_copies:
        copy.wait()
    hidden = hidden_ref.shape[1]
    step = min(hidden, 512)

    @pl.loop(0, hidden // step)
    def _(at):
        columns = pl.ds(pl.multiple_of(at * step, step), step)
        gated = jnp.dot(
            combined_ref[...], first_ref[:, columns], preferred_element_type=jnp.float32
        )
        hidden_ref[:, columns] = jnp.maximum(gated, 0.0).astype(jnp.bfloat16)

    for copy in second_copies:
        copy.wait()
    width = out_ref.shape[1]
    wide_step = min(width, 256)

    @pl.loop(0, width // wide_step)
    def _(at):
        columns = pl.ds(pl.multiple_of(at * wide_step, wide_step), wide_step)
        out_ref[:, columns] = jnp.dot(
            hidden_ref[...], second_ref[:, columns], preferred_element_type=jnp.float32
        ).astype(jnp.bfloat16)


def perceptron(combined, first, first_masks, second, second_masks):
    rows, width = combined.shape
    hidden = first[0].shape[-1]
    return pl.pallas_call(
        functools.partial(perceptron_kernel, first_masks, second_masks),
        out_shape=jax.ShapeDtypeStruct((rows, width), jnp.bfloat16),
        in_specs=[vmem()] + [hbm()] * (len(first) + len(second)),
        out_specs=vmem(),
        scratch_shapes=[
            pltpu.VMEM((width, hidden), jnp.bfloat16),
            pltpu.VMEM((hidden, width), jnp.bfloat16),
            pltpu.VMEM((rows, hidden), jnp.bfloat16),
            pltpu.SemaphoreType.DMA((sum(len(group) for group in first_masks),)),
            pltpu.SemaphoreType.DMA((sum(len(group) for group in second_masks),)),
        ],
        compiler_params=params(),
        cost_estimate=pl.CostEstimate(
            flops=4 * rows * width * hidden, bytes_accessed=4 * width * hidden, transcendentals=0
        ),
        name="perceptron",
    )(combined, *first, *second)


def first_pieces(shard, wide, order):
    pieces = {0: shard}
    for bit in order:
        pieces[bit] = swap(shard, wide, bit)
    return pieces


def other_pieces(pieces, wide, order):
    late = {}
    known = [order[0]]
    for bit in order[1:]:
        for mask in known:
            held = late[mask] if mask in late else pieces[mask]
            late[mask ^ bit] = swap(held, wide, bit)
        known = known + [bit] + [mask ^ bit for mask in known]
    return late


def crossed(masks):
    return tuple(mask ^ 1 for mask in masks)


def shards(
    features,
    stripe_owner,
    dense_weight,
    sparse_weight,
    send_blocks,
    target_block,
    first_weight,
    second_weight,
    wide,
    narrow,
):
    block_rows = sparse_weight.shape[2]
    stripes = stripe_owner.shape[1]
    bits = [1 << at for at in range(1, wide.bit_length() - 1)]
    orders = (bits, bits[::-1])
    hops = len(bits)
    me, part = lax.axis_index("wide"), lax.axis_index("narrow")
    owners = lax.dynamic_index_in_dim(stripe_owner, part, 0, keepdims=False)
    core = me & 1
    lists = jnp.transpose(send_blocks, (0, 2, 1))
    targets = jnp.transpose(target_block, (0, 2, 1))

    weights = [
        first_pieces(shard, wide, order)
        for shard, order in zip((first_weight, second_weight), orders)
    ]
    picked, kept, given = pick(lists, features, block_rows)
    received = lax.all_to_all(picked, "narrow", 0, 0)

    given = swap(given, wide, 1)
    carried = [jnp.where((owners[k] & 1) == core, kept, given) for k in range(stripes)]
    for hop in range(hops):
        for k in range(stripes):
            bit = orders[k % 2][hop]
            came = swap(carried[k], wide, bit)
            carried[k] = jnp.where(((owners[k] ^ me) & bit) == 0, carried[k], came)
    mine = jnp.stack(carried)
    other = swap(mine, wide, 1)

    dense, degree = prepare(dense_weight)

    early_masks = [tuple(pieces) for pieces in weights]
    stacks = join([list(pieces.values()) for pieces in weights], [degree])
    crossed_stacks = [swap(stack, wide, 1) for stack in stacks]
    forward = tie(
        [pieces[mask] for pieces, order in zip(weights, orders) for mask in order[:-1]],
        crossed_stacks,
    )
    at = 0
    for pieces, order in zip(weights, orders):
        for mask in order[:-1]:
            pieces[mask] = forward[at]
            at += 1
    more = [other_pieces(pieces, wide, order) for pieces, order in zip(weights, orders)]
    ends = [
        list(pieces.values())[0] if len(pieces) == 1 else jnp.stack(list(pieces.values()))
        for pieces in more
    ]
    more_masks = [tuple(pieces) for pieces in more]
    refs, masks = [], []
    for at in range(2):
        refs.append((stacks[at], crossed_stacks[at], ends[at], swap(ends[at], wide, 1)))
        masks.append(
            (early_masks[at], crossed(early_masks[at]), more_masks[at], crossed(more_masks[at]))
        )

    dense_total = dense_sum(dense, mine, other)
    combined = combine(targets, features, dense_total, degree, sparse_weight, received)
    return perceptron(combined, refs[0], masks[0], refs[1], masks[1])


def solution(mesh):
    placed = (
        P(("wide", "narrow"), None),
        P(),
        P(("wide", "narrow"), None),
        P(("wide", "narrow"), None, None, None),
        P(("wide", "narrow"), None, None),
        P(("wide", "narrow"), None, None),
        P("wide", None),
        P("wide", None),
    )
    local = functools.partial(shards, wide=mesh.shape["wide"], narrow=mesh.shape["narrow"])
    return jax.shard_map(
        local, mesh=mesh, in_specs=placed, out_specs=P(("wide", "narrow"), None), check_vma=False
    )
```

time: 80.8 us -> 56.9 us (0.70)
  waiting for transfers between devices: 37.8 us -> 16.7 us
  Pallas kernels: 14.2 us -> 11.8 us
  other arithmetic: 2.45 us -> 1.16 us
  starting transfers between devices: 18 us -> 19.1 us
    ppermute x3 -> x0, waiting for transfers between devices: 20.4 us -> none  [turn(): lax.ppermute(block, 'narrow', [(i, (i + step) % count) for i in range(cou...]
    ppermute x3 -> x0, starting transfers between devices: 6.14 us -> none  [turn(): lax.ppermute(block, 'narrow', [(i, (i + step) % count) for i in range(cou...]
    all_to_all x0 -> x1, starting transfers between devices: none -> 5 us  [shards(): received = lax.all_to_all(picked, 'narrow', 0, 0)]
    ppermute x13 -> x16, starting transfers between devices: 11.9 us -> 14.1 us  [swap(): return lax.ppermute(block, 'wide', [(i, i ^ bit) for i in range(count)])]
    pallas_call x2 -> x4, Pallas kernels: 10.1 us -> 8.79 us  [the longest x1 6.16 us: perceptron(): pl.pallas_call(functools.partial(perceptron_kernel, first_masks, second_m...]
    concatenate x3 -> x0, other arithmetic: 1.15 us -> none  [the longest x2 1.1 us: shards(): first = jnp.concatenate([first, first_new])]
    pallas_call x1, Pallas kernels: 1.8 us -> 0.72 us  [dense_sum(): pl.pallas_call(dense_kernel, out_shape=jax.ShapeDtypeStruct((rows, width)...]
    dynamic_slice x1 -> x0, local copies, waits for them, and re-layouts: 1.01 us -> none  [shards(): lax.dynamic_slice_in_dim(features, (1 - core) * half, half)]
  transfers between devices with their start and end apart: 16 -> 17, of which waited for: 7 -> 5; matrix products, arithmetic and copies ran while one was open for 4% -> 3% of each run, Pallas kernels for 13% -> 7%
where the time goes in v2:
time: 56.9 us; the launch traced here: 56.5 us
  starting transfers between devices  19.1 us (34%)
  waiting for transfers between devices  16.7 us (29%)
  Pallas kernels  11.8 us (21%)
  local copies, waits for them, and re-layouts  4.97 us (9%)
  between operations  2.83 us (5%)
  other arithmetic  1.16 us (2%)
    ppermute x16, waiting for transfers between devices, swap(): return lax.ppermute(block, 'wide', [(i, i ^ bit) for i in range(count)])  16.7 us
    ppermute x16, starting transfers between devices, swap(): return lax.ppermute(block, 'wide', [(i, i ^ bit) for i in range(count)])  14.1 us
    pallas_call x1, Pallas kernels, perceptron(): pl.pallas_call(functools.partial(perceptron_kernel, first_masks, second_m...  6.16 us
    all_to_all x1, starting transfers between devices, shards(): received = lax.all_to_all(picked, 'narrow', 0, 0)  5 us
    unnamed x22, local copies, waits for them, and re-layouts  4.31 us
    pallas_call x1, Pallas kernels, pick(): pl.pallas_call(functools.partial(pick_kernel, parts, cap, block_rows), ou...  1.68 us
    pallas_call x1, Pallas kernels, combine(): pl.pallas_call(functools.partial(combine_kernel, parts, cap), out_shape=j...  1.42 us
    pallas_call x1, Pallas kernels, join(): pl.pallas_call(functools.partial(join_kernel, sizes), out_shape=[jax.Shap...  1.21 us
  transfers between devices with their start and end apart: 17, of which 5 were waited for; matrix products, arithmetic and copies ran while one was open for 3% of the time, Pallas kernels for 7%

profile of v2, /device:TPU:0, one launch (start us, length us, event | category | flops | bytes accessed | tf_op | source)
XLA Modules:
  0.0 56.5 jit_solution(2300194869052670094)
XLA Ops:
  0.0 1.1 %copy-done.2 = bf16[512,512]{1,0:T(8,128)(2,1)S(1)} copy-done((bf16[512,512]{1,0:T(8,128)(2,1)S(1)}, bf16[512,512]{1,0:T(8,128)(2,1)}, u32[]{:S(2)}) %copy-start.2) | copy-done | bytes 524312
  1.1 0.7 %copy-done.9 = s32[1,4,2]{1,2,0:T(2,128)S(1)} copy-done((s32[1,4,2]{1,2,0:T(2,128)S(1)}, s32[1,4,2]{1,2,0:T(2,128)}, u32[]{:S(2)}) %copy-start.9) | copy-done | bytes 56
  1.7 1.7 %pick_blocks.1 = (bf16[4,256,512]{2,1,0:T(8,128)(2,1)}, bf16[256,512]{1,0:T(8,128)(2,1)S(1)}, bf16[256,512]{1,0:T(8,128)(2,1)S(1)}) custom-call(s32[1,2,4]{2,1,0:T(2,128)S(1)} %bitcast.8, bf16[512,512]{1,0:T(8,128)(2,1)S(1)} %copy-done.2), custom_call_target="tpu_custom_call" | custom-call | tf_op jit(solution)/shard_map/pick_blocks/pallas_call | solution.py:76
  3.4 0.5 collective-permute-start
  3.9 2.6 %collective-permute-start.6 = (bf16[64,2048]{1,0:T(8,128)(2,1)}, bf16[64,2048]{1,0:T(8,128)(2,1)S(1)}, u32[]{:S(2)}, u32[]{:S(2)}) collective-permute-start(bf16[64,2048]{1,0:T(8,128)(2,1)} %refs_0_.1), channel_id=1, source_target_pairs={{0,8},{4,12},{8,0},{12,4},{16,24},{20,28},{24,16},{28,20},{1,9},{5... | collective-permute-start | bytes 786440 | tf_op jit(solution)/shard_map/ppermute | solution.py:35
  6.5 1.6 %collective-permute-start.7 = (bf16[64,2048]{1,0:T(8,128)(2,1)}, bf16[64,2048]{1,0:T(8,128)(2,1)S(1)}, u32[]{:S(2)}, u32[]{:S(2)}) collective-permute-start(bf16[64,2048]{1,0:T(8,128)(2,1)} %refs_0_.1), channel_id=1, source_target_pairs={{0,16},{4,20},{8,24},{12,28},{16,0},{20,4},{24,8},{28,12},{1,17},{... | collective-permute-start | bytes 786440 | tf_op jit(solution)/shard_map/ppermute | solution.py:35
  8.1 0.5 collective-permute-start.8
  8.5 0.1 collective-permute-start.9
  8.6 0.1 constant_dynamic-slice_fusion
  8.7 0.6 %fusion = (s32[1,1]{0,1:T(1,128)}, s32[1,1]{0,1:T(1,128)}) fusion(s32[1,2]{0,1:T(2,128)S(1)} %constant_dynamic-slice_fusion), kind=kLoop, calls=%fused_computation.8 | loop fusion | bytes 16 | tf_op jit(solution)/shard_map/slice | solution.py:376
  10.6 2.0 %collective-permute-start.1 = (bf16[256,512]{1,0:T(8,128)(2,1)S(1)}, bf16[256,512]{1,0:T(8,128)(2,1)}, u32[]{:S(2)}, u32[]{:S(2)}) collective-permute-start(bf16[256,512]{1,0:T(8,128)(2,1)S(1)} %get-tuple-element.23), channel_id=1, source_target_pairs={{0,8},{4,12},{8,0},{12,4},{16,24},{20,28},{24,16},{28,20},{1,9},{5... | collective-permute-start | bytes 786440 | tf_op jit(solution)/shard_map/ppermute | solution.py:35
  12.6 1.2 %collective-permute-done.6.refs_1_.refs_0_ = bf16[64,2048]{1,0:T(8,128)(2,1)S(1)} collective-permute-done((bf16[64,2048]{1,0:T(8,128)(2,1)}, bf16[64,2048]{1,0:T(8,128)(2,1)S(1)}, u32[]{:S(2)}, u32[]{:S(2)}) %collective-permute-start.6) | collective-permute-done | bytes 262176 | tf_op jit(solution)/shard_map/ppermute | solution.py:35
  13.9 2.0 %collective-permute-start.3 = (bf16[256,512]{1,0:T(8,128)(2,1)S(1)}, bf16[256,512]{1,0:T(8,128)(2,1)}, u32[]{:S(2)}, u32[]{:S(2)}) collective-permute-start(bf16[256,512]{1,0:T(8,128)(2,1)S(1)} %get-tuple-element.24), channel_id=1, source_target_pairs={{0,16},{4,20},{8,24},{12,28},{16,0},{20,4},{24,8},{28,12},{1,17},{... | collective-permute-start | bytes 786440 | tf_op jit(solution)/shard_map/ppermute | solution.py:35
  15.9 5.0 %all-to-all-start = ((bf16[4,256,512]{2,1,0:T(8,128)(2,1)}), bf16[4,256,512]{2,1,0:T(8,128)(2,1)S(1)}, u32[]{:S(2)}, u32[]{:S(2)}) async-start(bf16[4,256,512]{2,1,0:T(8,128)(2,1)} %get-tuple-element.18), calls=%async_computation | async-start | bytes 2097152 | tf_op jit(solution)/shard_map/all_to_all | solution.py:368
  22.2 1.6 %copy-done.1 = s32[512,1024]{1,0:T(8,128)S(1)} copy-done((s32[512,1024]{1,0:T(8,128)S(1)}, s32[512,1024]{1,0:T(8,128)}, u32[]{:S(2)}) %copy-start.1) | copy-done | bytes 2097176
  23.8 0.6 %dense_rows.1 = (bf16[512,1024]{1,0:T(8,128)(2,1)S(1)}, f32[512,1]{1,0:T(8,128)S(1)}) custom-call(s32[512,1024]{1,0:T(8,128)S(1)} %copy-done.1), custom_call_target="tpu_custom_call" | custom-call | flops 1048576 | bytes 3145728 | tf_op jit(solution)/shard_map/dense_rows/pallas_call | solution.py:147
  24.4 1.0 %copy-done.4 = bf16[512,1024]{1,0:T(8,128)(2,1)} copy-done((bf16[512,1024]{1,0:T(8,128)(2,1)}, bf16[512,1024]{1,0:T(8,128)(2,1)S(1)}, u32[]{:S(2)}) %copy-start.4) | copy-done | bytes 1048600
  25.4 1.2 %join_pieces.1 = (bf16[3,64,2048]{2,1,0:T(8,128)(2,1)}, bf16[3,256,512]{2,1,0:T(8,128)(2,1)}) custom-call(bf16[64,2048]{1,0:T(8,128)(2,1)S(1)} %copy-done.6, bf16[64,2048]{1,0:T(8,128)(2,1)S(1)} %collective-permute-done.6.refs_1_.refs_0_, bf16[64,2048]{1,0:T(8,128)(2,1)S(1)} %collective-permute-done.7.refs_2_, bf16[256,512]{1,0:T(8,128)(2,1)S(1)} %copy-done.7, ...), custom_call_target="tpu_custom_call" | custom-call | tf_op jit(solution)/shard_map/join_pieces/pallas_call | solution.py:109
  26.6 0.1 collective-permute-start.10
  26.7 0.5 collective-permute-start.11
  27.2 1.0 %broadcast_select_fusion.3 = bf16[256,512]{1,0:T(8,128)(2,1)S(1)} fusion(bf16[256,512]{1,0:T(8,128)(2,1)S(1)} %get-tuple-element.23, bf16[256,512]{1,0:T(8,128)(2,1)} %collective-permute-done.1, pred[]{:T(512)S(6)} %eq.19), kind=kLoop, calls=%fused_computation.6 | loop fusion | flops 131072 | bytes 786433 | tf_op jit(solution)/shard_map/jit(_where)/select_n | solution.py:376
  28.1 0.6 %collective-permute-start.2 = (bf16[256,512]{1,0:T(8,128)(2,1)S(1)}, bf16[256,512]{1,0:T(8,128)(2,1)S(1)}, u32[]{:S(2)}, u32[]{:S(2)}) collective-permute-start(bf16[256,512]{1,0:T(8,128)(2,1)S(1)} %broadcast_select_fusion.3), channel_id=1, source_target_pairs={{0,16},{4,20},{8,24},{12,28},{16,0},{20,4},{24,8},{28,12},{1,17},{... | collective-permute-start | bytes 786440 | tf_op jit(solution)/shard_map/ppermute | solution.py:35
  28.8 0.6 %collective-permute-start.4 = (bf16[256,512]{1,0:T(8,128)(2,1)S(1)}, bf16[256,512]{1,0:T(8,128)(2,1)S(1)}, u32[]{:S(2)}, u32[]{:S(2)}) collective-permute-start(bf16[256,512]{1,0:T(8,128)(2,1)S(1)} %broadcast_select_fusion.1), channel_id=1, source_target_pairs={{0,8},{4,12},{8,0},{12,4},{16,24},{20,28},{24,16},{28,20},{1,9},{5... | collective-permute-start | bytes 786440 | tf_op jit(solution)/shard_map/ppermute | solution.py:35
  29.4 7.1 %collective-permute-done.2 = bf16[256,512]{1,0:T(8,128)(2,1)S(1)} collective-permute-done((bf16[256,512]{1,0:T(8,128)(2,1)S(1)}, bf16[256,512]{1,0:T(8,128)(2,1)S(1)}, u32[]{:S(2)}, u32[]{:S(2)}) %collective-permute-start.2) | collective-permute-done | bytes 262176 | tf_op jit(solution)/shard_map/ppermute | solution.py:35
  36.5 0.3 collective-permute-done.4
  37.1 2.5 %collective-permute-start.12 = (bf16[64,2048]{1,0:T(8,128)(2,1)S(1)}, bf16[64,2048]{1,0:T(8,128)(2,1)S(1)}, u32[]{:S(2)}, u32[]{:S(2)}) collective-permute-start(bf16[64,2048]{1,0:T(8,128)(2,1)S(1)} %get-tuple-element.21), channel_id=1, source_target_pairs={{0,16},{4,20},{8,24},{12,28},{16,0},{20,4},{24,8},{28,12},{1,17},{... | collective-permute-start | bytes 786440 | tf_op jit(solution)/shard_map/ppermute | solution.py:35
  39.6 0.5 collective-permute-start.14
  40.2 6.4 %collective-permute-done.12.refs_2_ = bf16[64,2048]{1,0:T(8,128)(2,1)S(1)} collective-permute-done((bf16[64,2048]{1,0:T(8,128)(2,1)S(1)}, bf16[64,2048]{1,0:T(8,128)(2,1)S(1)}, u32[]{:S(2)}, u32[]{:S(2)}) %collective-permute-start.12) | collective-permute-done | bytes 262176 | tf_op jit(solution)/shard_map/ppermute | solution.py:35
  46.5 1.6 %collective-permute-done.14.refs_6_ = bf16[256,512]{1,0:T(8,128)(2,1)} collective-permute-done((bf16[256,512]{1,0:T(8,128)(2,1)S(1)}, bf16[256,512]{1,0:T(8,128)(2,1)}, u32[]{:S(2)}, u32[]{:S(2)}) %collective-permute-start.14) | collective-permute-done | bytes 262176 | tf_op jit(solution)/shard_map/ppermute | solution.py:35
  48.1 0.7 %dense_product.1.dense_ref = f32[512,512]{1,0:T(8,128)S(1)} custom-call(bf16[512,1024]{1,0:T(8,128)(2,1)S(1)} %copy-done.5, bf16[2,256,512]{2,1,0:T(8,128)(2,1)S(1)} %pad_maximum_fusion.mine_ref, bf16[2,256,512]{2,1,0:T(8,128)(2,1)S(1)} %collective-permute-done.5.other_ref), custom_call_target="tpu_custom_call" | custom-call | flops 536870912 | bytes 4194304 | tf_op jit(solution)/shard_map/dense_product/pallas_call | solution.py:184
  48.9 1.4 %combine.1.combined_ref = bf16[512,512]{1,0:T(8,128)(2,1)S(1)} custom-call(s32[1,2,4]{2,1,0:T(2,128)S(1)} %bitcast.9, bf16[512,512]{1,0:T(8,128)(2,1)S(1)} %copy-done.3, f32[512,512]{1,0:T(8,128)S(1)} %dense_product.1.dense_ref, f32[512,1]{1,0:T(8,128)S(1)} %get-tuple-element.17.degree_ref.refs_6_, s32[1,4,128,128]{3,2,1,0:T(8,128)S(1)} %copy-done.8, ...), custom_call_target="tpu_custom_call" | custom-call | flops 134217728 | bytes 2097152 | tf_op jit(solution)/shard_map/combine/pallas_call | solution.py:246
  50.3 6.2 %perceptron.1 = bf16[512,512]{1,0:T(8,128)(2,1)} custom-call(bf16[512,512]{1,0:T(8,128)(2,1)S(1)} %combine.1.combined_ref, bf16[3,64,2048]{2,1,0:T(8,128)(2,1)} %get-tuple-element.19.refs_0_, bf16[3,64,2048]{2,1,0:T(8,128)(2,1)} %collective-permute-done.10.refs_2_.refs_1_, bf16[64,2048]{1,0:T(8,128)(2,1)S(1)} %collective-permute-done.12.refs_2_, ...), custom_call_target="tpu_custom_call" | custom-call | flops 2147483648 | bytes 4194304 | tf_op jit(solution)/shard_map/perceptron/pallas_call | solution.py:298
  (39 shorter events, 0.3 us)
Async XLA Ops:
  0.0 8.6 %copy-start = (s32[4,2]{0,1:T(2,128)S(1)}, s32[4,2]{0,1:T(2,128)}, u32[]{:S(2)}) copy-start(s32[4,2]{0,1:T(2,128)} %param.9) | copy-start | bytes 100
  0.0 1.1 %copy-start.2 = (bf16[512,512]{1,0:T(8,128)(2,1)S(1)}, bf16[512,512]{1,0:T(8,128)(2,1)}, u32[]{:S(2)}) copy-start(bf16[512,512]{1,0:T(8,128)(2,1)} %features_ref.3) | copy-start | bytes 1572868
  1.1 0.7 %copy-start.9 = (s32[1,4,2]{1,2,0:T(2,128)S(1)}, s32[1,4,2]{1,2,0:T(2,128)}, u32[]{:S(2)}) copy-start(s32[1,4,2]{1,2,0:T(2,128)} %param.12) | copy-start | bytes 100
  3.4 7.1 %collective-permute-start = (bf16[256,512]{1,0:T(8,128)(2,1)S(1)}, bf16[256,512]{1,0:T(8,128)(2,1)S(1)}, u32[]{:S(2)}, u32[]{:S(2)}) collective-permute-start(bf16[256,512]{1,0:T(8,128)(2,1)S(1)} %get-tuple-element.16), channel_id=1, source_target_pairs={{0,4},{4,0},{8,12},{12,8},{16,20},{20,16},{24,28},{28,24},{1,5},{5... | collective-permute-start | bytes 786440 | tf_op jit(solution)/shard_map/ppermute | solution.py:35
  3.9 9.9 %collective-permute-start.6 = (bf16[64,2048]{1,0:T(8,128)(2,1)}, bf16[64,2048]{1,0:T(8,128)(2,1)S(1)}, u32[]{:S(2)}, u32[]{:S(2)}) collective-permute-start(bf16[64,2048]{1,0:T(8,128)(2,1)} %refs_0_.1), channel_id=1, source_target_pairs={{0,8},{4,12},{8,0},{12,4},{16,24},{20,28},{24,16},{28,20},{1,9},{5... | collective-permute-start | bytes 786440 | tf_op jit(solution)/shard_map/ppermute | solution.py:35
  6.5 18.8 %collective-permute-start.7 = (bf16[64,2048]{1,0:T(8,128)(2,1)}, bf16[64,2048]{1,0:T(8,128)(2,1)S(1)}, u32[]{:S(2)}, u32[]{:S(2)}) collective-permute-start(bf16[64,2048]{1,0:T(8,128)(2,1)} %refs_0_.1), channel_id=1, source_target_pairs={{0,16},{4,20},{8,24},{12,28},{16,0},{20,4},{24,8},{28,12},{1,17},{... | collective-permute-start | bytes 786440 | tf_op jit(solution)/shard_map/ppermute | solution.py:35
  8.1 17.3 %collective-permute-start.8 = (bf16[256,512]{1,0:T(8,128)(2,1)}, bf16[256,512]{1,0:T(8,128)(2,1)S(1)}, u32[]{:S(2)}, u32[]{:S(2)}) collective-permute-start(bf16[256,512]{1,0:T(8,128)(2,1)} %refs_3_.1), channel_id=1, source_target_pairs={{0,16},{4,20},{8,24},{12,28},{16,0},{20,4},{24,8},{28,12},{1,17},{... | collective-permute-start | bytes 786440 | tf_op jit(solution)/shard_map/ppermute | solution.py:35
  8.5 16.8 %collective-permute-start.9 = (bf16[256,512]{1,0:T(8,128)(2,1)}, bf16[256,512]{1,0:T(8,128)(2,1)S(1)}, u32[]{:S(2)}, u32[]{:S(2)}) collective-permute-start(bf16[256,512]{1,0:T(8,128)(2,1)} %refs_3_.1), channel_id=1, source_target_pairs={{0,8},{4,12},{8,0},{12,4},{16,24},{20,28},{24,16},{28,20},{1,9},{5... | collective-permute-start | bytes 786440 | tf_op jit(solution)/shard_map/ppermute | solution.py:35
  10.6 16.5 %collective-permute-start.1 = (bf16[256,512]{1,0:T(8,128)(2,1)S(1)}, bf16[256,512]{1,0:T(8,128)(2,1)}, u32[]{:S(2)}, u32[]{:S(2)}) collective-permute-start(bf16[256,512]{1,0:T(8,128)(2,1)S(1)} %get-tuple-element.23), channel_id=1, source_target_pairs={{0,8},{4,12},{8,0},{12,4},{16,24},{20,28},{24,16},{28,20},{1,9},{5... | collective-permute-start | bytes 786440 | tf_op jit(solution)/shard_map/ppermute | solution.py:35
  13.9 14.8 %collective-permute-start.3 = (bf16[256,512]{1,0:T(8,128)(2,1)S(1)}, bf16[256,512]{1,0:T(8,128)(2,1)}, u32[]{:S(2)}, u32[]{:S(2)}) collective-permute-start(bf16[256,512]{1,0:T(8,128)(2,1)S(1)} %get-tuple-element.24), channel_id=1, source_target_pairs={{0,16},{4,20},{8,24},{12,28},{16,0},{20,4},{24,8},{28,12},{1,17},{... | collective-permute-start | bytes 786440 | tf_op jit(solution)/shard_map/ppermute | solution.py:35
  15.9 9.5 %copy-start.6 = (bf16[64,2048]{1,0:T(8,128)(2,1)S(1)}, bf16[64,2048]{1,0:T(8,128)(2,1)}, u32[]{:S(2)}) copy-start(bf16[64,2048]{1,0:T(8,128)(2,1)} %refs_0_.1) | copy-start | bytes 786436
  15.9 9.5 %copy-start.7 = (bf16[256,512]{1,0:T(8,128)(2,1)S(1)}, bf16[256,512]{1,0:T(8,128)(2,1)}, u32[]{:S(2)}) copy-start(bf16[256,512]{1,0:T(8,128)(2,1)} %refs_3_.1) | copy-start | bytes 786436
  15.9 33.0 %all-to-all-start = ((bf16[4,256,512]{2,1,0:T(8,128)(2,1)}), bf16[4,256,512]{2,1,0:T(8,128)(2,1)S(1)}, u32[]{:S(2)}, u32[]{:S(2)}) async-start(bf16[4,256,512]{2,1,0:T(8,128)(2,1)} %get-tuple-element.18), calls=%async_computation | async-start | bytes 2097152 | tf_op jit(solution)/shard_map/all_to_all | solution.py:368
  22.2 1.6 %copy-start.1 = (s32[512,1024]{1,0:T(8,128)S(1)}, s32[512,1024]{1,0:T(8,128)}, u32[]{:S(2)}) copy-start(s32[512,1024]{1,0:T(8,128)} %dense_ref.1) | copy-start | bytes 6291460
  24.4 1.0 %copy-start.4 = (bf16[512,1024]{1,0:T(8,128)(2,1)}, bf16[512,1024]{1,0:T(8,128)(2,1)S(1)}, u32[]{:S(2)}) copy-start(bf16[512,1024]{1,0:T(8,128)(2,1)S(1)} %get-tuple-element.14.dense_ref) | copy-start | bytes 3145732
  26.6 10.4 %collective-permute-start.10 = (bf16[3,64,2048]{2,1,0:T(8,128)(2,1)}, bf16[3,64,2048]{2,1,0:T(8,128)(2,1)}, u32[]{:S(2)}, u32[]{:S(2)}) collective-permute-start(bf16[3,64,2048]{2,1,0:T(8,128)(2,1)} %get-tuple-element.19.refs_0_), channel_id=1, source_target_pairs={{0,4},{4,0},{8,12},{12,8},{16,20},{20,16},{24,28},{28,24},{1,5},{5... | collective-permute-start | bytes 2359304 | tf_op jit(solution)/shard_map/ppermute | solution.py:35
  26.7 10.4 %collective-permute-start.11 = (bf16[3,256,512]{2,1,0:T(8,128)(2,1)}, bf16[3,256,512]{2,1,0:T(8,128)(2,1)}, u32[]{:S(2)}, u32[]{:S(2)}) collective-permute-start(bf16[3,256,512]{2,1,0:T(8,128)(2,1)} %get-tuple-element.20.refs_4_), channel_id=1, source_target_pairs={{0,4},{4,0},{8,12},{12,8},{16,20},{20,16},{24,28},{28,24},{1,5},{5... | collective-permute-start | bytes 2359304 | tf_op jit(solution)/shard_map/ppermute | solution.py:35
  28.1 8.4 %collective-permute-start.2 = (bf16[256,512]{1,0:T(8,128)(2,1)S(1)}, bf16[256,512]{1,0:T(8,128)(2,1)S(1)}, u32[]{:S(2)}, u32[]{:S(2)}) collective-permute-start(bf16[256,512]{1,0:T(8,128)(2,1)S(1)} %broadcast_select_fusion.3), channel_id=1, source_target_pairs={{0,16},{4,20},{8,24},{12,28},{16,0},{20,4},{24,8},{28,12},{1,17},{... | collective-permute-start | bytes 786440 | tf_op jit(solution)/shard_map/ppermute | solution.py:35
  28.8 8.1 %collective-permute-start.4 = (bf16[256,512]{1,0:T(8,128)(2,1)S(1)}, bf16[256,512]{1,0:T(8,128)(2,1)S(1)}, u32[]{:S(2)}, u32[]{:S(2)}) collective-permute-start(bf16[256,512]{1,0:T(8,128)(2,1)S(1)} %broadcast_select_fusion.1), channel_id=1, source_target_pairs={{0,8},{4,12},{8,0},{12,4},{16,24},{20,28},{24,16},{28,20},{1,9},{5... | collective-permute-start | bytes 786440 | tf_op jit(solution)/shard_map/ppermute | solution.py:35
  36.5 11.6 %copy-start.5 = (bf16[512,1024]{1,0:T(8,128)(2,1)S(1)}, bf16[512,1024]{1,0:T(8,128)(2,1)}, u32[]{:S(2)}) copy-start(bf16[512,1024]{1,0:T(8,128)(2,1)} %copy-done.4) | copy-start | bytes 3145732
  36.9 11.2 %collective-permute-start.5 = (bf16[2,256,512]{2,1,0:T(8,128)(2,1)S(1)}, bf16[2,256,512]{2,1,0:T(8,128)(2,1)S(1)}, u32[]{:S(2)}, u32[]{:S(2)}) collective-permute-start(bf16[2,256,512]{2,1,0:T(8,128)(2,1)S(1)} %pad_maximum_fusion.mine_ref), channel_id=1, source_target_pairs={{0,4},{4,0},{8,12},{12,8},{16,20},{20,16},{24,28},{28,24},{1,5},{5... | collective-permute-start | bytes 1572872 | tf_op jit(solution)/shard_map/ppermute | solution.py:35
  37.0 11.8 %copy-start.3 = (bf16[512,512]{1,0:T(8,128)(2,1)S(1)}, bf16[512,512]{1,0:T(8,128)(2,1)}, u32[]{:S(2)}) copy-start(bf16[512,512]{1,0:T(8,128)(2,1)} %features_ref.3) | copy-start | bytes 1572868
  37.1 11.8 %copy-start.8 = (s32[1,4,128,128]{3,2,1,0:T(8,128)S(1)}, s32[1,4,128,128]{3,2,1,0:T(8,128)}, u32[]{:S(2)}) copy-start(s32[1,4,128,128]{3,2,1,0:T(8,128)} %tiles_ref.1) | copy-start | bytes 786436
  37.1 11.8 %copy-start.10 = (s32[1,4,2]{1,2,0:T(2,128)S(1)}, s32[1,4,2]{1,2,0:T(2,128)}, u32[]{:S(2)}) copy-start(s32[1,4,2]{1,2,0:T(2,128)} %param.13) | copy-start | bytes 100
  37.1 9.5 %collective-permute-start.12 = (bf16[64,2048]{1,0:T(8,128)(2,1)S(1)}, bf16[64,2048]{1,0:T(8,128)(2,1)S(1)}, u32[]{:S(2)}, u32[]{:S(2)}) collective-permute-start(bf16[64,2048]{1,0:T(8,128)(2,1)S(1)} %get-tuple-element.21), channel_id=1, source_target_pairs={{0,16},{4,20},{8,24},{12,28},{16,0},{20,4},{24,8},{28,12},{1,17},{... | collective-permute-start | bytes 786440 | tf_op jit(solution)/shard_map/ppermute | solution.py:35
  39.6 8.5 %collective-permute-start.14 = (bf16[256,512]{1,0:T(8,128)(2,1)S(1)}, bf16[256,512]{1,0:T(8,128)(2,1)}, u32[]{:S(2)}, u32[]{:S(2)}) collective-permute-start(bf16[256,512]{1,0:T(8,128)(2,1)S(1)} %get-tuple-element.22), channel_id=1, source_target_pairs={{0,8},{4,12},{8,0},{12,4},{16,24},{20,28},{24,16},{28,20},{1,9},{5... | collective-permute-start | bytes 786440 | tf_op jit(solution)/shard_map/ppermute | solution.py:35
  46.5 3.8 %collective-permute-start.13 = (bf16[64,2048]{1,0:T(8,128)(2,1)S(1)}, bf16[64,2048]{1,0:T(8,128)(2,1)}, u32[]{:S(2)}, u32[]{:S(2)}) collective-permute-start(bf16[64,2048]{1,0:T(8,128)(2,1)S(1)} %collective-permute-done.12.refs_2_), channel_id=1, source_target_pairs={{0,4},{4,0},{8,12},{12,8},{16,20},{20,16},{24,28},{28,24},{1,5},{5... | collective-permute-start | bytes 786440 | tf_op jit(solution)/shard_map/ppermute | solution.py:35
  48.1 2.2 %collective-permute-start.15 = (bf16[256,512]{1,0:T(8,128)(2,1)}, bf16[256,512]{1,0:T(8,128)(2,1)}, u32[]{:S(2)}, u32[]{:S(2)}) collective-permute-start(bf16[256,512]{1,0:T(8,128)(2,1)} %collective-permute-done.14.refs_6_), channel_id=1, source_target_pairs={{0,4},{4,0},{8,12},{12,8},{16,20},{20,16},{24,28},{28,24},{1,5},{5... | collective-permute-start | bytes 786440 | tf_op jit(solution)/shard_map/ppermute | solution.py:35

commit v3 on v0

v3 whole, which is shorter than its diff:
```python
import functools

import jax
import jax.numpy as jnp
from jax import lax
from jax.experimental import pallas as pl
from jax.experimental.pallas import tpu as pltpu
from jax.sharding import PartitionSpec as P

LANES = 128
ABSENT = 64.0
VMEM_LIMIT = 48 * 1024 * 1024
SLACK = 0
LARGE_LIMIT = 48 * 1024 * 1024
SLACK_BLOCKS = 0
LAYER_LIMIT = 52 * 1024 * 1024
SLACK_STRIPES = 4 * 10**9


def params(limit=VMEM_LIMIT):
    return pltpu.CompilerParams(vmem_limit_bytes=limit)


def vmem():
    return pl.BlockSpec(memory_space=pltpu.VMEM)


def smem():
    return pl.BlockSpec(memory_space=pltpu.SMEM)


def anywhere():
    return pl.BlockSpec(memory_space=pl.ANY)


def hbm():
    return pl.BlockSpec(memory_space=pltpu.HBM)


def swap(block, count, bit):
    return lax.ppermute(block, "wide", [(i, i ^ bit) for i in range(count)])


def pick_kernel(parts, cap, block_rows, lists_ref, features_ref, out_ref, empty_ref, sems):
    empty_ref[...] = jnp.full(empty_ref.shape, ABSENT, empty_ref.dtype)
    copies = []
    for to in range(parts):
        for slot in range(cap):
            listed = lists_ref[0, slot, to]
            target = out_ref.at[to, pl.ds(slot * block_rows, block_rows)]
            sem = sems.at[len(copies)]
            start = pl.multiple_of(jnp.maximum(listed, 0) * block_rows, block_rows)
            real = pltpu.make_async_copy(features_ref.at[pl.ds(start, block_rows)], target, sem)
            blank = pltpu.make_async_copy(empty_ref, target, sem)

            @pl.when(listed >= 0)
            def _():
                real.start()

            @pl.when(listed < 0)
            def _():
                blank.start()

            copies.append(blank)
    for copy in copies:
        copy.wait()


def pick(lists, features, block_rows):
    _, cap, parts = lists.shape
    width = features.shape[1]
    return pl.pallas_call(
        functools.partial(pick_kernel, parts, cap, block_rows),
        out_shape=jax.ShapeDtypeStruct((parts, cap * block_rows, width), features.dtype),
        in_specs=[smem(), hbm()],
        out_specs=hbm(),
        scratch_shapes=[
            pltpu.VMEM((block_rows, width), features.dtype),
            pltpu.SemaphoreType.DMA((parts * cap,)),
        ],
        compiler_params=params(LARGE_LIMIT),
        name="pick_blocks",
    )(lists, features)


def halves_kernel(owners_ref, mine_ref, other_ref, *rest):
    outs, sems = rest[:-1], rest[-1]
    core, part = lax.rem(lax.axis_index("wide"), 2), lax.axis_index("narrow")
    half = outs[0].shape[0]
    rows = pl.ds(pl.multiple_of(core * half, half), half)
    copies = []
    for k, out in enumerate(outs):
        own = (owners_ref[k, part] & 1) == core
        kept = pltpu.make_async_copy(mine_ref.at[rows], out, sems.at[k])
        came = pltpu.make_async_copy(other_ref.at[rows], out, sems.at[k])

        @pl.when(own)
        def _():
            kept.start()

        @pl.when(jnp.logical_not(own))
        def _():
            came.start()

        copies.append(kept)
    for copy in copies:
        copy.wait()


def halves(owners, mine, other):
    rows, width = mine.shape
    stripes = owners.shape[0]
    return pl.pallas_call(
        halves_kernel,
        out_shape=[jax.ShapeDtypeStruct((rows // 2, width), mine.dtype)] * stripes,
        in_specs=[smem(), anywhere(), anywhere()],
        out_specs=[anywhere()] * stripes,
        scratch_shapes=[pltpu.SemaphoreType.DMA((stripes,))],
        compiler_params=params(),
        name="stripe_halves",
    )(owners, mine, other)


def choose_kernel(bits, stacked, others, owners_ref, *refs):
    count = len(bits)
    refs = refs[: 2 * count] + refs[2 * count + others :]
    sems = refs[-1]
    me, part = lax.axis_index("wide"), lax.axis_index("narrow")
    copies = []
    for k, bit in enumerate(bits):
        out = refs[2 * count].at[k] if stacked else refs[2 * count + k]
        same = ((owners_ref[k, part] ^ me) & bit) == 0
        kept = pltpu.make_async_copy(refs[k], out, sems.at[k])
        came = pltpu.make_async_copy(refs[count + k], out, sems.at[k])

        @pl.when(same)
        def _():
            kept.start()

        @pl.when(jnp.logical_not(same))
        def _():
            came.start()

        copies.append(kept)
    for copy in copies:
        copy.wait()


def choose(owners, bits, carried, came, stacked, after):
    count = len(bits)
    shape, dtype = carried[0].shape, carried[0].dtype
    if stacked:
        out_shape, out_specs = jax.ShapeDtypeStruct((count,) + shape, dtype), anywhere()
    else:
        out_shape, out_specs = [jax.ShapeDtypeStruct(shape, dtype)] * count, [anywhere()] * count
    return pl.pallas_call(
        functools.partial(choose_kernel, bits, stacked, len(after)),
        out_shape=out_shape,
        in_specs=[smem()] + [anywhere()] * (2 * count + len(after)),
        out_specs=out_specs,
        scratch_shapes=[pltpu.SemaphoreType.DMA((count,))],
        compiler_params=params(),
        name="stripe_choice",
    )(owners, *carried, *came, *after)


def pack_kernel(first_ref, second_ref, out_ref, sems):
    rows, width = first_ref.shape[0], out_ref.shape[2]
    copies = [pltpu.make_async_copy(second_ref, out_ref.at[1], sems.at[0])]
    for at in range(first_ref.shape[1] // width):
        copies.append(
            pltpu.make_async_copy(
                first_ref.at[:, pl.ds(at * width, width)],
                out_ref.at[0, pl.ds(at * rows, rows)],
                sems.at[1 + at],
            )
        )
    for copy in copies:
        copy.start()
    for copy in copies:
        copy.wait()


def pack(first, second):
    blocks = first.shape[1] // second.shape[1]
    return pl.pallas_call(
        pack_kernel,
        out_shape=jax.ShapeDtypeStruct((2,) + second.shape, second.dtype),
        in_specs=[hbm()] * 2,
        out_specs=hbm(),
        scratch_shapes=[pltpu.SemaphoreType.DMA((1 + blocks,))],
        compiler_params=params(LARGE_LIMIT),
        name="pack_weights",
    )(first, second)


def split_kernel(parts, count, *refs):
    ins, stack_ref, outs, sems = refs[:count], refs[-2 - len(parts)], refs[-1 - len(parts) : -1], refs[-1]
    copies = []
    for out, (at, part) in zip(outs, parts):
        copies.append(pltpu.make_async_copy(ins[at].at[part], out, sems.at[len(copies)]))
    for at in range(count):
        copies.append(pltpu.make_async_copy(ins[at], stack_ref.at[at], sems.at[len(copies)]))
    for copy in copies:
        copy.start()
    for copy in copies:
        copy.wait()


def split(packs, parts, after):
    shape, dtype = packs[0].shape, packs[0].dtype
    stack, *outs = pl.pallas_call(
        functools.partial(split_kernel, parts, len(packs)),
        out_shape=[jax.ShapeDtypeStruct((len(packs),) + shape, dtype)]
        + [jax.ShapeDtypeStruct(shape[1:], dtype)] * len(parts),
        in_specs=[anywhere()] * (len(packs) + len(after)),
        out_specs=[anywhere()] * (1 + len(parts)),
        scratch_shapes=[pltpu.SemaphoreType.DMA((len(parts) + len(packs),))],
        compiler_params=params(),
        name="split_packs",
    )(*packs, *after)
    return stack, outs


def tie_kernel(*refs):
    pass


def tie(blocks, after, work=0):
    return pl.pallas_call(
        tie_kernel,
        out_shape=[jax.ShapeDtypeStruct(block.shape, block.dtype) for block in blocks],
        in_specs=[anywhere()] * (len(blocks) + len(after)),
        out_specs=[anywhere()] * len(blocks),
        input_output_aliases={at: at for at in range(len(blocks))},
        compiler_params=params(),
        cost_estimate=pl.CostEstimate(flops=work, bytes_accessed=0, transcendentals=0),
        name="tie",
    )(*blocks, *after)


def prepare_kernel(dense_ref, out_ref, degree_ref):
    values = dense_ref[...]
    out_ref[...] = values.astype(jnp.float32).astype(jnp.bfloat16)
    sums = 1.0 + jnp.sum(values, axis=1, keepdims=True).astype(jnp.float32)
    degree_ref[...] = jnp.broadcast_to(sums, degree_ref.shape)


def prepare(dense_weight):
    rows, columns = dense_weight.shape
    step = rows // 4
    return pl.pallas_call(
        prepare_kernel,
        grid=(rows // step,),
        out_shape=[
            jax.ShapeDtypeStruct((rows, columns), jnp.bfloat16),
            jax.ShapeDtypeStruct((rows, LANES), jnp.float32),
        ],
        in_specs=[pl.BlockSpec((step, columns), lambda i: (i, 0))],
        out_specs=[
            pl.BlockSpec((step, columns), lambda i: (i, 0)),
            pl.BlockSpec((step, LANES), lambda i: (i, 0)),
        ],
        compiler_params=params(),
        cost_estimate=pl.CostEstimate(
            flops=2 * rows * columns, bytes_accessed=6 * rows * columns, transcendentals=0
        ),
        name="dense_rows",
    )(dense_weight)


def add_stripes(dense_ref, mine_ref, other_ref, total_ref):
    stripes, half, _ = mine_ref.shape
    core = lax.rem(lax.axis_index("wide"), 2)
    total = None
    for stripe in range(stripes):
        for ref, side in ((mine_ref, core), (other_ref, 1 - core)):
            start = pl.multiple_of((2 * stripe + side) * half, half)
            part = jnp.dot(
                dense_ref[:, pl.ds(start, half)], ref[stripe], preferred_element_type=jnp.float32
            )
            total = part if total is None else total + part
    total_ref[...] = total


def add_blocks(targets_ref, tiles_ref, received_ref, total_ref, count_ref):
    _, parts, block_rows, _ = tiles_ref.shape
    for source in range(parts):
        tile = tiles_ref[0, source]
        weight = jnp.sum(tile, axis=1, keepdims=True).astype(jnp.float32)
        tile = tile.astype(jnp.float32).astype(jnp.bfloat16)
        for slot in range(received_ref.shape[1] // block_rows):
            block = received_ref[source, pl.ds(slot * block_rows, block_rows), :]
            present = block[0:1, :].astype(jnp.float32) < ABSENT / 2
            product = jnp.dot(tile, block, preferred_element_type=jnp.float32)
            product = jnp.where(present, product, 0.0)
            start = pl.multiple_of(targets_ref[0, slot, source] * block_rows, block_rows)
            total_ref[pl.ds(start, block_rows), :] += product
            count_ref[pl.ds(start, block_rows), :] += jnp.where(present[:, :LANES], weight, 0.0)


def combine(features_ref, total_ref, count_ref, combined_ref):
    scale = lax.rsqrt(count_ref[...])
    for at in range(0, total_ref.shape[1], LANES):
        columns = pl.ds(at, LANES)
        combined_ref[:, columns] = (
            features_ref[:, columns].astype(jnp.float32) + total_ref[:, columns] * scale
        ).astype(jnp.bfloat16)


def place_first(pieces, first_ref):
    me, blocks = lax.axis_index("wide"), first_ref.shape[0]
    for ref, mask in pieces:
        rows = ref.shape[0] // blocks
        start = pl.multiple_of((me ^ mask) * rows, rows)
        for at in range(blocks):
            first_ref[at, pl.ds(start, rows), :] = ref[pl.ds(at * rows, rows), :]


def place_second(pieces, second_ref):
    me = lax.axis_index("wide")
    for ref, mask in pieces:
        rows = ref.shape[0]
        second_ref[pl.ds(pl.multiple_of((me ^ mask) * rows, rows), rows), :] = ref[...]


def layer_kernel(own, came, late, targets_ref, *refs):
    count = 7 + len(own) + len(came) + len(late)
    held = refs[count + 1 : 2 * count + 1]
    out_ref = refs[count]
    first_ref, second_ref, hidden_ref, total_ref, combined_ref, sems = refs[2 * count + 1 :]
    copies = [
        pltpu.make_async_copy(ref, target, sems.at[at])
        for at, (ref, target) in enumerate(zip(refs[:count], held))
    ]
    for copy in copies:
        copy.start()
    dense_ref, mine_ref, other_ref, count_ref, tiles_ref, received_ref, features_ref = held[:7]
    packs = list(zip(held[7:], own))
    for ref, masks in zip(held[7 + len(own) :], came):
        packs += [(ref.at[at], mask) for at, mask in enumerate(masks)]
    pieces = [[(ref.at[which], mask) for ref, mask in packs] for which in range(2)]
    for ref, (which, masks) in zip(held[7 + len(own) + len(came) :], late):
        pieces[which] += [
            (ref if len(masks) == 1 else ref.at[at], mask) for at, mask in enumerate(masks)
        ]
    for copy in copies[:3]:
        copy.wait()
    add_stripes(dense_ref, mine_ref, other_ref, total_ref)
    for copy in copies[3:7]:
        copy.wait()
    add_blocks(targets_ref, tiles_ref, received_ref, total_ref, count_ref)
    combine(features_ref, total_ref, count_ref, combined_ref)
    for copy in copies[7:]:
        copy.wait()
    place_first(pieces[0], first_ref)
    width = first_ref.shape[2]
    for at in range(first_ref.shape[0]):
        gated = jnp.dot(combined_ref[...], first_ref[at], preferred_element_type=jnp.float32)
        hidden_ref[:, pl.ds(at * width, width)] = jnp.maximum(gated, 0.0).astype(jnp.bfloat16)
    place_second(pieces[1], second_ref)
    out_ref[...] = jnp.dot(
        hidden_ref[...], second_ref[...], preferred_element_type=jnp.float32
    ).astype(jnp.bfloat16)


def layer(targets, arrays, own, came, late, count):
    features = arrays[-1]
    rows, width = features.shape
    refs = list(arrays) + [block for block, _ in own + came] + [block for block, _, _ in late]
    depth = own[0][0].shape[1] * count
    return pl.pallas_call(
        functools.partial(
            layer_kernel,
            tuple(mask for _, mask in own),
            tuple(masks for _, masks in came),
            tuple((which, masks) for _, which, masks in late),
        ),
        out_shape=jax.ShapeDtypeStruct((rows, width), jnp.bfloat16),
        in_specs=[smem()] + [anywhere()] * len(refs),
        out_specs=vmem(),
        scratch_shapes=[pltpu.VMEM(ref.shape, ref.dtype) for ref in refs]
        + [
            pltpu.VMEM((depth // width, width, width), jnp.bfloat16),
            pltpu.VMEM((depth, width), jnp.bfloat16),
            pltpu.VMEM((rows, depth), jnp.bfloat16),
            pltpu.VMEM((rows, width), jnp.float32),
            pltpu.VMEM((rows, width), jnp.bfloat16),
            pltpu.SemaphoreType.DMA((len(refs),)),
        ],
        compiler_params=params(LAYER_LIMIT),
        cost_estimate=pl.CostEstimate(
            flops=4 * rows * width * depth, bytes_accessed=4 * width * depth, transcendentals=0
        ),
        name="layer",
    )(targets, *refs)


def other_pieces(pieces, wide, order):
    late = {}
    known = [order[0]]
    for bit in order[1:]:
        for mask in known:
            held = late[mask] if mask in late else pieces[mask]
            late[mask ^ bit] = swap(held, wide, bit)
        known = known + [bit] + [mask ^ bit for mask in known]
    return late


def crossed(masks):
    return tuple(mask ^ 1 for mask in masks)


def shards(
    features,
    stripe_owner,
    dense_weight,
    sparse_weight,
    send_blocks,
    target_block,
    first_weight,
    second_weight,
    wide,
    narrow,
):
    block_rows = sparse_weight.shape[2]
    stripes = stripe_owner.shape[1]
    bits = [1 << at for at in range(1, wide.bit_length() - 1)]
    orders = (bits, bits[::-1])
    hops = len(bits)
    owners = jnp.transpose(stripe_owner)
    lists = jnp.transpose(send_blocks, (0, 2, 1))
    targets = jnp.transpose(target_block, (0, 2, 1))

    own = pack(first_weight, second_weight)
    packs = [swap(own, wide, bit) for bit in bits]
    received = lax.all_to_all(pick(lists, features, block_rows), "narrow", 0, 0)
    (received,) = tie([received], [], SLACK_BLOCKS)

    dense, degree = prepare(dense_weight)

    carried = halves(owners, features, swap(features, wide, 1))
    along = [tuple(orders[k % 2][hop] for k in range(stripes)) for hop in range(hops)]
    came = [swap(block, wide, bit) for block, bit in zip(carried, along[0])]

    own_crossed = swap(own, wide, 1)
    parts = [(bits.index(bit), which) for which in range(2) for bit in orders[which][:-1]]
    stack, forward = split(packs, tuple(parts), [own_crossed] + list(carried))
    masks = tuple(bits)
    stacks = [(stack, masks), (swap(stack, wide, 1), crossed(masks))]
    ends, end_masks = [], []
    for which in range(2):
        held = {bits[at]: block for (at, of), block in zip(parts, forward) if of == which}
        late = other_pieces(held, wide, orders[which])
        blocks = list(late.values())
        ends.append(blocks[0] if len(blocks) == 1 else jnp.stack(blocks))
        end_masks.append(tuple(late))

    for hop in range(1, hops):
        carried = choose(owners, along[hop - 1], carried, came, False, [degree, stack])
        came = [swap(block, wide, bit) for block, bit in zip(carried, along[hop])]
    carried = choose(owners, along[-1], carried, came, True, ends)
    (other,) = tie([swap(carried, wide, 1)], [], SLACK_STRIPES)

    ends = tie(ends, [stacks[1][0]])
    crossed_ends = tie([swap(end, wide, 1) for end in ends], [], SLACK)
    late = []
    for which in range(2):
        late.append((ends[which], which, end_masks[which]))
        late.append((crossed_ends[which], which, crossed(end_masks[which])))

    arrays = (dense, carried, other, degree, sparse_weight, received, features)
    return layer(targets, arrays, [(own, 0), (own_crossed, 1)], stacks, late, wide)


def solution(mesh):
    placed = (
        P(("wide", "narrow"), None),
        P(),
        P(("wide", "narrow"), None),
        P(("wide", "narrow"), None, None, None),
        P(("wide", "narrow"), None, None),
        P(("wide", "narrow"), None, None),
        P("wide", None),
        P("wide", None),
    )
    local = functools.partial(shards, wide=mesh.shape["wide"], narrow=mesh.shape["narrow"])
    return jax.shard_map(
        local, mesh=mesh, in_specs=placed, out_specs=P(("wide", "narrow"), None), check_vma=False
    )
```

time: 129 us -> 50.1 us (0.39)
  waiting for transfers between devices: 74 us -> 14.3 us
  starting transfers between devices: 0.13 us -> 15.9 us
  between operations: 16 us -> 0.23 us
  matrix products: 14 us -> 0 us
  Pallas kernels: 0 us -> 12.7 us
  blocking collectives: 12.7 us -> 0 us
  other arithmetic: 2.63 us -> 0 us
  local copies, waits for them, and re-layouts: 9.02 us -> 6.71 us
    all_gather x3 -> x0, waiting for transfers between devices: 68 us -> none  [the longest x1 29.7 us: shards(): lax.all_gather(features, 'narrow', axis=0, tiled=True)]
    ppermute x0 -> x14, waiting for transfers between devices: none -> 14.3 us  [swap(): return lax.ppermute(block, 'wide', [(i, i ^ bit) for i in range(count)])]
    dot_general x5 -> x0, matrix products: 14 us -> none  [the longest x2 10 us: add_rows(): return jnp.dot(left, portion, preferred_element_type=jnp.float32)]
    pallas_call x0 -> x12, Pallas kernels: none -> 12.7 us  [the longest x1 7.04 us: layer(): pl.pallas_call(functools.partial(layer_kernel, tuple((mask for _, mask in...]
    all_gather x1 -> x0, blocking collectives: 12.7 us -> none  [shards(): lax.all_gather(lists_sent, 'narrow', axis=0, tiled=True)]
    ppermute x0 -> x14, starting transfers between devices: none -> 11 us  [swap(): return lax.ppermute(block, 'wide', [(i, i ^ bit) for i in range(count)])]
    unnamed x16 -> x38, local copies, waits for them, and re-layouts: 1.2 us -> 6.71 us
    all_to_all x0 -> x1, starting transfers between devices: none -> 4.88 us  [shards(): received = lax.all_to_all(pick(lists, features, block_rows), 'narrow', 0, 0)]
  transfers between devices with their start and end apart: 4 -> 15, of which waited for: 4 -> 6; matrix products, arithmetic and copies ran while one was open for 17% -> 0% of each run, Pallas kernels for 0% -> 11%
where the time goes in v3:
time: 50.1 us; the launch traced here: 49.8 us
  starting transfers between devices  15.9 us (32%)
  waiting for transfers between devices  14.3 us (29%)
  Pallas kernels  12.7 us (25%)
  local copies, waits for them, and re-layouts  6.71 us (13%)
    ppermute x14, waiting for transfers between devices, swap(): return lax.ppermute(block, 'wide', [(i, i ^ bit) for i in range(count)])  14.3 us
    ppermute x14, starting transfers between devices, swap(): return lax.ppermute(block, 'wide', [(i, i ^ bit) for i in range(count)])  11 us
    pallas_call x1, Pallas kernels, layer(): pl.pallas_call(functools.partial(layer_kernel, tuple((mask for _, mask in...  7.04 us
    unnamed x38, local copies, waits for them, and re-layouts  6.71 us
    all_to_all x1, starting transfers between devices, shards(): received = lax.all_to_all(pick(lists, features, block_rows), 'narrow', 0, 0)  4.88 us
    pallas_call x1, Pallas kernels, pick(): pl.pallas_call(functools.partial(pick_kernel, parts, cap, block_rows), ou...  1.6 us
    pallas_call x1, Pallas kernels, split(): pl.pallas_call(functools.partial(split_kernel, parts, len(packs)), out_sh...  1.4 us
    pallas_call x2, Pallas kernels, choose(): pl.pallas_call(functools.partial(choose_kernel, bits, stacked, len(after)...  1.28 us
  transfers between devices with their start and end apart: 15, of which 6 were waited for; matrix products, arithmetic and copies ran while one was open for 0% of the time, Pallas kernels for 11%

profile of v3, /device:TPU:0, one launch (start us, length us, event | category | flops | bytes accessed | tf_op | source)
XLA Modules:
  0.0 49.8 jit_solution(11044933126328389328)
XLA Ops:
  0.0 0.5 collective-permute-start
  0.5 0.9 %copy-done.14 = bf16[64,2048]{1,0:T(8,128)(2,1)S(1)} copy-done((bf16[64,2048]{1,0:T(8,128)(2,1)S(1)}, bf16[64,2048]{1,0:T(8,128)(2,1)}, u32[]{:S(2)}) %copy-start.14) | copy-done | bytes 262168
  1.4 0.9 %copy-done.15 = bf16[256,512]{1,0:T(8,128)(2,1)S(1)} copy-done((bf16[256,512]{1,0:T(8,128)(2,1)S(1)}, bf16[256,512]{1,0:T(8,128)(2,1)}, u32[]{:S(2)}) %copy-start.15) | copy-done | bytes 262168
  2.4 0.1 pack_weights.1.refs_7_
  2.5 0.1 collective-permute-start.5
  2.6 3.0 %collective-permute-start.4 = (bf16[2,256,512]{2,1,0:T(8,128)(2,1)S(1)}, bf16[2,256,512]{2,1,0:T(8,128)(2,1)}, u32[]{:S(2)}, u32[]{:S(2)}) collective-permute-start(bf16[2,256,512]{2,1,0:T(8,128)(2,1)S(1)} %pack_weights.1.refs_7_), channel_id=1, source_target_pairs={{0,16},{4,20},{8,24},{12,28},{16,0},{20,4},{24,8},{28,12},{1,17},{... | collective-permute-start | bytes 1572872 | tf_op jit(solution)/shard_map/ppermute | solution.py:41
  5.6 1.5 %collective-permute-start.3 = (bf16[2,256,512]{2,1,0:T(8,128)(2,1)S(1)}, bf16[2,256,512]{2,1,0:T(8,128)(2,1)}, u32[]{:S(2)}, u32[]{:S(2)}) collective-permute-start(bf16[2,256,512]{2,1,0:T(8,128)(2,1)S(1)} %pack_weights.1.refs_7_), channel_id=1, source_target_pairs={{0,8},{4,12},{8,0},{12,4},{16,24},{20,28},{24,16},{28,20},{1,9},{5... | collective-permute-start | bytes 1572872 | tf_op jit(solution)/shard_map/ppermute | solution.py:41
  7.1 1.0 %copy-done.1 = bf16[512,512]{1,0:T(8,128)(2,1)S(1)} copy-done((bf16[512,512]{1,0:T(8,128)(2,1)S(1)}, bf16[512,512]{1,0:T(8,128)(2,1)}, u32[]{:S(2)}) %copy-start.1) | copy-done | bytes 524312
  8.1 0.7 %copy-done.18 = s32[1,4,2]{1,2,0:T(2,128)S(1)} copy-done((s32[1,4,2]{1,2,0:T(2,128)S(1)}, s32[1,4,2]{1,2,0:T(2,128)}, u32[]{:S(2)}) %copy-start.18) | copy-done | bytes 56
  8.8 1.6 %pick_blocks.1 = bf16[4,256,512]{2,1,0:T(8,128)(2,1)} custom-call(s32[1,2,4]{2,1,0:T(2,128)S(1)} %bitcast.7, bf16[512,512]{1,0:T(8,128)(2,1)S(1)} %copy-done.1), custom_call_target="tpu_custom_call" | custom-call | tf_op jit(solution)/shard_map/pick_blocks/pallas_call | solution.py:72
  10.4 4.9 %all-to-all-start = ((bf16[4,256,512]{2,1,0:T(8,128)(2,1)}), bf16[4,256,512]{2,1,0:T(8,128)(2,1)S(1)}, u32[]{:S(2)}, u32[]{:S(2)}) async-start(bf16[4,256,512]{2,1,0:T(8,128)(2,1)} %pick_blocks.1), calls=%async_computation | async-start | bytes 2097152 | tf_op jit(solution)/shard_map/all_to_all | solution.py:437
  15.3 0.6 %stripe_halves.1 = (bf16[256,512]{1,0:T(8,128)(2,1)S(1)}, bf16[256,512]{1,0:T(8,128)(2,1)S(1)}) custom-call(s32[2,4]{1,0:T(2,128)S(1)} %bitcast.3, bf16[512,512]{1,0:T(8,128)(2,1)S(1)} %copy-done.2, bf16[512,512]{1,0:T(8,128)(2,1)S(1)} %collective-permute-done.other_ref), custom_call_target="tpu_custom_call" | custom-call | tf_op jit(solution)/shard_map/stripe_halves/pallas_call | solution.py:113
  16.0 0.6 %collective-permute-start.1 = (bf16[256,512]{1,0:T(8,128)(2,1)S(1)}, bf16[256,512]{1,0:T(8,128)(2,1)S(1)}, u32[]{:S(2)}, u32[]{:S(2)}) collective-permute-start(bf16[256,512]{1,0:T(8,128)(2,1)S(1)} %get-tuple-element.19.refs_3_.refs_0_), channel_id=1, source_target_pairs={{0,8},{4,12},{8,0},{12,4},{16,24},{20,28},{24,16},{28,20},{1,9},{5... | collective-permute-start | bytes 786440 | tf_op jit(solution)/shard_map/ppermute | solution.py:41
  16.6 0.5 %collective-permute-start.2 = (bf16[256,512]{1,0:T(8,128)(2,1)S(1)}, bf16[256,512]{1,0:T(8,128)(2,1)S(1)}, u32[]{:S(2)}, u32[]{:S(2)}) collective-permute-start(bf16[256,512]{1,0:T(8,128)(2,1)S(1)} %get-tuple-element.20.refs_4_.refs_1_), channel_id=1, source_target_pairs={{0,16},{4,20},{8,24},{12,28},{16,0},{20,4},{24,8},{28,12},{1,17},{... | collective-permute-start | bytes 786440 | tf_op jit(solution)/shard_map/ppermute | solution.py:41
  17.1 0.8 %collective-permute-done.4.refs_1_ = bf16[2,256,512]{2,1,0:T(8,128)(2,1)} collective-permute-done((bf16[2,256,512]{2,1,0:T(8,128)(2,1)S(1)}, bf16[2,256,512]{2,1,0:T(8,128)(2,1)}, u32[]{:S(2)}, u32[]{:S(2)}) %collective-permute-start.4) | collective-permute-done | bytes 524320 | tf_op jit(solution)/shard_map/ppermute | solution.py:41
  17.9 2.6 %collective-permute-done.3.refs_0_ = bf16[2,256,512]{2,1,0:T(8,128)(2,1)} collective-permute-done((bf16[2,256,512]{2,1,0:T(8,128)(2,1)S(1)}, bf16[2,256,512]{2,1,0:T(8,128)(2,1)}, u32[]{:S(2)}, u32[]{:S(2)}) %collective-permute-start.3) | collective-permute-done | bytes 524320 | tf_op jit(solution)/shard_map/ppermute | solution.py:41
  20.5 1.4 %split_packs.1 = (bf16[2,2,256,512]{3,2,1,0:T(8,128)(2,1)S(1)}, bf16[256,512]{1,0:T(8,128)(2,1)S(1)}, bf16[256,512]{1,0:T(8,128)(2,1)S(1)}) custom-call(bf16[2,256,512]{2,1,0:T(8,128)(2,1)} %collective-permute-done.3.refs_0_, bf16[2,256,512]{2,1,0:T(8,128)(2,1)} %collective-permute-done.4.refs_1_, ...), custom_call_target="tpu_custom_call" | custom-call | tf_op jit(solution)/shard_map/split_packs/pallas_call | solution.py:212
  22.0 0.6 %dense_rows.1 = (bf16[512,1024]{1,0:T(8,128)(2,1)S(1)}, f32[512,128]{1,0:T(8,128)S(1)}) custom-call(s32[512,1024]{1,0:T(8,128)S(1)} %copy-done.6), custom_call_target="tpu_custom_call" | custom-call | flops 1048576 | bytes 3145728 | tf_op jit(solution)/shard_map/dense_rows/pallas_call | solution.py:252
  22.7 1.0 %copy-done.9 = bf16[512,1024]{1,0:T(8,128)(2,1)} copy-done((bf16[512,1024]{1,0:T(8,128)(2,1)}, bf16[512,1024]{1,0:T(8,128)(2,1)S(1)}, u32[]{:S(2)}) %copy-start.9) | copy-done | bytes 1048600
  23.7 2.0 %collective-permute-start.9 = (bf16[256,512]{1,0:T(8,128)(2,1)S(1)}, bf16[256,512]{1,0:T(8,128)(2,1)}, u32[]{:S(2)}, u32[]{:S(2)}) collective-permute-start(bf16[256,512]{1,0:T(8,128)(2,1)S(1)} %get-tuple-element.26), channel_id=1, source_target_pairs={{0,8},{4,12},{8,0},{12,4},{16,24},{20,28},{24,16},{28,20},{1,9},{5... | collective-permute-start | bytes 786440 | tf_op jit(solution)/shard_map/ppermute | solution.py:41
  25.7 0.6 %stripe_choice.2 = (bf16[256,512]{1,0:T(8,128)(2,1)S(1)}, bf16[256,512]{1,0:T(8,128)(2,1)S(1)}) custom-call(s32[2,4]{1,0:T(2,128)S(1)} %bitcast.4, bf16[256,512]{1,0:T(8,128)(2,1)S(1)} %get-tuple-element.19.refs_3_.refs_0_, bf16[256,512]{1,0:T(8,128)(2,1)S(1)} %get-tuple-element.20.refs_4_.refs_1_, bf16[256,512]{1,0:T(8,128)(2,1)S(1)} %collective-permute-done.1.refs_2_, ...), custom_call_target="tpu_custom_call" | custom-call | tf_op jit(solution)/shard_map/stripe_choice/pallas_call | solution.py:156
  26.3 1.6 %collective-permute-start.6 = (bf16[256,512]{1,0:T(8,128)(2,1)S(1)}, bf16[256,512]{1,0:T(8,128)(2,1)S(1)}, u32[]{:S(2)}, u32[]{:S(2)}) collective-permute-start(bf16[256,512]{1,0:T(8,128)(2,1)S(1)} %get-tuple-element.23.refs_0_), channel_id=1, source_target_pairs={{0,16},{4,20},{8,24},{12,28},{16,0},{20,4},{24,8},{28,12},{1,17},{... | collective-permute-start | bytes 786440 | tf_op jit(solution)/shard_map/ppermute | solution.py:41
  27.9 0.5 %collective-permute-start.7 = (bf16[256,512]{1,0:T(8,128)(2,1)S(1)}, bf16[256,512]{1,0:T(8,128)(2,1)S(1)}, u32[]{:S(2)}, u32[]{:S(2)}) collective-permute-start(bf16[256,512]{1,0:T(8,128)(2,1)S(1)} %get-tuple-element.24.refs_1_), channel_id=1, source_target_pairs={{0,8},{4,12},{8,0},{12,4},{16,24},{20,28},{24,16},{28,20},{1,9},{5... | collective-permute-start | bytes 786440 | tf_op jit(solution)/shard_map/ppermute | solution.py:41
  28.4 4.3 %collective-permute-done.8.refs_4_.refs_0_ = bf16[256,512]{1,0:T(8,128)(2,1)S(1)} collective-permute-done((bf16[256,512]{1,0:T(8,128)(2,1)S(1)}, bf16[256,512]{1,0:T(8,128)(2,1)S(1)}, u32[]{:S(2)}, u32[]{:S(2)}) %collective-permute-start.8) | collective-permute-done | bytes 262176 | tf_op jit(solution)/shard_map/ppermute | solution.py:41
  32.9 5.1 %collective-permute-done.6.refs_2_ = bf16[256,512]{1,0:T(8,128)(2,1)S(1)} collective-permute-done((bf16[256,512]{1,0:T(8,128)(2,1)S(1)}, bf16[256,512]{1,0:T(8,128)(2,1)S(1)}, u32[]{:S(2)}, u32[]{:S(2)}) %collective-permute-start.6) | collective-permute-done | bytes 262176 | tf_op jit(solution)/shard_map/ppermute | solution.py:41
  38.0 0.6 %stripe_choice.3.refs_1_ = bf16[2,256,512]{2,1,0:T(8,128)(2,1)S(1)} custom-call(s32[2,4]{1,0:T(2,128)S(1)} %bitcast.5, bf16[256,512]{1,0:T(8,128)(2,1)S(1)} %get-tuple-element.23.refs_0_, bf16[256,512]{1,0:T(8,128)(2,1)S(1)} %get-tuple-element.24.refs_1_, bf16[256,512]{1,0:T(8,128)(2,1)S(1)} %collective-permute-done.6.refs_2_, ...), custom_call_target="tpu_custom_call" | custom-call | tf_op jit(solution)/shard_map/stripe_choice/pallas_call | solution.py:156
  38.7 0.5 collective-permute-start.12
  39.3 1.3 %collective-permute-done.10.refs_0_ = bf16[2,256,512]{2,1,0:T(8,128)(2,1)S(1)} collective-permute-done((bf16[2,256,512]{2,1,0:T(8,128)(2,1)S(1)}, bf16[2,256,512]{2,1,0:T(8,128)(2,1)S(1)}, u32[]{:S(2)}, u32[]{:S(2)}) %collective-permute-start.10) | collective-permute-done | bytes 524320 | tf_op jit(solution)/shard_map/ppermute | solution.py:41
  40.6 0.8 %copy-done.12 = bf16[2,256,512]{2,1,0:T(8,128)(2,1)} copy-done((bf16[2,256,512]{2,1,0:T(8,128)(2,1)}, bf16[2,256,512]{2,1,0:T(8,128)(2,1)S(1)}, u32[]{:S(2)}) %copy-start.12) | copy-done | bytes 524312
  41.4 1.0 %copy-done = bf16[4,256,512]{2,1,0:T(8,128)(2,1)} copy-done((bf16[4,256,512]{2,1,0:T(8,128)(2,1)}, bf16[4,256,512]{2,1,0:T(8,128)(2,1)S(1)}, u32[]{:S(2)}) %copy-start) | copy-done | bytes 1048600
  42.5 0.3 copy-done.13
  42.7 7.0 %layer.1 = bf16[512,512]{1,0:T(8,128)(2,1)} custom-call(s32[1,2,4]{2,1,0:T(2,128)S(1)} %bitcast.6, bf16[512,1024]{1,0:T(8,128)(2,1)} %copy-done.9, bf16[2,256,512]{2,1,0:T(8,128)(2,1)} %copy-done.8, bf16[2,256,512]{2,1,0:T(8,128)(2,1)} %copy-done.12, f32[512,128]{1,0:T(8,128)S(1)} %copy-done.11, s32[1,4,128,128]{3,2,1,0:T(8,128)S(1)} %copy-done.13, ...), custom_call_target="tpu_custom_call" | custom-call | flops 2147483648 | bytes 4194304 | tf_op jit(solution)/shard_map/layer/pallas_call | solution.py:372
  (48 shorter events, 0.5 us)
Async XLA Ops:
  0.0 15.3 %collective-permute-start = (bf16[512,512]{1,0:T(8,128)(2,1)}, bf16[512,512]{1,0:T(8,128)(2,1)S(1)}, u32[]{:S(2)}, u32[]{:S(2)}) collective-permute-start(bf16[512,512]{1,0:T(8,128)(2,1)} %refs_6_.1), channel_id=1, source_target_pairs={{0,4},{4,0},{8,12},{12,8},{16,20},{20,16},{24,28},{28,24},{1,5},{5... | collective-permute-start | bytes 1572872 | tf_op jit(solution)/shard_map/ppermute | solution.py:41
  0.5 0.9 %copy-start.14 = (bf16[64,2048]{1,0:T(8,128)(2,1)S(1)}, bf16[64,2048]{1,0:T(8,128)(2,1)}, u32[]{:S(2)}) copy-start(bf16[64,2048]{1,0:T(8,128)(2,1)} %first_ref.1) | copy-start | bytes 786436
  1.4 0.9 %copy-start.15 = (bf16[256,512]{1,0:T(8,128)(2,1)S(1)}, bf16[256,512]{1,0:T(8,128)(2,1)}, u32[]{:S(2)}) copy-start(bf16[256,512]{1,0:T(8,128)(2,1)} %second_ref.1) | copy-start | bytes 786436
  2.4 12.9 %copy-start.2 = (bf16[512,512]{1,0:T(8,128)(2,1)S(1)}, bf16[512,512]{1,0:T(8,128)(2,1)}, u32[]{:S(2)}) copy-start(bf16[512,512]{1,0:T(8,128)(2,1)} %refs_6_.1) | copy-start | bytes 1572868
  2.5 13.5 %copy-start.5 = (bf16[2,256,512]{2,1,0:T(8,128)(2,1)}, bf16[2,256,512]{2,1,0:T(8,128)(2,1)S(1)}, u32[]{:S(2)}) copy-start(bf16[2,256,512]{2,1,0:T(8,128)(2,1)S(1)} %pack_weights.1.refs_7_) | copy-start | bytes 1572868
  2.5 12.8 %copy-start.16 = (s32[4,2]{0,1:T(2,128)S(1)}, s32[4,2]{0,1:T(2,128)}, u32[]{:S(2)}) copy-start(s32[4,2]{0,1:T(2,128)} %param.9) | copy-start | bytes 100
  2.5 14.6 %collective-permute-start.5 = (bf16[2,256,512]{2,1,0:T(8,128)(2,1)S(1)}, bf16[2,256,512]{2,1,0:T(8,128)(2,1)S(1)}, u32[]{:S(2)}, u32[]{:S(2)}) collective-permute-start(bf16[2,256,512]{2,1,0:T(8,128)(2,1)S(1)} %pack_weights.1.refs_7_), channel_id=1, source_target_pairs={{0,4},{4,0},{8,12},{12,8},{16,20},{20,16},{24,28},{28,24},{1,5},{5... | collective-permute-start | bytes 1572872 | tf_op jit(solution)/shard_map/ppermute | solution.py:41
  2.6 15.2 %collective-permute-start.4 = (bf16[2,256,512]{2,1,0:T(8,128)(2,1)S(1)}, bf16[2,256,512]{2,1,0:T(8,128)(2,1)}, u32[]{:S(2)}, u32[]{:S(2)}) collective-permute-start(bf16[2,256,512]{2,1,0:T(8,128)(2,1)S(1)} %pack_weights.1.refs_7_), channel_id=1, source_target_pairs={{0,16},{4,20},{8,24},{12,28},{16,0},{20,4},{24,8},{28,12},{1,17},{... | collective-permute-start | bytes 1572872 | tf_op jit(solution)/shard_map/ppermute | solution.py:41
  5.6 14.9 %collective-permute-start.3 = (bf16[2,256,512]{2,1,0:T(8,128)(2,1)S(1)}, bf16[2,256,512]{2,1,0:T(8,128)(2,1)}, u32[]{:S(2)}, u32[]{:S(2)}) collective-permute-start(bf16[2,256,512]{2,1,0:T(8,128)(2,1)S(1)} %pack_weights.1.refs_7_), channel_id=1, source_target_pairs={{0,8},{4,12},{8,0},{12,4},{16,24},{20,28},{24,16},{28,20},{1,9},{5... | collective-permute-start | bytes 1572872 | tf_op jit(solution)/shard_map/ppermute | solution.py:41
  7.1 1.0 %copy-start.1 = (bf16[512,512]{1,0:T(8,128)(2,1)S(1)}, bf16[512,512]{1,0:T(8,128)(2,1)}, u32[]{:S(2)}) copy-start(bf16[512,512]{1,0:T(8,128)(2,1)} %refs_6_.1) | copy-start | bytes 1572868
  10.4 31.0 %all-to-all-start = ((bf16[4,256,512]{2,1,0:T(8,128)(2,1)}), bf16[4,256,512]{2,1,0:T(8,128)(2,1)S(1)}, u32[]{:S(2)}, u32[]{:S(2)}) async-start(bf16[4,256,512]{2,1,0:T(8,128)(2,1)} %pick_blocks.1), calls=%async_computation | async-start | bytes 2097152 | tf_op jit(solution)/shard_map/all_to_all | solution.py:437
  15.3 6.7 %copy-start.6 = (s32[512,1024]{1,0:T(8,128)S(1)}, s32[512,1024]{1,0:T(8,128)}, u32[]{:S(2)}) copy-start(s32[512,1024]{1,0:T(8,128)} %dense_ref.1) | copy-start | bytes 6291460
  16.0 9.7 %collective-permute-start.1 = (bf16[256,512]{1,0:T(8,128)(2,1)S(1)}, bf16[256,512]{1,0:T(8,128)(2,1)S(1)}, u32[]{:S(2)}, u32[]{:S(2)}) collective-permute-start(bf16[256,512]{1,0:T(8,128)(2,1)S(1)} %get-tuple-element.19.refs_3_.refs_0_), channel_id=1, source_target_pairs={{0,8},{4,12},{8,0},{12,4},{16,24},{20,28},{24,16},{28,20},{1,9},{5... | collective-permute-start | bytes 786440 | tf_op jit(solution)/shard_map/ppermute | solution.py:41
  16.6 9.1 %collective-permute-start.2 = (bf16[256,512]{1,0:T(8,128)(2,1)S(1)}, bf16[256,512]{1,0:T(8,128)(2,1)S(1)}, u32[]{:S(2)}, u32[]{:S(2)}) collective-permute-start(bf16[256,512]{1,0:T(8,128)(2,1)S(1)} %get-tuple-element.20.refs_4_.refs_1_), channel_id=1, source_target_pairs={{0,16},{4,20},{8,24},{12,28},{16,0},{20,4},{24,8},{28,12},{1,17},{... | collective-permute-start | bytes 786440 | tf_op jit(solution)/shard_map/ppermute | solution.py:41
  17.1 4.8 %copy-start.7 = (bf16[2,256,512]{2,1,0:T(8,128)(2,1)}, bf16[2,256,512]{2,1,0:T(8,128)(2,1)S(1)}, u32[]{:S(2)}) copy-start(bf16[2,256,512]{2,1,0:T(8,128)(2,1)S(1)} %collective-permute-done.5.refs_2_.refs_8_) | copy-start | bytes 1572868
  21.9 4.4 %copy-start.3 = (bf16[2,2,256,512]{3,2,1,0:T(8,128)(2,1)}, bf16[2,2,256,512]{3,2,1,0:T(8,128)(2,1)S(1)}, u32[]{:S(2)}) copy-start(bf16[2,2,256,512]{3,2,1,0:T(8,128)(2,1)S(1)} %get-tuple-element.22.refs_5_.refs_9_) | copy-start | bytes 3145732
  21.9 16.8 %collective-permute-start.11 = (bf16[2,2,256,512]{3,2,1,0:T(8,128)(2,1)S(1)}, bf16[2,2,256,512]{3,2,1,0:T(8,128)(2,1)S(1)}, u32[]{:S(2)}, u32[]{:S(2)}) collective-permute-start(bf16[2,2,256,512]{3,2,1,0:T(8,128)(2,1)S(1)} %get-tuple-element.22.refs_5_.refs_9_), channel_id=1, source_target_pairs={{0,4},{4,0},{8,12},{12,8},{16,20},{20,16},{24,28},{28,24},{1,5},{5... | collective-permute-start | bytes 3145736 | tf_op jit(solution)/shard_map/ppermute | solution.py:41
  22.7 1.0 %copy-start.9 = (bf16[512,1024]{1,0:T(8,128)(2,1)}, bf16[512,1024]{1,0:T(8,128)(2,1)S(1)}, u32[]{:S(2)}) copy-start(bf16[512,1024]{1,0:T(8,128)(2,1)S(1)} %get-tuple-element.18.refs_0_) | copy-start | bytes 3145732
  23.6 15.0 %copy-start.10 = (f32[512,128]{1,0:T(8,128)}, f32[512,128]{1,0:T(8,128)S(1)}, u32[]{:S(2)}) copy-start(f32[512,128]{1,0:T(8,128)S(1)} %get-tuple-element.21.refs_4_.refs_3_) | copy-start | bytes 786436
  23.6 9.1 %collective-permute-start.8 = (bf16[256,512]{1,0:T(8,128)(2,1)S(1)}, bf16[256,512]{1,0:T(8,128)(2,1)S(1)}, u32[]{:S(2)}, u32[]{:S(2)}) collective-permute-start(bf16[256,512]{1,0:T(8,128)(2,1)S(1)} %get-tuple-element.25), channel_id=1, source_target_pairs={{0,16},{4,20},{8,24},{12,28},{16,0},{20,4},{24,8},{28,12},{1,17},{... | collective-permute-start | bytes 786440 | tf_op jit(solution)/shard_map/ppermute | solution.py:41
  23.7 9.2 %collective-permute-start.9 = (bf16[256,512]{1,0:T(8,128)(2,1)S(1)}, bf16[256,512]{1,0:T(8,128)(2,1)}, u32[]{:S(2)}, u32[]{:S(2)}) collective-permute-start(bf16[256,512]{1,0:T(8,128)(2,1)S(1)} %get-tuple-element.26), channel_id=1, source_target_pairs={{0,8},{4,12},{8,0},{12,4},{16,24},{20,28},{24,16},{28,20},{1,9},{5... | collective-permute-start | bytes 786440 | tf_op jit(solution)/shard_map/ppermute | solution.py:41
  26.3 11.6 %collective-permute-start.6 = (bf16[256,512]{1,0:T(8,128)(2,1)S(1)}, bf16[256,512]{1,0:T(8,128)(2,1)S(1)}, u32[]{:S(2)}, u32[]{:S(2)}) collective-permute-start(bf16[256,512]{1,0:T(8,128)(2,1)S(1)} %get-tuple-element.23.refs_0_), channel_id=1, source_target_pairs={{0,16},{4,20},{8,24},{12,28},{16,0},{20,4},{24,8},{28,12},{1,17},{... | collective-permute-start | bytes 786440 | tf_op jit(solution)/shard_map/ppermute | solution.py:41
  27.9 10.1 %collective-permute-start.7 = (bf16[256,512]{1,0:T(8,128)(2,1)S(1)}, bf16[256,512]{1,0:T(8,128)(2,1)S(1)}, u32[]{:S(2)}, u32[]{:S(2)}) collective-permute-start(bf16[256,512]{1,0:T(8,128)(2,1)S(1)} %get-tuple-element.24.refs_1_), channel_id=1, source_target_pairs={{0,8},{4,12},{8,0},{12,4},{16,24},{20,28},{24,16},{28,20},{1,9},{5... | collective-permute-start | bytes 786440 | tf_op jit(solution)/shard_map/ppermute | solution.py:41
  38.6 2.0 %copy-start.8 = (bf16[2,256,512]{2,1,0:T(8,128)(2,1)}, bf16[2,256,512]{2,1,0:T(8,128)(2,1)S(1)}, u32[]{:S(2)}) copy-start(bf16[2,256,512]{2,1,0:T(8,128)(2,1)S(1)} %stripe_choice.3.refs_1_) | copy-start | bytes 1572868
  38.6 2.0 %collective-permute-start.10 = (bf16[2,256,512]{2,1,0:T(8,128)(2,1)S(1)}, bf16[2,256,512]{2,1,0:T(8,128)(2,1)S(1)}, u32[]{:S(2)}, u32[]{:S(2)}) collective-permute-start(bf16[2,256,512]{2,1,0:T(8,128)(2,1)S(1)} %stripe_choice.3.refs_1_), channel_id=1, source_target_pairs={{0,4},{4,0},{8,12},{12,8},{16,20},{20,16},{24,28},{28,24},{1,5},{5... | collective-permute-start | bytes 1572872 | tf_op jit(solution)/shard_map/ppermute | solution.py:41
  38.7 1.9 %copy-start.4 = (bf16[2,2,256,512]{3,2,1,0:T(8,128)(2,1)}, bf16[2,2,256,512]{3,2,1,0:T(8,128)(2,1)S(1)}, u32[]{:S(2)}) copy-start(bf16[2,2,256,512]{3,2,1,0:T(8,128)(2,1)S(1)} %collective-permute-done.11.refs_2_.refs_10_) | copy-start | bytes 3145732
  38.7 3.7 %collective-permute-start.12 = (bf16[256,512]{1,0:T(8,128)(2,1)S(1)}, bf16[256,512]{1,0:T(8,128)(2,1)S(1)}, u32[]{:S(2)}, u32[]{:S(2)}) collective-permute-start(bf16[256,512]{1,0:T(8,128)(2,1)S(1)} %get-tuple-element.27.refs_11_), channel_id=1, source_target_pairs={{0,4},{4,0},{8,12},{12,8},{16,20},{20,16},{24,28},{28,24},{1,5},{5... | collective-permute-start | bytes 786440 | tf_op jit(solution)/shard_map/ppermute | solution.py:41
  39.2 3.2 %collective-permute-start.13 = (bf16[256,512]{1,0:T(8,128)(2,1)}, bf16[256,512]{1,0:T(8,128)(2,1)S(1)}, u32[]{:S(2)}, u32[]{:S(2)}) collective-permute-start(bf16[256,512]{1,0:T(8,128)(2,1)} %get-tuple-element.28.refs_13_), channel_id=1, source_target_pairs={{0,4},{4,0},{8,12},{12,8},{16,20},{20,16},{24,28},{28,24},{1,5},{5... | collective-permute-start | bytes 786440 | tf_op jit(solution)/shard_map/ppermute | solution.py:41
  41.4 1.0 %copy-start.11 = (f32[512,128]{1,0:T(8,128)S(1)}, f32[512,128]{1,0:T(8,128)}, u32[]{:S(2)}) copy-start(f32[512,128]{1,0:T(8,128)} %copy-done.10) | copy-start | bytes 786436
  41.4 1.3 %copy-start.13 = (s32[1,4,128,128]{3,2,1,0:T(8,128)S(1)}, s32[1,4,128,128]{3,2,1,0:T(8,128)}, u32[]{:S(2)}) copy-start(s32[1,4,128,128]{3,2,1,0:T(8,128)} %refs_4_.1) | copy-start | bytes 786436
  41.4 1.3 %copy-start.17 = (s32[1,4,2]{1,2,0:T(2,128)S(1)}, s32[1,4,2]{1,2,0:T(2,128)}, u32[]{:S(2)}) copy-start(s32[1,4,2]{1,2,0:T(2,128)} %param.13) | copy-start | bytes 100
  41.4 1.0 %copy-start = (bf16[4,256,512]{2,1,0:T(8,128)(2,1)}, bf16[4,256,512]{2,1,0:T(8,128)(2,1)S(1)}, u32[]{:S(2)}) copy-start(bf16[4,256,512]{2,1,0:T(8,128)(2,1)S(1)} %tie.5.refs_5_) | copy-start | bytes 3145732
  (2 other events, 1.5 us)

commit v4 on v3

--- a/solution.py
+++ b/solution.py
@@ -10,11 +10,14 @@
 LANES = 128
 ABSENT = 64.0
 VMEM_LIMIT = 48 * 1024 * 1024
-SLACK = 0
 LARGE_LIMIT = 48 * 1024 * 1024
-SLACK_BLOCKS = 0
-LAYER_LIMIT = 52 * 1024 * 1024
-SLACK_STRIPES = 4 * 10**9
+SLACK_WEIGHTS = 0
+ROWS_FLOPS = 10**9
+ROWS_LIMIT = 48 * 2**20
+LAYER_FLOPS = 10**11
+LAYER_BYTES = 4 * 10**6
+LAYER_LIMIT = 48 * 2**20
+SLACK_STRIPES = 2 * 10**9
 
 
 def params(limit=VMEM_LIMIT):
@@ -160,6 +163,7 @@
         out_specs=out_specs,
         scratch_shapes=[pltpu.SemaphoreType.DMA((count,))],
         compiler_params=params(),
+        cost_estimate=pl.CostEstimate(flops=SLACK_STRIPES, bytes_accessed=0, transcendentals=0),
         name="stripe_choice",
     )(owners, *carried, *came, *after)
 
@@ -217,6 +221,7 @@
         out_specs=[anywhere()] * (1 + len(parts)),
         scratch_shapes=[pltpu.SemaphoreType.DMA((len(parts) + len(packs),))],
         compiler_params=params(),
+        cost_estimate=pl.CostEstimate(flops=SLACK_WEIGHTS, bytes_accessed=0, transcendentals=0),
         name="split_packs",
     )(*packs, *after)
     return stack, outs
@@ -239,11 +244,8 @@
     )(*blocks, *after)
 
 
-def prepare_kernel(dense_ref, out_ref, degree_ref):
-    values = dense_ref[...]
-    out_ref[...] = values.astype(jnp.float32).astype(jnp.bfloat16)
-    sums = 1.0 + jnp.sum(values, axis=1, keepdims=True).astype(jnp.float32)
-    degree_ref[...] = jnp.broadcast_to(sums, degree_ref.shape)
+def prepare_kernel(dense_ref, out_ref):
+    out_ref[...] = dense_ref[...].astype(jnp.float32).astype(jnp.bfloat16)
 
 
 def prepare(dense_weight):
@@ -252,15 +254,9 @@
     return pl.pallas_call(
         prepare_kernel,
         grid=(rows // step,),
-        out_shape=[
-            jax.ShapeDtypeStruct((rows, columns), jnp.bfloat16),
-            jax.ShapeDtypeStruct((rows, LANES), jnp.float32),
-        ],
+        out_shape=jax.ShapeDtypeStruct((rows, columns), jnp.bfloat16),
         in_specs=[pl.BlockSpec((step, columns), lambda i: (i, 0))],
-        out_specs=[
-            pl.BlockSpec((step, columns), lambda i: (i, 0)),
-            pl.BlockSpec((step, LANES), lambda i: (i, 0)),
-        ],
+        out_specs=pl.BlockSpec((step, columns), lambda i: (i, 0)),
         compiler_params=params(),
         cost_estimate=pl.CostEstimate(
             flops=2 * rows * columns, bytes_accessed=6 * rows * columns, transcendentals=0
@@ -286,9 +282,9 @@
 def add_blocks(targets_ref, tiles_ref, received_ref, total_ref, count_ref):
     _, parts, block_rows, _ = tiles_ref.shape
     for source in range(parts):
-        tile = tiles_ref[0, source]
-        weight = jnp.sum(tile, axis=1, keepdims=True).astype(jnp.float32)
-        tile = tile.astype(jnp.float32).astype(jnp.bfloat16)
+        tile = tiles_ref[0, source].astype(jnp.float32).astype(jnp.bfloat16)
+        ones = jnp.ones((tile.shape[1], LANES), jnp.bfloat16)
+        weight = jnp.dot(tile, ones, preferred_element_type=jnp.float32)
         for slot in range(received_ref.shape[1] // block_rows):
             block = received_ref[source, pl.ds(slot * block_rows, block_rows), :]
             present = block[0:1, :].astype(jnp.float32) < ABSENT / 2
@@ -324,34 +320,55 @@
         second_ref[pl.ds(pl.multiple_of((me ^ mask) * rows, rows), rows), :] = ref[...]
 
 
-def layer_kernel(own, came, late, targets_ref, *refs):
-    count = 7 + len(own) + len(came) + len(late)
+def rows_kernel(
+    targets_ref, dense_ref, mine_ref, other_ref, tiles_ref, received_ref, features_ref, out_ref,
+    total_ref, count_ref
+):
+    ones = jnp.ones((dense_ref.shape[1], LANES), jnp.bfloat16)
+    count_ref[...] = 1.0 + jnp.dot(dense_ref[...], ones, preferred_element_type=jnp.float32)
+    add_stripes(dense_ref, mine_ref, other_ref, total_ref)
+    add_blocks(targets_ref, tiles_ref, received_ref, total_ref, count_ref)
+    combine(features_ref, total_ref, count_ref, out_ref)
+
+
+def combined_rows(targets, dense, mine, other, tiles, received, features):
+    return pl.pallas_call(
+        rows_kernel,
+        out_shape=jax.ShapeDtypeStruct(features.shape, features.dtype),
+        in_specs=[smem()] + [vmem()] * 6,
+        out_specs=vmem(),
+        scratch_shapes=[
+            pltpu.VMEM(features.shape, jnp.float32),
+            pltpu.VMEM((features.shape[0], LANES), jnp.float32),
+        ],
+        compiler_params=params(ROWS_LIMIT),
+        cost_estimate=pl.CostEstimate(
+            flops=ROWS_FLOPS, bytes_accessed=4 * 10**6, transcendentals=0
+        ),
+        name="combined_rows",
+    )(targets, dense, mine, other, tiles, received, features)
+
+
+def layer_kernel(own, came, late, combined_ref, *refs):
+    count = len(own) + len(came) + len(late)
     held = refs[count + 1 : 2 * count + 1]
     out_ref = refs[count]
-    first_ref, second_ref, hidden_ref, total_ref, combined_ref, sems = refs[2 * count + 1 :]
+    first_ref, second_ref, hidden_ref, sems = refs[2 * count + 1 :]
     copies = [
         pltpu.make_async_copy(ref, target, sems.at[at])
         for at, (ref, target) in enumerate(zip(refs[:count], held))
     ]
     for copy in copies:
         copy.start()
-    dense_ref, mine_ref, other_ref, count_ref, tiles_ref, received_ref, features_ref = held[:7]
-    packs = list(zip(held[7:], own))
-    for ref, masks in zip(held[7 + len(own) :], came):
+    packs = list(zip(held, own))
+    for ref, masks in zip(held[len(own) :], came):
         packs += [(ref.at[at], mask) for at, mask in enumerate(masks)]
     pieces = [[(ref.at[which], mask) for ref, mask in packs] for which in range(2)]
-    for ref, (which, masks) in zip(held[7 + len(own) + len(came) :], late):
+    for ref, (which, masks) in zip(held[len(own) + len(came) :], late):
         pieces[which] += [
             (ref if len(masks) == 1 else ref.at[at], mask) for at, mask in enumerate(masks)
         ]
-    for copy in copies[:3]:
-        copy.wait()
-    add_stripes(dense_ref, mine_ref, other_ref, total_ref)
-    for copy in copies[3:7]:
-        copy.wait()
-    add_blocks(targets_ref, tiles_ref, received_ref, total_ref, count_ref)
-    combine(features_ref, total_ref, count_ref, combined_ref)
-    for copy in copies[7:]:
+    for copy in copies:
         copy.wait()
     place_first(pieces[0], first_ref)
     width = first_ref.shape[2]
@@ -364,10 +381,9 @@
     ).astype(jnp.bfloat16)
 
 
-def layer(targets, arrays, own, came, late, count):
-    features = arrays[-1]
-    rows, width = features.shape
-    refs = list(arrays) + [block for block, _ in own + came] + [block for block, _, _ in late]
+def layer(combined, own, came, late, count):
+    rows, width = combined.shape
+    refs = [block for block, _ in own + came] + [block for block, _, _ in late]
     depth = own[0][0].shape[1] * count
     return pl.pallas_call(
         functools.partial(
@@ -377,23 +393,21 @@
             tuple((which, masks) for _, which, masks in late),
         ),
         out_shape=jax.ShapeDtypeStruct((rows, width), jnp.bfloat16),
-        in_specs=[smem()] + [anywhere()] * len(refs),
+        in_specs=[vmem()] + [anywhere()] * len(refs),
         out_specs=vmem(),
         scratch_shapes=[pltpu.VMEM(ref.shape, ref.dtype) for ref in refs]
         + [
             pltpu.VMEM((depth // width, width, width), jnp.bfloat16),
             pltpu.VMEM((depth, width), jnp.bfloat16),
             pltpu.VMEM((rows, depth), jnp.bfloat16),
-            pltpu.VMEM((rows, width), jnp.float32),
-            pltpu.VMEM((rows, width), jnp.bfloat16),
             pltpu.SemaphoreType.DMA((len(refs),)),
         ],
         compiler_params=params(LAYER_LIMIT),
         cost_estimate=pl.CostEstimate(
-            flops=4 * rows * width * depth, bytes_accessed=4 * width * depth, transcendentals=0
+            flops=LAYER_FLOPS, bytes_accessed=LAYER_BYTES, transcendentals=0
         ),
         name="layer",
-    )(targets, *refs)
+    )(combined, *refs)
 
 
 def other_pieces(pieces, wide, order):
@@ -435,9 +449,8 @@
     own = pack(first_weight, second_weight)
     packs = [swap(own, wide, bit) for bit in bits]
     received = lax.all_to_all(pick(lists, features, block_rows), "narrow", 0, 0)
-    (received,) = tie([received], [], SLACK_BLOCKS)
-
-    dense, degree = prepare(dense_weight)
+
+    dense = prepare(dense_weight)
 
     carried = halves(owners, features, swap(features, wide, 1))
     along = [tuple(orders[k % 2][hop] for k in range(stripes)) for hop in range(hops)]
@@ -446,8 +459,6 @@
     own_crossed = swap(own, wide, 1)
     parts = [(bits.index(bit), which) for which in range(2) for bit in orders[which][:-1]]
     stack, forward = split(packs, tuple(parts), [own_crossed] + list(carried))
-    masks = tuple(bits)
-    stacks = [(stack, masks), (swap(stack, wide, 1), crossed(masks))]
     ends, end_masks = [], []
     for which in range(2):
         held = {bits[at]: block for (at, of), block in zip(parts, forward) if of == which}
@@ -456,21 +467,25 @@
         ends.append(blocks[0] if len(blocks) == 1 else jnp.stack(blocks))
         end_masks.append(tuple(late))
 
+    masks = tuple(bits)
+    stacks = [(stack, masks), (swap(stack, wide, 1), crossed(masks))]
     for hop in range(1, hops):
-        carried = choose(owners, along[hop - 1], carried, came, False, [degree, stack])
+        carried = choose(owners, along[hop - 1], carried, came, False, [dense, stack])
         came = [swap(block, wide, bit) for block, bit in zip(carried, along[hop])]
     carried = choose(owners, along[-1], carried, came, True, ends)
-    (other,) = tie([swap(carried, wide, 1)], [], SLACK_STRIPES)
-
+    other = swap(carried, wide, 1)
     ends = tie(ends, [stacks[1][0]])
-    crossed_ends = tie([swap(end, wide, 1) for end in ends], [], SLACK)
+
+    crossed_ends = [swap(end, wide, 1) for end in ends]
     late = []
     for which in range(2):
         late.append((ends[which], which, end_masks[which]))
         late.append((crossed_ends[which], which, crossed(end_masks[which])))
 
-    arrays = (dense, carried, other, degree, sparse_weight, received, features)
-    return layer(targets, arrays, [(own, 0), (own_crossed, 1)], stacks, late, wide)
+    combined = combined_rows(
+        targets, dense, carried, other, sparse_weight, received, features
+    )
+    return layer(combined, [(own, 0), (own_crossed, 1)], stacks, late, wide)
 
 
 def solution(mesh):

time: 50.1 us -> 49.5 us (0.988)
  local copies, waits for them, and re-layouts: 6.71 us -> 5.89 us
    pallas_call x1, Pallas kernels: 7.04 us -> 4.86 us  [layer(): pl.pallas_call(functools.partial(layer_kernel, tuple((mask for _, mask in...]
    pallas_call x1 -> x2, Pallas kernels: 0.63 us -> 2.55 us  [the longest x1 2.37 us: combined_rows(): pl.pallas_call(rows_kernel, out_shape=jax.ShapeDtypeStruct(features.shape...]
    unnamed x38, local copies, waits for them, and re-layouts: 6.71 us -> 5.89 us
    all_to_all x1, waiting for transfers between devices: 0.01 us -> 0.63 us  [shards(): received = lax.all_to_all(pick(lists, features, block_rows), 'narrow', 0, 0)]
  transfers between devices with their start and end apart: 15 -> 15, of which waited for: 6 -> 9; matrix products, arithmetic and copies ran while one was open for 0% -> 0% of each run, Pallas kernels for 11% -> 15%
where the time goes in v4:
time: 49.5 us; the launch traced here: 49.1 us
  starting transfers between devices  15.9 us (32%)
  waiting for transfers between devices  14.6 us (29%)
  Pallas kernels  12.4 us (25%)
  local copies, waits for them, and re-layouts  5.89 us (12%)
    ppermute x14, waiting for transfers between devices, swap(): return lax.ppermute(block, 'wide', [(i, i ^ bit) for i in range(count)])  14 us
    ppermute x14, starting transfers between devices, swap(): return lax.ppermute(block, 'wide', [(i, i ^ bit) for i in range(count)])  11 us
    unnamed x38, local copies, waits for them, and re-layouts  5.89 us
    all_to_all x1, starting transfers between devices, shards(): received = lax.all_to_all(pick(lists, features, block_rows), 'narrow', 0, 0)  4.88 us
    pallas_call x1, Pallas kernels, layer(): pl.pallas_call(functools.partial(layer_kernel, tuple((mask for _, mask in...  4.86 us
    pallas_call x1, Pallas kernels, combined_rows(): pl.pallas_call(rows_kernel, out_shape=jax.ShapeDtypeStruct(features.shape...  2.37 us
    pallas_call x1, Pallas kernels, pick(): pl.pallas_call(functools.partial(pick_kernel, parts, cap, block_rows), ou...  1.59 us
    pallas_call x1, Pallas kernels, split(): pl.pallas_call(functools.partial(split_kernel, parts, len(packs)), out_sh...  1.39 us
  transfers between devices with their start and end apart: 15, of which 9 were waited for; matrix products, arithmetic and copies ran while one was open for 0% of the time, Pallas kernels for 15%

profile of v4, /device:TPU:0, one launch (start us, length us, event | category | flops | bytes accessed | tf_op | source)
XLA Modules:
  0.0 49.1 jit_solution(9409032831846941147)
XLA Ops:
  0.0 0.5 collective-permute-start
  0.5 0.9 %copy-done.12 = bf16[64,2048]{1,0:T(8,128)(2,1)S(1)} copy-done((bf16[64,2048]{1,0:T(8,128)(2,1)S(1)}, bf16[64,2048]{1,0:T(8,128)(2,1)}, u32[]{:S(2)}) %copy-start.12) | copy-done | bytes 262168
  1.4 0.9 %copy-done.13 = bf16[256,512]{1,0:T(8,128)(2,1)S(1)} copy-done((bf16[256,512]{1,0:T(8,128)(2,1)S(1)}, bf16[256,512]{1,0:T(8,128)(2,1)}, u32[]{:S(2)}) %copy-start.13) | copy-done | bytes 262168
  2.6 3.0 %collective-permute-start.4 = (bf16[2,256,512]{2,1,0:T(8,128)(2,1)S(1)}, bf16[2,256,512]{2,1,0:T(8,128)(2,1)}, u32[]{:S(2)}, u32[]{:S(2)}) collective-permute-start(bf16[2,256,512]{2,1,0:T(8,128)(2,1)S(1)} %pack_weights.1.refs_0_), channel_id=1, source_target_pairs={{0,16},{4,20},{8,24},{12,28},{16,0},{20,4},{24,8},{28,12},{1,17},{... | collective-permute-start | bytes 1572872 | tf_op jit(solution)/shard_map/ppermute | solution.py:44
  5.6 1.5 %collective-permute-start.3 = (bf16[2,256,512]{2,1,0:T(8,128)(2,1)S(1)}, bf16[2,256,512]{2,1,0:T(8,128)(2,1)}, u32[]{:S(2)}, u32[]{:S(2)}) collective-permute-start(bf16[2,256,512]{2,1,0:T(8,128)(2,1)S(1)} %pack_weights.1.refs_0_), channel_id=1, source_target_pairs={{0,8},{4,12},{8,0},{12,4},{16,24},{20,28},{24,16},{28,20},{1,9},{5... | collective-permute-start | bytes 1572872 | tf_op jit(solution)/shard_map/ppermute | solution.py:44
  7.1 1.0 %copy-done = bf16[512,512]{1,0:T(8,128)(2,1)S(1)} copy-done((bf16[512,512]{1,0:T(8,128)(2,1)S(1)}, bf16[512,512]{1,0:T(8,128)(2,1)}, u32[]{:S(2)}) %copy-start) | copy-done | bytes 524312
  8.1 0.7 %copy-done.16 = s32[1,4,2]{1,2,0:T(2,128)S(1)} copy-done((s32[1,4,2]{1,2,0:T(2,128)S(1)}, s32[1,4,2]{1,2,0:T(2,128)}, u32[]{:S(2)}) %copy-start.16) | copy-done | bytes 56
  8.8 1.6 %pick_blocks.1 = bf16[4,256,512]{2,1,0:T(8,128)(2,1)} custom-call(s32[1,2,4]{2,1,0:T(2,128)S(1)} %bitcast.7, bf16[512,512]{1,0:T(8,128)(2,1)S(1)} %copy-done), custom_call_target="tpu_custom_call" | custom-call | tf_op jit(solution)/shard_map/pick_blocks/pallas_call | solution.py:75
  10.4 4.9 %all-to-all-start = ((bf16[4,256,512]{2,1,0:T(8,128)(2,1)}), bf16[4,256,512]{2,1,0:T(8,128)(2,1)S(1)}, u32[]{:S(2)}, u32[]{:S(2)}) async-start(bf16[4,256,512]{2,1,0:T(8,128)(2,1)} %pick_blocks.1), calls=%async_computation | async-start | bytes 2097152 | tf_op jit(solution)/shard_map/all_to_all | solution.py:451
  15.3 0.6 %stripe_halves.1 = (bf16[256,512]{1,0:T(8,128)(2,1)S(1)}, bf16[256,512]{1,0:T(8,128)(2,1)S(1)}) custom-call(s32[2,4]{1,0:T(2,128)S(1)} %bitcast.3, bf16[512,512]{1,0:T(8,128)(2,1)S(1)} %copy-done.1, bf16[512,512]{1,0:T(8,128)(2,1)S(1)} %collective-permute-done.other_ref), custom_call_target="tpu_custom_call" | custom-call | tf_op jit(solution)/shard_map/stripe_halves/pallas_call | solution.py:116
  16.0 0.6 %collective-permute-start.1 = (bf16[256,512]{1,0:T(8,128)(2,1)S(1)}, bf16[256,512]{1,0:T(8,128)(2,1)S(1)}, u32[]{:S(2)}, u32[]{:S(2)}) collective-permute-start(bf16[256,512]{1,0:T(8,128)(2,1)S(1)} %get-tuple-element.14.refs_3_.refs_0_), channel_id=1, source_target_pairs={{0,8},{4,12},{8,0},{12,4},{16,24},{20,28},{24,16},{28,20},{1,9},{5... | collective-permute-start | bytes 786440 | tf_op jit(solution)/shard_map/ppermute | solution.py:44
  16.6 0.5 %collective-permute-start.2 = (bf16[256,512]{1,0:T(8,128)(2,1)S(1)}, bf16[256,512]{1,0:T(8,128)(2,1)S(1)}, u32[]{:S(2)}, u32[]{:S(2)}) collective-permute-start(bf16[256,512]{1,0:T(8,128)(2,1)S(1)} %get-tuple-element.15.refs_4_.refs_1_), channel_id=1, source_target_pairs={{0,16},{4,20},{8,24},{12,28},{16,0},{20,4},{24,8},{28,12},{1,17},{... | collective-permute-start | bytes 786440 | tf_op jit(solution)/shard_map/ppermute | solution.py:44
  17.1 0.8 %collective-permute-done.4.refs_1_ = bf16[2,256,512]{2,1,0:T(8,128)(2,1)} collective-permute-done((bf16[2,256,512]{2,1,0:T(8,128)(2,1)S(1)}, bf16[2,256,512]{2,1,0:T(8,128)(2,1)}, u32[]{:S(2)}, u32[]{:S(2)}) %collective-permute-start.4) | collective-permute-done | bytes 524320 | tf_op jit(solution)/shard_map/ppermute | solution.py:44
  17.9 2.6 %collective-permute-done.3.refs_0_ = bf16[2,256,512]{2,1,0:T(8,128)(2,1)} collective-permute-done((bf16[2,256,512]{2,1,0:T(8,128)(2,1)S(1)}, bf16[2,256,512]{2,1,0:T(8,128)(2,1)}, u32[]{:S(2)}, u32[]{:S(2)}) %collective-permute-start.3) | collective-permute-done | bytes 524320 | tf_op jit(solution)/shard_map/ppermute | solution.py:44
  20.5 1.4 %split_packs.1 = (bf16[2,2,256,512]{3,2,1,0:T(8,128)(2,1)S(1)}, bf16[256,512]{1,0:T(8,128)(2,1)S(1)}, bf16[256,512]{1,0:T(8,128)(2,1)S(1)}) custom-call(bf16[2,256,512]{2,1,0:T(8,128)(2,1)} %collective-permute-done.3.refs_0_, bf16[2,256,512]{2,1,0:T(8,128)(2,1)} %collective-permute-done.4.refs_1_, ...), custom_call_target="tpu_custom_call" | custom-call | tf_op jit(solution)/shard_map/split_packs/pallas_call | solution.py:216
  22.0 0.2 dense_rows.1.refs_4_.dense_ref
  22.3 2.0 %collective-permute-start.9 = (bf16[256,512]{1,0:T(8,128)(2,1)S(1)}, bf16[256,512]{1,0:T(8,128)(2,1)}, u32[]{:S(2)}, u32[]{:S(2)}) collective-permute-start(bf16[256,512]{1,0:T(8,128)(2,1)S(1)} %get-tuple-element.20), channel_id=1, source_target_pairs={{0,8},{4,12},{8,0},{12,4},{16,24},{20,28},{24,16},{28,20},{1,9},{5... | collective-permute-start | bytes 786440 | tf_op jit(solution)/shard_map/ppermute | solution.py:44
  24.3 0.6 %collective-permute-done.1.refs_2_ = bf16[256,512]{1,0:T(8,128)(2,1)S(1)} collective-permute-done((bf16[256,512]{1,0:T(8,128)(2,1)S(1)}, bf16[256,512]{1,0:T(8,128)(2,1)S(1)}, u32[]{:S(2)}, u32[]{:S(2)}) %collective-permute-start.1) | collective-permute-done | bytes 262176 | tf_op jit(solution)/shard_map/ppermute | solution.py:44
  24.8 0.6 %stripe_choice.2 = (bf16[256,512]{1,0:T(8,128)(2,1)S(1)}, bf16[256,512]{1,0:T(8,128)(2,1)S(1)}) custom-call(s32[2,4]{1,0:T(2,128)S(1)} %bitcast.4, bf16[256,512]{1,0:T(8,128)(2,1)S(1)} %get-tuple-element.14.refs_3_.refs_0_, bf16[256,512]{1,0:T(8,128)(2,1)S(1)} %get-tuple-element.15.refs_4_.refs_1_, bf16[256,512]{1,0:T(8,128)(2,1)S(1)} %collective-permute-done.1.refs_2_, ...), custom_call_target="tpu_custom_call" | custom-call | flops 2000000000 | tf_op jit(solution)/shard_map/stripe_choice/pallas_call | solution.py:159
  25.5 1.0 %collective-permute-start.6 = (bf16[256,512]{1,0:T(8,128)(2,1)S(1)}, bf16[256,512]{1,0:T(8,128)(2,1)S(1)}, u32[]{:S(2)}, u32[]{:S(2)}) collective-permute-start(bf16[256,512]{1,0:T(8,128)(2,1)S(1)} %get-tuple-element.17.refs_0_), channel_id=1, source_target_pairs={{0,16},{4,20},{8,24},{12,28},{16,0},{20,4},{24,8},{28,12},{1,17},{... | collective-permute-start | bytes 786440 | tf_op jit(solution)/shard_map/ppermute | solution.py:44
  26.5 1.0 %collective-permute-start.7 = (bf16[256,512]{1,0:T(8,128)(2,1)S(1)}, bf16[256,512]{1,0:T(8,128)(2,1)S(1)}, u32[]{:S(2)}, u32[]{:S(2)}) collective-permute-start(bf16[256,512]{1,0:T(8,128)(2,1)S(1)} %get-tuple-element.18.refs_1_), channel_id=1, source_target_pairs={{0,8},{4,12},{8,0},{12,4},{16,24},{20,28},{24,16},{28,20},{1,9},{5... | collective-permute-start | bytes 786440 | tf_op jit(solution)/shard_map/ppermute | solution.py:44
  27.6 3.9 %collective-permute-done.8.refs_4_.refs_0_ = bf16[256,512]{1,0:T(8,128)(2,1)} collective-permute-done((bf16[256,512]{1,0:T(8,128)(2,1)S(1)}, bf16[256,512]{1,0:T(8,128)(2,1)}, u32[]{:S(2)}, u32[]{:S(2)}) %collective-permute-start.8) | collective-permute-done | bytes 262176 | tf_op jit(solution)/shard_map/ppermute | solution.py:44
  31.6 5.0 %collective-permute-done.6.refs_2_ = bf16[256,512]{1,0:T(8,128)(2,1)S(1)} collective-permute-done((bf16[256,512]{1,0:T(8,128)(2,1)S(1)}, bf16[256,512]{1,0:T(8,128)(2,1)S(1)}, u32[]{:S(2)}, u32[]{:S(2)}) %collective-permute-start.6) | collective-permute-done | bytes 262176 | tf_op jit(solution)/shard_map/ppermute | solution.py:44
  36.7 0.6 %stripe_choice.3.mine_ref = bf16[2,256,512]{2,1,0:T(8,128)(2,1)S(1)} custom-call(s32[2,4]{1,0:T(2,128)S(1)} %bitcast.5, bf16[256,512]{1,0:T(8,128)(2,1)S(1)} %get-tuple-element.17.refs_0_, bf16[256,512]{1,0:T(8,128)(2,1)S(1)} %get-tuple-element.18.refs_1_, bf16[256,512]{1,0:T(8,128)(2,1)S(1)} %collective-permute-done.6.refs_2_, ...), custom_call_target="tpu_custom_call" | custom-call | flops 2000000000 | tf_op jit(solution)/shard_map/stripe_choice/pallas_call | solution.py:159
  37.4 0.5 collective-permute-start.12
  38.0 0.4 copy-done.3
  38.4 0.9 %collective-permute-done.10.other_ref = bf16[2,256,512]{2,1,0:T(8,128)(2,1)S(1)} collective-permute-done((bf16[2,256,512]{2,1,0:T(8,128)(2,1)S(1)}, bf16[2,256,512]{2,1,0:T(8,128)(2,1)S(1)}, u32[]{:S(2)}, u32[]{:S(2)}) %collective-permute-start.10) | collective-permute-done | bytes 524320 | tf_op jit(solution)/shard_map/ppermute | solution.py:44
  39.3 0.8 %copy-done.5 = bf16[2,256,512]{2,1,0:T(8,128)(2,1)} copy-done((bf16[2,256,512]{2,1,0:T(8,128)(2,1)}, bf16[2,256,512]{2,1,0:T(8,128)(2,1)S(1)}, u32[]{:S(2)}) %copy-start.5) | copy-done | bytes 524312
  40.1 0.6 %all-to-all-done.received_ref = bf16[4,256,512]{2,1,0:T(8,128)(2,1)S(1)} async-done(((bf16[4,256,512]{2,1,0:T(8,128)(2,1)}), bf16[4,256,512]{2,1,0:T(8,128)(2,1)S(1)}, u32[]{:S(2)}, u32[]{:S(2)}) %all-to-all-start) | async-done | bytes 1048608 | tf_op jit(solution)/shard_map/all_to_all | solution.py:451
  40.7 1.0 %copy-done.6 = bf16[2,256,512]{2,1,0:T(8,128)(2,1)S(1)} copy-done((bf16[2,256,512]{2,1,0:T(8,128)(2,1)S(1)}, bf16[2,256,512]{2,1,0:T(8,128)(2,1)}, u32[]{:S(2)}) %copy-start.6) | copy-done | bytes 524312
  41.8 2.4 %combined_rows.1.combined_ref = bf16[512,512]{1,0:T(8,128)(2,1)S(1)} custom-call(s32[1,2,4]{2,1,0:T(2,128)S(1)} %bitcast.6, bf16[512,1024]{1,0:T(8,128)(2,1)S(1)} %dense_rows.1.refs_4_.dense_ref, bf16[2,256,512]{2,1,0:T(8,128)(2,1)S(1)} %stripe_choice.3.mine_ref, bf16[2,256,512]{2,1,0:T(8,128)(2,1)S(1)} %copy-done.6, s32[1,4,128,128]{3,2,1,0:T(8,128)S(1)} %copy-done.11, ...), custom_call_target="tpu_custom_call" | custom-call | flops 1000000000 | bytes 4000000 | tf_op jit(solution)/shard_map/combined_rows/pallas_call | solution.py:335
  44.2 4.9 %layer.1 = bf16[512,512]{1,0:T(8,128)(2,1)} custom-call(bf16[512,512]{1,0:T(8,128)(2,1)S(1)} %combined_rows.1.combined_ref, bf16[2,256,512]{2,1,0:T(8,128)(2,1)S(1)} %copy-done.8, bf16[2,256,512]{2,1,0:T(8,128)(2,1)S(1)} %copy-done.10, bf16[2,2,256,512]{3,2,1,0:T(8,128)(2,1)S(1)} %copy-done.18, bf16[2,2,256,512]{3,2,1,0:T(8,128)(2,1)S(1)} %copy-done.4, ...), custom_call_target="tpu_custom_call" | custom-call | flops 99999997952 | bytes 4000000 | tf_op jit(solution)/shard_map/layer/pallas_call | solution.py:388
  (46 shorter events, 0.8 us)
Async XLA Ops:
  0.0 15.3 %collective-permute-start = (bf16[512,512]{1,0:T(8,128)(2,1)}, bf16[512,512]{1,0:T(8,128)(2,1)S(1)}, u32[]{:S(2)}, u32[]{:S(2)}) collective-permute-start(bf16[512,512]{1,0:T(8,128)(2,1)} %features_ref.3), channel_id=1, source_target_pairs={{0,4},{4,0},{8,12},{12,8},{16,20},{20,16},{24,28},{28,24},{1,5},{5... | collective-permute-start | bytes 1572872 | tf_op jit(solution)/shard_map/ppermute | solution.py:44
  0.5 0.9 %copy-start.12 = (bf16[64,2048]{1,0:T(8,128)(2,1)S(1)}, bf16[64,2048]{1,0:T(8,128)(2,1)}, u32[]{:S(2)}) copy-start(bf16[64,2048]{1,0:T(8,128)(2,1)} %first_ref.1) | copy-start | bytes 786436
  1.4 0.9 %copy-start.13 = (bf16[256,512]{1,0:T(8,128)(2,1)S(1)}, bf16[256,512]{1,0:T(8,128)(2,1)}, u32[]{:S(2)}) copy-start(bf16[256,512]{1,0:T(8,128)(2,1)} %second_ref.1) | copy-start | bytes 786436
  2.4 12.9 %copy-start.1 = (bf16[512,512]{1,0:T(8,128)(2,1)S(1)}, bf16[512,512]{1,0:T(8,128)(2,1)}, u32[]{:S(2)}) copy-start(bf16[512,512]{1,0:T(8,128)(2,1)} %features_ref.3) | copy-start | bytes 1572868
  2.5 13.5 %copy-start.7 = (bf16[2,256,512]{2,1,0:T(8,128)(2,1)}, bf16[2,256,512]{2,1,0:T(8,128)(2,1)S(1)}, u32[]{:S(2)}) copy-start(bf16[2,256,512]{2,1,0:T(8,128)(2,1)S(1)} %pack_weights.1.refs_0_) | copy-start | bytes 1572868
  2.5 12.8 %copy-start.14 = (s32[4,2]{0,1:T(2,128)S(1)}, s32[4,2]{0,1:T(2,128)}, u32[]{:S(2)}) copy-start(s32[4,2]{0,1:T(2,128)} %param.9) | copy-start | bytes 100
  2.5 14.6 %collective-permute-start.5 = (bf16[2,256,512]{2,1,0:T(8,128)(2,1)S(1)}, bf16[2,256,512]{2,1,0:T(8,128)(2,1)S(1)}, u32[]{:S(2)}, u32[]{:S(2)}) collective-permute-start(bf16[2,256,512]{2,1,0:T(8,128)(2,1)S(1)} %pack_weights.1.refs_0_), channel_id=1, source_target_pairs={{0,4},{4,0},{8,12},{12,8},{16,20},{20,16},{24,28},{28,24},{1,5},{5... | collective-permute-start | bytes 1572872 | tf_op jit(solution)/shard_map/ppermute | solution.py:44
  2.6 15.2 %collective-permute-start.4 = (bf16[2,256,512]{2,1,0:T(8,128)(2,1)S(1)}, bf16[2,256,512]{2,1,0:T(8,128)(2,1)}, u32[]{:S(2)}, u32[]{:S(2)}) collective-permute-start(bf16[2,256,512]{2,1,0:T(8,128)(2,1)S(1)} %pack_weights.1.refs_0_), channel_id=1, source_target_pairs={{0,16},{4,20},{8,24},{12,28},{16,0},{20,4},{24,8},{28,12},{1,17},{... | collective-permute-start | bytes 1572872 | tf_op jit(solution)/shard_map/ppermute | solution.py:44
  5.6 14.9 %collective-permute-start.3 = (bf16[2,256,512]{2,1,0:T(8,128)(2,1)S(1)}, bf16[2,256,512]{2,1,0:T(8,128)(2,1)}, u32[]{:S(2)}, u32[]{:S(2)}) collective-permute-start(bf16[2,256,512]{2,1,0:T(8,128)(2,1)S(1)} %pack_weights.1.refs_0_), channel_id=1, source_target_pairs={{0,8},{4,12},{8,0},{12,4},{16,24},{20,28},{24,16},{28,20},{1,9},{5... | collective-permute-start | bytes 1572872 | tf_op jit(solution)/shard_map/ppermute | solution.py:44
  7.1 1.0 %copy-start = (bf16[512,512]{1,0:T(8,128)(2,1)S(1)}, bf16[512,512]{1,0:T(8,128)(2,1)}, u32[]{:S(2)}) copy-start(bf16[512,512]{1,0:T(8,128)(2,1)} %features_ref.3) | copy-start | bytes 1572868
  10.4 30.3 %all-to-all-start = ((bf16[4,256,512]{2,1,0:T(8,128)(2,1)}), bf16[4,256,512]{2,1,0:T(8,128)(2,1)S(1)}, u32[]{:S(2)}, u32[]{:S(2)}) async-start(bf16[4,256,512]{2,1,0:T(8,128)(2,1)} %pick_blocks.1), calls=%async_computation | async-start | bytes 2097152 | tf_op jit(solution)/shard_map/all_to_all | solution.py:451
  15.3 6.7 %copy-start.2 = (s32[512,1024]{1,0:T(8,128)S(1)}, s32[512,1024]{1,0:T(8,128)}, u32[]{:S(2)}) copy-start(s32[512,1024]{1,0:T(8,128)} %dense_ref.1) | copy-start | bytes 6291460
  16.0 8.9 %collective-permute-start.1 = (bf16[256,512]{1,0:T(8,128)(2,1)S(1)}, bf16[256,512]{1,0:T(8,128)(2,1)S(1)}, u32[]{:S(2)}, u32[]{:S(2)}) collective-permute-start(bf16[256,512]{1,0:T(8,128)(2,1)S(1)} %get-tuple-element.14.refs_3_.refs_0_), channel_id=1, source_target_pairs={{0,8},{4,12},{8,0},{12,4},{16,24},{20,28},{24,16},{28,20},{1,9},{5... | collective-permute-start | bytes 786440 | tf_op jit(solution)/shard_map/ppermute | solution.py:44
  16.6 8.3 %collective-permute-start.2 = (bf16[256,512]{1,0:T(8,128)(2,1)S(1)}, bf16[256,512]{1,0:T(8,128)(2,1)S(1)}, u32[]{:S(2)}, u32[]{:S(2)}) collective-permute-start(bf16[256,512]{1,0:T(8,128)(2,1)S(1)} %get-tuple-element.15.refs_4_.refs_1_), channel_id=1, source_target_pairs={{0,16},{4,20},{8,24},{12,28},{16,0},{20,4},{24,8},{28,12},{1,17},{... | collective-permute-start | bytes 786440 | tf_op jit(solution)/shard_map/ppermute | solution.py:44
  17.1 5.1 %copy-start.9 = (bf16[2,256,512]{2,1,0:T(8,128)(2,1)}, bf16[2,256,512]{2,1,0:T(8,128)(2,1)S(1)}, u32[]{:S(2)}) copy-start(bf16[2,256,512]{2,1,0:T(8,128)(2,1)S(1)} %collective-permute-done.5.refs_2_.refs_1_) | copy-start | bytes 1572868
  21.9 3.6 %copy-start.17 = (bf16[2,2,256,512]{3,2,1,0:T(8,128)(2,1)}, bf16[2,2,256,512]{3,2,1,0:T(8,128)(2,1)S(1)}, u32[]{:S(2)}) copy-start(bf16[2,2,256,512]{3,2,1,0:T(8,128)(2,1)S(1)} %get-tuple-element.16.refs_5_.refs_2_) | copy-start | bytes 3145732
  21.9 15.5 %collective-permute-start.11 = (bf16[2,2,256,512]{3,2,1,0:T(8,128)(2,1)S(1)}, bf16[2,2,256,512]{3,2,1,0:T(8,128)(2,1)S(1)}, u32[]{:S(2)}, u32[]{:S(2)}) collective-permute-start(bf16[2,2,256,512]{3,2,1,0:T(8,128)(2,1)S(1)} %get-tuple-element.16.refs_5_.refs_2_), channel_id=1, source_target_pairs={{0,4},{4,0},{8,12},{12,8},{16,20},{20,16},{24,28},{28,24},{1,5},{5... | collective-permute-start | bytes 3145736 | tf_op jit(solution)/shard_map/ppermute | solution.py:44
  22.2 9.3 %collective-permute-start.8 = (bf16[256,512]{1,0:T(8,128)(2,1)S(1)}, bf16[256,512]{1,0:T(8,128)(2,1)}, u32[]{:S(2)}, u32[]{:S(2)}) collective-permute-start(bf16[256,512]{1,0:T(8,128)(2,1)S(1)} %get-tuple-element.19), channel_id=1, source_target_pairs={{0,16},{4,20},{8,24},{12,28},{16,0},{20,4},{24,8},{28,12},{1,17},{... | collective-permute-start | bytes 786440 | tf_op jit(solution)/shard_map/ppermute | solution.py:44
  22.3 9.3 %collective-permute-start.9 = (bf16[256,512]{1,0:T(8,128)(2,1)S(1)}, bf16[256,512]{1,0:T(8,128)(2,1)}, u32[]{:S(2)}, u32[]{:S(2)}) collective-permute-start(bf16[256,512]{1,0:T(8,128)(2,1)S(1)} %get-tuple-element.20), channel_id=1, source_target_pairs={{0,8},{4,12},{8,0},{12,4},{16,24},{20,28},{24,16},{28,20},{1,9},{5... | collective-permute-start | bytes 786440 | tf_op jit(solution)/shard_map/ppermute | solution.py:44
  25.5 11.1 %collective-permute-start.6 = (bf16[256,512]{1,0:T(8,128)(2,1)S(1)}, bf16[256,512]{1,0:T(8,128)(2,1)S(1)}, u32[]{:S(2)}, u32[]{:S(2)}) collective-permute-start(bf16[256,512]{1,0:T(8,128)(2,1)S(1)} %get-tuple-element.17.refs_0_), channel_id=1, source_target_pairs={{0,16},{4,20},{8,24},{12,28},{16,0},{20,4},{24,8},{28,12},{1,17},{... | collective-permute-start | bytes 786440 | tf_op jit(solution)/shard_map/ppermute | solution.py:44
  26.5 14.2 %copy-start.11 = (s32[1,4,128,128]{3,2,1,0:T(8,128)S(1)}, s32[1,4,128,128]{3,2,1,0:T(8,128)}, u32[]{:S(2)}) copy-start(s32[1,4,128,128]{3,2,1,0:T(8,128)} %tiles_ref.1) | copy-start | bytes 786436
  26.5 14.2 %copy-start.15 = (s32[1,4,2]{1,2,0:T(2,128)S(1)}, s32[1,4,2]{1,2,0:T(2,128)}, u32[]{:S(2)}) copy-start(s32[1,4,2]{1,2,0:T(2,128)} %param.13) | copy-start | bytes 100
  26.5 10.1 %collective-permute-start.7 = (bf16[256,512]{1,0:T(8,128)(2,1)S(1)}, bf16[256,512]{1,0:T(8,128)(2,1)S(1)}, u32[]{:S(2)}, u32[]{:S(2)}) collective-permute-start(bf16[256,512]{1,0:T(8,128)(2,1)S(1)} %get-tuple-element.18.refs_1_), channel_id=1, source_target_pairs={{0,8},{4,12},{8,0},{12,4},{16,24},{20,28},{24,16},{28,20},{1,9},{5... | collective-permute-start | bytes 786440 | tf_op jit(solution)/shard_map/ppermute | solution.py:44
  37.3 2.0 %collective-permute-start.10 = (bf16[2,256,512]{2,1,0:T(8,128)(2,1)S(1)}, bf16[2,256,512]{2,1,0:T(8,128)(2,1)S(1)}, u32[]{:S(2)}, u32[]{:S(2)}) collective-permute-start(bf16[2,256,512]{2,1,0:T(8,128)(2,1)S(1)} %stripe_choice.3.mine_ref), channel_id=1, source_target_pairs={{0,4},{4,0},{8,12},{12,8},{16,20},{20,16},{24,28},{28,24},{1,5},{5... | collective-permute-start | bytes 1572872 | tf_op jit(solution)/shard_map/ppermute | solution.py:44
  37.4 1.0 %copy-start.3 = (bf16[2,2,256,512]{3,2,1,0:T(8,128)(2,1)}, bf16[2,2,256,512]{3,2,1,0:T(8,128)(2,1)S(1)}, u32[]{:S(2)}) copy-start(bf16[2,2,256,512]{3,2,1,0:T(8,128)(2,1)S(1)} %collective-permute-done.11.refs_2_.refs_3_) | copy-start | bytes 3145732
  37.4 6.7 %collective-permute-start.12 = (bf16[256,512]{1,0:T(8,128)(2,1)}, bf16[256,512]{1,0:T(8,128)(2,1)}, u32[]{:S(2)}, u32[]{:S(2)}) collective-permute-start(bf16[256,512]{1,0:T(8,128)(2,1)} %get-tuple-element.21.refs_4_), channel_id=1, source_target_pairs={{0,4},{4,0},{8,12},{12,8},{16,20},{20,16},{24,28},{28,24},{1,5},{5... | collective-permute-start | bytes 786440 | tf_op jit(solution)/shard_map/ppermute | solution.py:44
  37.9 6.3 %collective-permute-start.13 = (bf16[256,512]{1,0:T(8,128)(2,1)}, bf16[256,512]{1,0:T(8,128)(2,1)}, u32[]{:S(2)}, u32[]{:S(2)}) collective-permute-start(bf16[256,512]{1,0:T(8,128)(2,1)} %get-tuple-element.22.refs_6_), channel_id=1, source_target_pairs={{0,4},{4,0},{8,12},{12,8},{16,20},{20,16},{24,28},{28,24},{1,5},{5... | collective-permute-start | bytes 786440 | tf_op jit(solution)/shard_map/ppermute | solution.py:44
  40.7 1.0 %copy-start.6 = (bf16[2,256,512]{2,1,0:T(8,128)(2,1)S(1)}, bf16[2,256,512]{2,1,0:T(8,128)(2,1)}, u32[]{:S(2)}) copy-start(bf16[2,256,512]{2,1,0:T(8,128)(2,1)} %copy-done.5) | copy-start | bytes 1572868
  41.7 2.4 %copy-start.4 = (bf16[2,2,256,512]{3,2,1,0:T(8,128)(2,1)S(1)}, bf16[2,2,256,512]{3,2,1,0:T(8,128)(2,1)}, u32[]{:S(2)}) copy-start(bf16[2,2,256,512]{3,2,1,0:T(8,128)(2,1)} %copy-done.3) | copy-start | bytes 3145732
  41.7 2.4 %copy-start.8 = (bf16[2,256,512]{2,1,0:T(8,128)(2,1)S(1)}, bf16[2,256,512]{2,1,0:T(8,128)(2,1)}, u32[]{:S(2)}) copy-start(bf16[2,256,512]{2,1,0:T(8,128)(2,1)} %copy-done.7) | copy-start | bytes 1572868
  41.8 2.4 %copy-start.10 = (bf16[2,256,512]{2,1,0:T(8,128)(2,1)S(1)}, bf16[2,256,512]{2,1,0:T(8,128)(2,1)}, u32[]{:S(2)}) copy-start(bf16[2,256,512]{2,1,0:T(8,128)(2,1)} %copy-done.9) | copy-start | bytes 1572868
  41.8 2.4 %copy-start.18 = (bf16[2,2,256,512]{3,2,1,0:T(8,128)(2,1)S(1)}, bf16[2,2,256,512]{3,2,1,0:T(8,128)(2,1)}, u32[]{:S(2)}) copy-start(bf16[2,2,256,512]{3,2,1,0:T(8,128)(2,1)} %copy-done.17) | copy-start | bytes 3145732
  (2 other events, 1.5 us)

commit v5 on v4

--- a/solution.py
+++ b/solution.py
@@ -11,8 +11,8 @@
 ABSENT = 64.0
 VMEM_LIMIT = 48 * 1024 * 1024
 LARGE_LIMIT = 48 * 1024 * 1024
-SLACK_WEIGHTS = 0
-ROWS_FLOPS = 10**9
+SLACK_WEIGHTS = 2 * 10**9
+ROWS_FLOPS = 0
 ROWS_LIMIT = 48 * 2**20
 LAYER_FLOPS = 10**11
 LAYER_BYTES = 4 * 10**6
@@ -168,63 +168,35 @@
     )(owners, *carried, *came, *after)
 
 
-def pack_kernel(first_ref, second_ref, out_ref, sems):
-    rows, width = first_ref.shape[0], out_ref.shape[2]
-    copies = [pltpu.make_async_copy(second_ref, out_ref.at[1], sems.at[0])]
-    for at in range(first_ref.shape[1] // width):
-        copies.append(
-            pltpu.make_async_copy(
-                first_ref.at[:, pl.ds(at * width, width)],
-                out_ref.at[0, pl.ds(at * rows, rows)],
-                sems.at[1 + at],
-            )
-        )
+def join_kernel(sizes, *refs):
+    count = sum(sizes)
+    sems, outs = refs[-1], refs[count:-1]
+    copies, at = [], 0
+    for out, size in zip(outs, sizes):
+        for place in range(size):
+            copies.append(pltpu.make_async_copy(refs[at], out.at[place], sems.at[at]))
+            at += 1
     for copy in copies:
         copy.start()
     for copy in copies:
         copy.wait()
 
 
-def pack(first, second):
-    blocks = first.shape[1] // second.shape[1]
-    return pl.pallas_call(
-        pack_kernel,
-        out_shape=jax.ShapeDtypeStruct((2,) + second.shape, second.dtype),
-        in_specs=[hbm()] * 2,
-        out_specs=hbm(),
-        scratch_shapes=[pltpu.SemaphoreType.DMA((1 + blocks,))],
-        compiler_params=params(LARGE_LIMIT),
-        name="pack_weights",
-    )(first, second)
-
-
-def split_kernel(parts, count, *refs):
-    ins, stack_ref, outs, sems = refs[:count], refs[-2 - len(parts)], refs[-1 - len(parts) : -1], refs[-1]
-    copies = []
-    for out, (at, part) in zip(outs, parts):
-        copies.append(pltpu.make_async_copy(ins[at].at[part], out, sems.at[len(copies)]))
-    for at in range(count):
-        copies.append(pltpu.make_async_copy(ins[at], stack_ref.at[at], sems.at[len(copies)]))
-    for copy in copies:
-        copy.start()
-    for copy in copies:
-        copy.wait()
-
-
-def split(packs, parts, after):
-    shape, dtype = packs[0].shape, packs[0].dtype
-    stack, *outs = pl.pallas_call(
-        functools.partial(split_kernel, parts, len(packs)),
-        out_shape=[jax.ShapeDtypeStruct((len(packs),) + shape, dtype)]
-        + [jax.ShapeDtypeStruct(shape[1:], dtype)] * len(parts),
-        in_specs=[anywhere()] * (len(packs) + len(after)),
-        out_specs=[anywhere()] * (1 + len(parts)),
-        scratch_shapes=[pltpu.SemaphoreType.DMA((len(parts) + len(packs),))],
+def join(stacks):
+    flat = [piece for stack in stacks for piece in stack]
+    sizes = tuple(len(stack) for stack in stacks)
+    return pl.pallas_call(
+        functools.partial(join_kernel, sizes),
+        out_shape=[
+            jax.ShapeDtypeStruct((len(stack),) + stack[0].shape, stack[0].dtype) for stack in stacks
+        ],
+        in_specs=[anywhere()] * len(flat),
+        out_specs=[anywhere()] * len(stacks),
+        scratch_shapes=[pltpu.SemaphoreType.DMA((len(flat),))],
         compiler_params=params(),
         cost_estimate=pl.CostEstimate(flops=SLACK_WEIGHTS, bytes_accessed=0, transcendentals=0),
-        name="split_packs",
-    )(*packs, *after)
-    return stack, outs
+        name="join_pieces",
+    )(*flat)
 
 
 def tie_kernel(*refs):
@@ -295,22 +267,23 @@
             count_ref[pl.ds(start, block_rows), :] += jnp.where(present[:, :LANES], weight, 0.0)
 
 
-def combine(features_ref, total_ref, count_ref, combined_ref):
+def combine(features_ref, total_ref, more_ref, count_ref, combined_ref):
     scale = lax.rsqrt(count_ref[...])
     for at in range(0, total_ref.shape[1], LANES):
         columns = pl.ds(at, LANES)
         combined_ref[:, columns] = (
-            features_ref[:, columns].astype(jnp.float32) + total_ref[:, columns] * scale
+            features_ref[:, columns].astype(jnp.float32)
+            + (total_ref[:, columns] + more_ref[:, columns]) * scale
         ).astype(jnp.bfloat16)
 
 
 def place_first(pieces, first_ref):
-    me, blocks = lax.axis_index("wide"), first_ref.shape[0]
+    me, (blocks, _, width) = lax.axis_index("wide"), first_ref.shape
     for ref, mask in pieces:
-        rows = ref.shape[0] // blocks
+        rows = ref.shape[0]
         start = pl.multiple_of((me ^ mask) * rows, rows)
         for at in range(blocks):
-            first_ref[at, pl.ds(start, rows), :] = ref[pl.ds(at * rows, rows), :]
+            first_ref[at, pl.ds(start, rows), :] = ref[:, pl.ds(at * width, width)]
 
 
 def place_second(pieces, second_ref):
@@ -320,22 +293,46 @@
         second_ref[pl.ds(pl.multiple_of((me ^ mask) * rows, rows), rows), :] = ref[...]
 
 
+def blocks_kernel(targets_ref, tiles_ref, received_ref, total_ref, count_ref):
+    total_ref[...] = jnp.zeros_like(total_ref)
+    count_ref[...] = jnp.ones_like(count_ref)
+    add_blocks(targets_ref, tiles_ref, received_ref, total_ref, count_ref)
+
+
+def block_sums(targets, tiles, received, rows):
+    width = received.shape[2]
+    return pl.pallas_call(
+        blocks_kernel,
+        out_shape=[
+            jax.ShapeDtypeStruct((rows, width), jnp.float32),
+            jax.ShapeDtypeStruct((rows, LANES), jnp.float32),
+        ],
+        in_specs=[smem(), vmem(), vmem()],
+        out_specs=[vmem(), vmem()],
+        compiler_params=params(ROWS_LIMIT),
+        cost_estimate=pl.CostEstimate(
+            flops=ROWS_FLOPS, bytes_accessed=2 * 10**6, transcendentals=0
+        ),
+        name="block_sums",
+    )(targets, tiles, received)
+
+
 def rows_kernel(
-    targets_ref, dense_ref, mine_ref, other_ref, tiles_ref, received_ref, features_ref, out_ref,
-    total_ref, count_ref
+    dense_ref, mine_ref, other_ref, total_ref, count_ref, features_ref, out_ref, sum_ref, degree_ref
 ):
     ones = jnp.ones((dense_ref.shape[1], LANES), jnp.bfloat16)
-    count_ref[...] = 1.0 + jnp.dot(dense_ref[...], ones, preferred_element_type=jnp.float32)
-    add_stripes(dense_ref, mine_ref, other_ref, total_ref)
-    add_blocks(targets_ref, tiles_ref, received_ref, total_ref, count_ref)
-    combine(features_ref, total_ref, count_ref, out_ref)
-
-
-def combined_rows(targets, dense, mine, other, tiles, received, features):
+    degree_ref[...] = count_ref[...] + jnp.dot(
+        dense_ref[...], ones, preferred_element_type=jnp.float32
+    )
+    add_stripes(dense_ref, mine_ref, other_ref, sum_ref)
+    combine(features_ref, sum_ref, total_ref, degree_ref, out_ref)
+
+
+def combined_rows(dense, mine, other, total, count, features):
     return pl.pallas_call(
         rows_kernel,
         out_shape=jax.ShapeDtypeStruct(features.shape, features.dtype),
-        in_specs=[smem()] + [vmem()] * 6,
+        in_specs=[vmem()] * 6,
         out_specs=vmem(),
         scratch_shapes=[
             pltpu.VMEM(features.shape, jnp.float32),
@@ -346,13 +343,12 @@
             flops=ROWS_FLOPS, bytes_accessed=4 * 10**6, transcendentals=0
         ),
         name="combined_rows",
-    )(targets, dense, mine, other, tiles, received, features)
-
-
-def layer_kernel(own, came, late, combined_ref, *refs):
-    count = len(own) + len(came) + len(late)
-    held = refs[count + 1 : 2 * count + 1]
-    out_ref = refs[count]
+    )(dense, mine, other, total, count, features)
+
+
+def layer_kernel(parts, combined_ref, *refs):
+    count = len(parts)
+    out_ref, held = refs[count], refs[count + 1 : 2 * count + 1]
     first_ref, second_ref, hidden_ref, sems = refs[2 * count + 1 :]
     copies = [
         pltpu.make_async_copy(ref, target, sems.at[at])
@@ -360,14 +356,11 @@
     ]
     for copy in copies:
         copy.start()
-    packs = list(zip(held, own))
-    for ref, masks in zip(held[len(own) :], came):
-        packs += [(ref.at[at], mask) for at, mask in enumerate(masks)]
-    pieces = [[(ref.at[which], mask) for ref, mask in packs] for which in range(2)]
-    for ref, (which, masks) in zip(held[len(own) + len(came) :], late):
-        pieces[which] += [
-            (ref if len(masks) == 1 else ref.at[at], mask) for at, mask in enumerate(masks)
-        ]
+    pieces = ([], [])
+    for ref, (which, masks) in zip(held, parts):
+        pieces[which].extend(
+            (ref if len(ref.shape) == 2 else ref.at[at], mask) for at, mask in enumerate(masks)
+        )
     for copy in copies:
         copy.wait()
     place_first(pieces[0], first_ref)
@@ -381,17 +374,11 @@
     ).astype(jnp.bfloat16)
 
 
-def layer(combined, own, came, late, count):
+def layer(combined, parts, depth):
     rows, width = combined.shape
-    refs = [block for block, _ in own + came] + [block for block, _, _ in late]
-    depth = own[0][0].shape[1] * count
-    return pl.pallas_call(
-        functools.partial(
-            layer_kernel,
-            tuple(mask for _, mask in own),
-            tuple(masks for _, masks in came),
-            tuple((which, masks) for _, which, masks in late),
-        ),
+    refs = [block for block, _, _ in parts]
+    return pl.pallas_call(
+        functools.partial(layer_kernel, tuple((which, masks) for _, which, masks in parts)),
         out_shape=jax.ShapeDtypeStruct((rows, width), jnp.bfloat16),
         in_specs=[vmem()] + [anywhere()] * len(refs),
         out_specs=vmem(),
@@ -446,8 +433,12 @@
     lists = jnp.transpose(send_blocks, (0, 2, 1))
     targets = jnp.transpose(target_block, (0, 2, 1))
 
-    own = pack(first_weight, second_weight)
-    packs = [swap(own, wide, bit) for bit in bits]
+    pieces = []
+    for shard in (first_weight, second_weight):
+        held = {0: shard}
+        for bit in bits:
+            held[bit] = swap(shard, wide, bit)
+        pieces.append(held)
     received = lax.all_to_all(pick(lists, features, block_rows), "narrow", 0, 0)
 
     dense = prepare(dense_weight)
@@ -456,36 +447,32 @@
     along = [tuple(orders[k % 2][hop] for k in range(stripes)) for hop in range(hops)]
     came = [swap(block, wide, bit) for block, bit in zip(carried, along[0])]
 
-    own_crossed = swap(own, wide, 1)
-    parts = [(bits.index(bit), which) for which in range(2) for bit in orders[which][:-1]]
-    stack, forward = split(packs, tuple(parts), [own_crossed] + list(carried))
+    stacks = join([list(held.values()) for held in pieces])
+    crossed_stacks = [swap(stack, wide, 1) for stack in stacks]
+    masks = (0,) + tuple(bits)
     ends, end_masks = [], []
-    for which in range(2):
-        held = {bits[at]: block for (at, of), block in zip(parts, forward) if of == which}
-        late = other_pieces(held, wide, orders[which])
+    for held, order in zip(pieces, orders):
+        late = other_pieces(held, wide, order)
         blocks = list(late.values())
         ends.append(blocks[0] if len(blocks) == 1 else jnp.stack(blocks))
         end_masks.append(tuple(late))
 
-    masks = tuple(bits)
-    stacks = [(stack, masks), (swap(stack, wide, 1), crossed(masks))]
     for hop in range(1, hops):
-        carried = choose(owners, along[hop - 1], carried, came, False, [dense, stack])
+        carried = choose(owners, along[hop - 1], carried, came, False, [dense, stacks[0]])
         came = [swap(block, wide, bit) for block, bit in zip(carried, along[hop])]
     carried = choose(owners, along[-1], carried, came, True, ends)
     other = swap(carried, wide, 1)
-    ends = tie(ends, [stacks[1][0]])
-
-    crossed_ends = [swap(end, wide, 1) for end in ends]
-    late = []
+    ends = tie(ends, crossed_stacks)
+    parts = []
     for which in range(2):
-        late.append((ends[which], which, end_masks[which]))
-        late.append((crossed_ends[which], which, crossed(end_masks[which])))
-
-    combined = combined_rows(
-        targets, dense, carried, other, sparse_weight, received, features
-    )
-    return layer(combined, [(own, 0), (own_crossed, 1)], stacks, late, wide)
+        parts.append((stacks[which], which, masks))
+        parts.append((crossed_stacks[which], which, crossed(masks)))
+        parts.append((ends[which], which, end_masks[which]))
+        parts.append((swap(ends[which], wide, 1), which, crossed(end_masks[which])))
+
+    total, count = block_sums(targets, sparse_weight, received, features.shape[0])
+    combined = combined_rows(dense, carried, other, total, count, features)
+    return layer(combined, parts, second_weight.shape[0] * wide)
 
 
 def solution(mesh):

time: 49.5 us -> 48.6 us (0.982)
  waiting for transfers between devices: 14.6 us -> 9.75 us
  starting transfers between devices: 15.9 us -> 19.9 us
  Pallas kernels: 12.4 us -> 13.7 us
  local copies, waits for them, and re-layouts: 5.89 us -> 4.63 us
    ppermute x14 -> x16, waiting for transfers between devices: 14 us -> 9.42 us  [swap(): return lax.ppermute(block, 'wide', [(i, i ^ bit) for i in range(count)])]
    ppermute x14 -> x16, starting transfers between devices: 11 us -> 14.5 us  [swap(): return lax.ppermute(block, 'wide', [(i, i ^ bit) for i in range(count)])]
    unnamed x38 -> x32, local copies, waits for them, and re-layouts: 5.89 us -> 4.63 us
    pallas_call x2, Pallas kernels: 1.28 us -> 2 us  [choose(): pl.pallas_call(functools.partial(choose_kernel, bits, stacked, len(after)...]
    pallas_call x3, Pallas kernels: 6.36 us -> 6.88 us  [the longest x1 4.78 us: layer(): pl.pallas_call(functools.partial(layer_kernel, tuple(((which, masks) for...]
  transfers between devices with their start and end apart: 15 -> 17, of which waited for: 9 -> 5; matrix products, arithmetic and copies ran while one was open for 0% -> 0% of each run, Pallas kernels for 15% -> 18%
where the time goes in v5:
time: 48.6 us; the launch traced here: 48.2 us
  starting transfers between devices  19.9 us (41%)
  Pallas kernels  13.7 us (28%)
  waiting for transfers between devices  9.75 us (20%)
  local copies, waits for them, and re-layouts  4.63 us (10%)
    ppermute x16, starting transfers between devices, swap(): return lax.ppermute(block, 'wide', [(i, i ^ bit) for i in range(count)])  14.5 us
    ppermute x16, waiting for transfers between devices, swap(): return lax.ppermute(block, 'wide', [(i, i ^ bit) for i in range(count)])  9.42 us
    all_to_all x1, starting transfers between devices, shards(): received = lax.all_to_all(pick(lists, features, block_rows), 'narrow', 0, 0)  5.32 us
    pallas_call x1, Pallas kernels, layer(): pl.pallas_call(functools.partial(layer_kernel, tuple(((which, masks) for...  4.78 us
    unnamed x32, local copies, waits for them, and re-layouts  4.63 us
    pallas_call x1, Pallas kernels, combined_rows(): pl.pallas_call(rows_kernel, out_shape=jax.ShapeDtypeStruct(features.shape...  2.38 us
    pallas_call x2, Pallas kernels, choose(): pl.pallas_call(functools.partial(choose_kernel, bits, stacked, len(after)...  2 us
    pallas_call x1, Pallas kernels, pick(): pl.pallas_call(functools.partial(pick_kernel, parts, cap, block_rows), ou...  1.59 us
  transfers between devices with their start and end apart: 17, of which 5 were waited for; matrix products, arithmetic and copies ran while one was open for 0% of the time, Pallas kernels for 18%

profile of v5, /device:TPU:0, one launch (start us, length us, event | category | flops | bytes accessed | tf_op | source)
XLA Modules:
  0.0 48.2 jit_solution(7834887396087157438)
XLA Ops:
  0.0 0.5 collective-permute-start
  0.5 2.5 %collective-permute-start.3 = (bf16[64,2048]{1,0:T(8,128)(2,1)}, bf16[64,2048]{1,0:T(8,128)(2,1)S(1)}, u32[]{:S(2)}, u32[]{:S(2)}) collective-permute-start(bf16[64,2048]{1,0:T(8,128)(2,1)} %refs_0_.1), channel_id=1, source_target_pairs={{0,8},{4,12},{8,0},{12,4},{16,24},{20,28},{24,16},{28,20},{1,9},{5... | collective-permute-start | bytes 786440 | tf_op jit(solution)/shard_map/ppermute | solution.py:44
  3.0 1.6 %collective-permute-start.6 = (bf16[256,512]{1,0:T(8,128)(2,1)}, bf16[256,512]{1,0:T(8,128)(2,1)}, u32[]{:S(2)}, u32[]{:S(2)}) collective-permute-start(bf16[256,512]{1,0:T(8,128)(2,1)} %refs_3_.1), channel_id=1, source_target_pairs={{0,16},{4,20},{8,24},{12,28},{16,0},{20,4},{24,8},{28,12},{1,17},{... | collective-permute-start | bytes 786440 | tf_op jit(solution)/shard_map/ppermute | solution.py:44
  4.6 0.5 collective-permute-start.4
  5.1 1.0 %copy-done = bf16[512,512]{1,0:T(8,128)(2,1)S(1)} copy-done((bf16[512,512]{1,0:T(8,128)(2,1)S(1)}, bf16[512,512]{1,0:T(8,128)(2,1)}, u32[]{:S(2)}) %copy-start) | copy-done | bytes 524312
  6.2 0.7 %copy-done.7 = s32[1,4,2]{1,2,0:T(2,128)S(1)} copy-done((s32[1,4,2]{1,2,0:T(2,128)S(1)}, s32[1,4,2]{1,2,0:T(2,128)}, u32[]{:S(2)}) %copy-start.7) | copy-done | bytes 56
  6.9 1.6 %pick_blocks.1 = bf16[4,256,512]{2,1,0:T(8,128)(2,1)} custom-call(s32[1,2,4]{2,1,0:T(2,128)S(1)} %bitcast.6, bf16[512,512]{1,0:T(8,128)(2,1)S(1)} %copy-done), custom_call_target="tpu_custom_call" | custom-call | tf_op jit(solution)/shard_map/pick_blocks/pallas_call | solution.py:75
  8.5 5.3 %all-to-all-start = ((bf16[4,256,512]{2,1,0:T(8,128)(2,1)}), bf16[4,256,512]{2,1,0:T(8,128)(2,1)S(1)}, u32[]{:S(2)}, u32[]{:S(2)}) async-start(bf16[4,256,512]{2,1,0:T(8,128)(2,1)} %pick_blocks.1), calls=%async_computation | async-start | bytes 2097152 | tf_op jit(solution)/shard_map/all_to_all | solution.py:442
  13.8 0.6 %stripe_halves.1 = (bf16[256,512]{1,0:T(8,128)(2,1)S(1)}, bf16[256,512]{1,0:T(8,128)(2,1)S(1)}) custom-call(s32[2,4]{1,0:T(2,128)S(1)} %bitcast.3, bf16[512,512]{1,0:T(8,128)(2,1)S(1)} %copy-done.1, bf16[512,512]{1,0:T(8,128)(2,1)S(1)} %collective-permute-done.other_ref), custom_call_target="tpu_custom_call" | custom-call | tf_op jit(solution)/shard_map/stripe_halves/pallas_call | solution.py:116
  14.5 1.6 %collective-permute-start.1 = (bf16[256,512]{1,0:T(8,128)(2,1)S(1)}, bf16[256,512]{1,0:T(8,128)(2,1)S(1)}, u32[]{:S(2)}, u32[]{:S(2)}) collective-permute-start(bf16[256,512]{1,0:T(8,128)(2,1)S(1)} %get-tuple-element.15.refs_0_), channel_id=1, source_target_pairs={{0,8},{4,12},{8,0},{12,4},{16,24},{20,28},{24,16},{28,20},{1,9},{5... | collective-permute-start | bytes 786440 | tf_op jit(solution)/shard_map/ppermute | solution.py:44
  16.0 1.6 %collective-permute-start.2 = (bf16[256,512]{1,0:T(8,128)(2,1)S(1)}, bf16[256,512]{1,0:T(8,128)(2,1)S(1)}, u32[]{:S(2)}, u32[]{:S(2)}) collective-permute-start(bf16[256,512]{1,0:T(8,128)(2,1)S(1)} %get-tuple-element.16.refs_1_), channel_id=1, source_target_pairs={{0,16},{4,20},{8,24},{12,28},{16,0},{20,4},{24,8},{28,12},{1,17},{... | collective-permute-start | bytes 786440 | tf_op jit(solution)/shard_map/ppermute | solution.py:44
  17.6 1.6 %copy-done.2 = s32[512,1024]{1,0:T(8,128)S(1)} copy-done((s32[512,1024]{1,0:T(8,128)S(1)}, s32[512,1024]{1,0:T(8,128)}, u32[]{:S(2)}) %copy-start.2) | copy-done | bytes 2097176
  19.2 0.2 dense_rows.1.refs_4_.dense_ref
  19.3 0.6 %collective-permute-start.10 = (bf16[256,512]{1,0:T(8,128)(2,1)}, bf16[256,512]{1,0:T(8,128)(2,1)}, u32[]{:S(2)}, u32[]{:S(2)}) collective-permute-start(bf16[256,512]{1,0:T(8,128)(2,1)} %collective-permute-done.6.refs_5_), channel_id=1, source_target_pairs={{0,8},{4,12},{8,0},{12,4},{16,24},{20,28},{24,16},{28,20},{1,9},{5... | collective-permute-start | bytes 786440 | tf_op jit(solution)/shard_map/ppermute | solution.py:44
  20.0 1.1 %join_pieces.1 = (bf16[3,64,2048]{2,1,0:T(8,128)(2,1)S(1)}, bf16[3,256,512]{2,1,0:T(8,128)(2,1)S(1)}) custom-call(bf16[64,2048]{1,0:T(8,128)(2,1)S(1)} %copy-done.13, bf16[64,2048]{1,0:T(8,128)(2,1)S(1)} %collective-permute-done.3.refs_1_, bf16[64,2048]{1,0:T(8,128)(2,1)S(1)} %collective-permute-done.4.refs_2_, bf16[256,512]{1,0:T(8,128)(2,1)S(1)} %copy-done.14, ...), custom_call_target="tpu_custom_call" | custom-call | flops 2000000000 | tf_op jit(solution)/shard_map/join_pieces/pallas_call | solution.py:188
  21.2 0.5 %collective-permute-start.13 = (bf16[3,256,512]{2,1,0:T(8,128)(2,1)S(1)}, bf16[3,256,512]{2,1,0:T(8,128)(2,1)S(1)}, u32[]{:S(2)}, u32[]{:S(2)}) collective-permute-start(bf16[3,256,512]{2,1,0:T(8,128)(2,1)S(1)} %get-tuple-element.22.refs_4_), channel_id=1, source_target_pairs={{0,4},{4,0},{8,12},{12,8},{16,20},{20,16},{24,28},{28,24},{1,5},{5... | collective-permute-start | bytes 2359304 | tf_op jit(solution)/shard_map/ppermute | solution.py:44
  21.7 1.2 %collective-permute-done.1.refs_2_ = bf16[256,512]{1,0:T(8,128)(2,1)S(1)} collective-permute-done((bf16[256,512]{1,0:T(8,128)(2,1)S(1)}, bf16[256,512]{1,0:T(8,128)(2,1)S(1)}, u32[]{:S(2)}, u32[]{:S(2)}) %collective-permute-start.1) | collective-permute-done | bytes 262176 | tf_op jit(solution)/shard_map/ppermute | solution.py:44
  22.8 2.5 %collective-permute-start.9 = (bf16[64,2048]{1,0:T(8,128)(2,1)}, bf16[64,2048]{1,0:T(8,128)(2,1)}, u32[]{:S(2)}, u32[]{:S(2)}) collective-permute-start(bf16[64,2048]{1,0:T(8,128)(2,1)} %copy-done.15), channel_id=1, source_target_pairs={{0,16},{4,20},{8,24},{12,28},{16,0},{20,4},{24,8},{28,12},{1,17},{... | collective-permute-start | bytes 786440 | tf_op jit(solution)/shard_map/ppermute | solution.py:44
  25.3 0.6 %stripe_choice.2 = (bf16[256,512]{1,0:T(8,128)(2,1)S(1)}, bf16[256,512]{1,0:T(8,128)(2,1)S(1)}) custom-call(s32[2,4]{1,0:T(2,128)S(1)} %bitcast.4, bf16[256,512]{1,0:T(8,128)(2,1)S(1)} %get-tuple-element.15.refs_0_, bf16[256,512]{1,0:T(8,128)(2,1)S(1)} %get-tuple-element.16.refs_1_, bf16[256,512]{1,0:T(8,128)(2,1)S(1)} %collective-permute-done.1.refs_2_, ...), custom_call_target="tpu_custom_call" | custom-call | flops 2000000000 | tf_op jit(solution)/shard_map/stripe_choice/pallas_call | solution.py:159
  26.1 1.4 %collective-permute-done.10.refs_5_.refs_1_ = bf16[256,512]{1,0:T(8,128)(2,1)} collective-permute-done((bf16[256,512]{1,0:T(8,128)(2,1)}, bf16[256,512]{1,0:T(8,128)(2,1)}, u32[]{:S(2)}, u32[]{:S(2)}) %collective-permute-start.10) | collective-permute-done | bytes 262176 | tf_op jit(solution)/shard_map/ppermute | solution.py:44
  27.5 1.5 %collective-permute-start.8 = (bf16[256,512]{1,0:T(8,128)(2,1)S(1)}, bf16[256,512]{1,0:T(8,128)(2,1)S(1)}, u32[]{:S(2)}, u32[]{:S(2)}) collective-permute-start(bf16[256,512]{1,0:T(8,128)(2,1)S(1)} %get-tuple-element.19.refs_1_), channel_id=1, source_target_pairs={{0,8},{4,12},{8,0},{12,4},{16,24},{20,28},{24,16},{28,20},{1,9},{5... | collective-permute-start | bytes 786440 | tf_op jit(solution)/shard_map/ppermute | solution.py:44
  29.0 3.9 %collective-permute-done.9.refs_4_.refs_0_ = bf16[64,2048]{1,0:T(8,128)(2,1)} collective-permute-done((bf16[64,2048]{1,0:T(8,128)(2,1)}, bf16[64,2048]{1,0:T(8,128)(2,1)}, u32[]{:S(2)}, u32[]{:S(2)}) %collective-permute-start.9) | collective-permute-done | bytes 262176 | tf_op jit(solution)/shard_map/ppermute | solution.py:44
  32.9 2.9 %collective-permute-done.7.refs_2_ = bf16[256,512]{1,0:T(8,128)(2,1)S(1)} collective-permute-done((bf16[256,512]{1,0:T(8,128)(2,1)S(1)}, bf16[256,512]{1,0:T(8,128)(2,1)S(1)}, u32[]{:S(2)}, u32[]{:S(2)}) %collective-permute-start.7) | collective-permute-done | bytes 262176 | tf_op jit(solution)/shard_map/ppermute | solution.py:44
  35.8 1.4 %stripe_choice.3.mine_ref = bf16[2,256,512]{2,1,0:T(8,128)(2,1)} custom-call(s32[2,4]{1,0:T(2,128)S(1)} %bitcast.5, bf16[256,512]{1,0:T(8,128)(2,1)S(1)} %get-tuple-element.18.refs_0_, bf16[256,512]{1,0:T(8,128)(2,1)S(1)} %get-tuple-element.19.refs_1_, bf16[256,512]{1,0:T(8,128)(2,1)S(1)} %collective-permute-done.7.refs_2_, ...), custom_call_target="tpu_custom_call" | custom-call | flops 2000000000 | tf_op jit(solution)/shard_map/stripe_choice/pallas_call | solution.py:159
  37.3 0.5 %collective-permute-start.14 = (bf16[64,2048]{1,0:T(8,128)(2,1)}, bf16[64,2048]{1,0:T(8,128)(2,1)}, u32[]{:S(2)}, u32[]{:S(2)}) collective-permute-start(bf16[64,2048]{1,0:T(8,128)(2,1)} %get-tuple-element.23.refs_2_), channel_id=1, source_target_pairs={{0,4},{4,0},{8,12},{12,8},{16,20},{20,16},{24,28},{28,24},{1,5},{5... | collective-permute-start | bytes 786440 | tf_op jit(solution)/shard_map/ppermute | solution.py:44
  37.9 0.3 copy-done.3
  38.2 0.5 collective-permute-start.15
  38.7 0.3 all-to-all-done.received_ref
  39.0 0.9 %copy-done.5 = s32[1,4,128,128]{3,2,1,0:T(8,128)S(1)} copy-done((s32[1,4,128,128]{3,2,1,0:T(8,128)S(1)}, s32[1,4,128,128]{3,2,1,0:T(8,128)}, u32[]{:S(2)}) %copy-start.5) | copy-done | bytes 262168
  39.9 1.0 %block_sums.1 = (f32[512,512]{1,0:T(8,128)S(1)}, f32[512,128]{1,0:T(8,128)S(1)}) custom-call(s32[1,2,4]{2,1,0:T(2,128)S(1)} %bitcast.7, s32[1,4,128,128]{3,2,1,0:T(8,128)S(1)} %copy-done.5, bf16[4,256,512]{2,1,0:T(8,128)(2,1)S(1)} %all-to-all-done.received_ref), custom_call_target="tpu_custom_call" | custom-call | bytes 2000000 | tf_op jit(solution)/shard_map/block_sums/pallas_call | solution.py:304
  41.0 2.4 %combined_rows.1.combined_ref = bf16[512,512]{1,0:T(8,128)(2,1)S(1)} custom-call(bf16[512,1024]{1,0:T(8,128)(2,1)S(1)} %dense_rows.1.refs_4_.dense_ref, bf16[2,256,512]{2,1,0:T(8,128)(2,1)} %stripe_choice.3.mine_ref, bf16[2,256,512]{2,1,0:T(8,128)(2,1)} %collective-permute-done.11.other_ref, f32[512,512]{1,0:T(8,128)S(1)} %get-tuple-element.20.total_ref, ...), custom_call_target="tpu_custom_call" | custom-call | bytes 4000000 | tf_op jit(solution)/shard_map/combined_rows/pallas_call | solution.py:332
  43.4 4.8 %layer.1 = bf16[512,512]{1,0:T(8,128)(2,1)} custom-call(bf16[512,512]{1,0:T(8,128)(2,1)S(1)} %combined_rows.1.combined_ref, bf16[3,64,2048]{2,1,0:T(8,128)(2,1)S(1)} %copy-done.10, bf16[3,64,2048]{2,1,0:T(8,128)(2,1)S(1)} %collective-permute-done.12.refs_2_.refs_1_, bf16[64,2048]{1,0:T(8,128)(2,1)} %get-tuple-element.23.refs_2_, ...), custom_call_target="tpu_custom_call" | custom-call | flops 99999997952 | bytes 4000000 | tf_op jit(solution)/shard_map/layer/pallas_call | solution.py:380
  (44 shorter events, 0.4 us)
Async XLA Ops:
  0.0 13.8 %copy-start.6 = (s32[4,2]{0,1:T(2,128)S(1)}, s32[4,2]{0,1:T(2,128)}, u32[]{:S(2)}) copy-start(s32[4,2]{0,1:T(2,128)} %param.9) | copy-start | bytes 100
  0.0 13.8 %collective-permute-start = (bf16[512,512]{1,0:T(8,128)(2,1)}, bf16[512,512]{1,0:T(8,128)(2,1)S(1)}, u32[]{:S(2)}, u32[]{:S(2)}) collective-permute-start(bf16[512,512]{1,0:T(8,128)(2,1)} %features_ref.3), channel_id=1, source_target_pairs={{0,4},{4,0},{8,12},{12,8},{16,20},{20,16},{24,28},{28,24},{1,5},{5... | collective-permute-start | bytes 1572872 | tf_op jit(solution)/shard_map/ppermute | solution.py:44
  0.5 15.6 %collective-permute-start.3 = (bf16[64,2048]{1,0:T(8,128)(2,1)}, bf16[64,2048]{1,0:T(8,128)(2,1)S(1)}, u32[]{:S(2)}, u32[]{:S(2)}) collective-permute-start(bf16[64,2048]{1,0:T(8,128)(2,1)} %refs_0_.1), channel_id=1, source_target_pairs={{0,8},{4,12},{8,0},{12,4},{16,24},{20,28},{24,16},{28,20},{1,9},{5... | collective-permute-start | bytes 786440 | tf_op jit(solution)/shard_map/ppermute | solution.py:44
  3.0 16.3 %collective-permute-start.6 = (bf16[256,512]{1,0:T(8,128)(2,1)}, bf16[256,512]{1,0:T(8,128)(2,1)}, u32[]{:S(2)}, u32[]{:S(2)}) collective-permute-start(bf16[256,512]{1,0:T(8,128)(2,1)} %refs_3_.1), channel_id=1, source_target_pairs={{0,16},{4,20},{8,24},{12,28},{16,0},{20,4},{24,8},{28,12},{1,17},{... | collective-permute-start | bytes 786440 | tf_op jit(solution)/shard_map/ppermute | solution.py:44
  4.6 15.4 %collective-permute-start.4 = (bf16[64,2048]{1,0:T(8,128)(2,1)}, bf16[64,2048]{1,0:T(8,128)(2,1)S(1)}, u32[]{:S(2)}, u32[]{:S(2)}) collective-permute-start(bf16[64,2048]{1,0:T(8,128)(2,1)} %refs_0_.1), channel_id=1, source_target_pairs={{0,16},{4,20},{8,24},{12,28},{16,0},{20,4},{24,8},{28,12},{1,17},{... | collective-permute-start | bytes 786440 | tf_op jit(solution)/shard_map/ppermute | solution.py:44
  5.0 14.9 %collective-permute-start.5 = (bf16[256,512]{1,0:T(8,128)(2,1)}, bf16[256,512]{1,0:T(8,128)(2,1)S(1)}, u32[]{:S(2)}, u32[]{:S(2)}) collective-permute-start(bf16[256,512]{1,0:T(8,128)(2,1)} %refs_3_.1), channel_id=1, source_target_pairs={{0,8},{4,12},{8,0},{12,4},{16,24},{20,28},{24,16},{28,20},{1,9},{5... | collective-permute-start | bytes 786440 | tf_op jit(solution)/shard_map/ppermute | solution.py:44
  5.1 1.0 %copy-start = (bf16[512,512]{1,0:T(8,128)(2,1)S(1)}, bf16[512,512]{1,0:T(8,128)(2,1)}, u32[]{:S(2)}) copy-start(bf16[512,512]{1,0:T(8,128)(2,1)} %features_ref.3) | copy-start | bytes 1572868
  6.8 6.9 %copy-start.1 = (bf16[512,512]{1,0:T(8,128)(2,1)S(1)}, bf16[512,512]{1,0:T(8,128)(2,1)}, u32[]{:S(2)}) copy-start(bf16[512,512]{1,0:T(8,128)(2,1)} %features_ref.3) | copy-start | bytes 1572868
  8.5 30.5 %all-to-all-start = ((bf16[4,256,512]{2,1,0:T(8,128)(2,1)}), bf16[4,256,512]{2,1,0:T(8,128)(2,1)S(1)}, u32[]{:S(2)}, u32[]{:S(2)}) async-start(bf16[4,256,512]{2,1,0:T(8,128)(2,1)} %pick_blocks.1), calls=%async_computation | async-start | bytes 2097152 | tf_op jit(solution)/shard_map/all_to_all | solution.py:442
  13.8 6.2 %copy-start.13 = (bf16[64,2048]{1,0:T(8,128)(2,1)S(1)}, bf16[64,2048]{1,0:T(8,128)(2,1)}, u32[]{:S(2)}) copy-start(bf16[64,2048]{1,0:T(8,128)(2,1)} %refs_0_.1) | copy-start | bytes 786436
  13.8 6.2 %copy-start.14 = (bf16[256,512]{1,0:T(8,128)(2,1)S(1)}, bf16[256,512]{1,0:T(8,128)(2,1)}, u32[]{:S(2)}) copy-start(bf16[256,512]{1,0:T(8,128)(2,1)} %refs_3_.1) | copy-start | bytes 786436
  14.5 8.4 %collective-permute-start.1 = (bf16[256,512]{1,0:T(8,128)(2,1)S(1)}, bf16[256,512]{1,0:T(8,128)(2,1)S(1)}, u32[]{:S(2)}, u32[]{:S(2)}) collective-permute-start(bf16[256,512]{1,0:T(8,128)(2,1)S(1)} %get-tuple-element.15.refs_0_), channel_id=1, source_target_pairs={{0,8},{4,12},{8,0},{12,4},{16,24},{20,28},{24,16},{28,20},{1,9},{5... | collective-permute-start | bytes 786440 | tf_op jit(solution)/shard_map/ppermute | solution.py:44
  16.0 5.1 %copy-start.15 = (bf16[64,2048]{1,0:T(8,128)(2,1)}, bf16[64,2048]{1,0:T(8,128)(2,1)S(1)}, u32[]{:S(2)}) copy-start(bf16[64,2048]{1,0:T(8,128)(2,1)S(1)} %collective-permute-done.3.refs_1_) | copy-start | bytes 786436
  16.0 9.3 %collective-permute-start.2 = (bf16[256,512]{1,0:T(8,128)(2,1)S(1)}, bf16[256,512]{1,0:T(8,128)(2,1)S(1)}, u32[]{:S(2)}, u32[]{:S(2)}) collective-permute-start(bf16[256,512]{1,0:T(8,128)(2,1)S(1)} %get-tuple-element.16.refs_1_), channel_id=1, source_target_pairs={{0,16},{4,20},{8,24},{12,28},{16,0},{20,4},{24,8},{28,12},{1,17},{... | collective-permute-start | bytes 786440 | tf_op jit(solution)/shard_map/ppermute | solution.py:44
  17.6 1.6 %copy-start.2 = (s32[512,1024]{1,0:T(8,128)S(1)}, s32[512,1024]{1,0:T(8,128)}, u32[]{:S(2)}) copy-start(s32[512,1024]{1,0:T(8,128)} %dense_ref.1) | copy-start | bytes 6291460
  19.3 8.2 %collective-permute-start.10 = (bf16[256,512]{1,0:T(8,128)(2,1)}, bf16[256,512]{1,0:T(8,128)(2,1)}, u32[]{:S(2)}, u32[]{:S(2)}) collective-permute-start(bf16[256,512]{1,0:T(8,128)(2,1)} %collective-permute-done.6.refs_5_), channel_id=1, source_target_pairs={{0,8},{4,12},{8,0},{12,4},{16,24},{20,28},{24,16},{28,20},{1,9},{5... | collective-permute-start | bytes 786440 | tf_op jit(solution)/shard_map/ppermute | solution.py:44
  21.1 4.9 %copy-start.9 = (bf16[3,64,2048]{2,1,0:T(8,128)(2,1)}, bf16[3,64,2048]{2,1,0:T(8,128)(2,1)S(1)}, u32[]{:S(2)}) copy-start(bf16[3,64,2048]{2,1,0:T(8,128)(2,1)S(1)} %get-tuple-element.17.refs_5_.refs_0_) | copy-start | bytes 2359300
  21.1 4.9 %copy-start.11 = (bf16[3,256,512]{2,1,0:T(8,128)(2,1)}, bf16[3,256,512]{2,1,0:T(8,128)(2,1)S(1)}, u32[]{:S(2)}) copy-start(bf16[3,256,512]{2,1,0:T(8,128)(2,1)S(1)} %get-tuple-element.22.refs_4_) | copy-start | bytes 2359300
  21.1 16.2 %collective-permute-start.12 = (bf16[3,64,2048]{2,1,0:T(8,128)(2,1)S(1)}, bf16[3,64,2048]{2,1,0:T(8,128)(2,1)S(1)}, u32[]{:S(2)}, u32[]{:S(2)}) collective-permute-start(bf16[3,64,2048]{2,1,0:T(8,128)(2,1)S(1)} %get-tuple-element.17.refs_5_.refs_0_), channel_id=1, source_target_pairs={{0,4},{4,0},{8,12},{12,8},{16,20},{20,16},{24,28},{28,24},{1,5},{5... | collective-permute-start | bytes 2359304 | tf_op jit(solution)/shard_map/ppermute | solution.py:44
  21.2 16.1 %collective-permute-start.13 = (bf16[3,256,512]{2,1,0:T(8,128)(2,1)S(1)}, bf16[3,256,512]{2,1,0:T(8,128)(2,1)S(1)}, u32[]{:S(2)}, u32[]{:S(2)}) collective-permute-start(bf16[3,256,512]{2,1,0:T(8,128)(2,1)S(1)} %get-tuple-element.22.refs_4_), channel_id=1, source_target_pairs={{0,4},{4,0},{8,12},{12,8},{16,20},{20,16},{24,28},{28,24},{1,5},{5... | collective-permute-start | bytes 2359304 | tf_op jit(solution)/shard_map/ppermute | solution.py:44
  22.8 10.0 %collective-permute-start.9 = (bf16[64,2048]{1,0:T(8,128)(2,1)}, bf16[64,2048]{1,0:T(8,128)(2,1)}, u32[]{:S(2)}, u32[]{:S(2)}) collective-permute-start(bf16[64,2048]{1,0:T(8,128)(2,1)} %copy-done.15), channel_id=1, source_target_pairs={{0,16},{4,20},{8,24},{12,28},{16,0},{20,4},{24,8},{28,12},{1,17},{... | collective-permute-start | bytes 786440 | tf_op jit(solution)/shard_map/ppermute | solution.py:44
  26.0 9.8 %collective-permute-start.7 = (bf16[256,512]{1,0:T(8,128)(2,1)S(1)}, bf16[256,512]{1,0:T(8,128)(2,1)S(1)}, u32[]{:S(2)}, u32[]{:S(2)}) collective-permute-start(bf16[256,512]{1,0:T(8,128)(2,1)S(1)} %get-tuple-element.18.refs_0_), channel_id=1, source_target_pairs={{0,16},{4,20},{8,24},{12,28},{16,0},{20,4},{24,8},{28,12},{1,17},{... | collective-permute-start | bytes 786440 | tf_op jit(solution)/shard_map/ppermute | solution.py:44
  27.5 8.3 %collective-permute-start.8 = (bf16[256,512]{1,0:T(8,128)(2,1)S(1)}, bf16[256,512]{1,0:T(8,128)(2,1)S(1)}, u32[]{:S(2)}, u32[]{:S(2)}) collective-permute-start(bf16[256,512]{1,0:T(8,128)(2,1)S(1)} %get-tuple-element.19.refs_1_), channel_id=1, source_target_pairs={{0,8},{4,12},{8,0},{12,4},{16,24},{20,28},{24,16},{28,20},{1,9},{5... | collective-permute-start | bytes 786440 | tf_op jit(solution)/shard_map/ppermute | solution.py:44
  37.2 1.8 %copy-start.8 = (s32[1,4,2]{1,2,0:T(2,128)S(1)}, s32[1,4,2]{1,2,0:T(2,128)}, u32[]{:S(2)}) copy-start(s32[1,4,2]{1,2,0:T(2,128)} %param.13) | copy-start | bytes 100
  37.2 3.8 %collective-permute-start.11 = (bf16[2,256,512]{2,1,0:T(8,128)(2,1)}, bf16[2,256,512]{2,1,0:T(8,128)(2,1)}, u32[]{:S(2)}, u32[]{:S(2)}) collective-permute-start(bf16[2,256,512]{2,1,0:T(8,128)(2,1)} %stripe_choice.3.mine_ref), channel_id=1, source_target_pairs={{0,4},{4,0},{8,12},{12,8},{16,20},{20,16},{24,28},{28,24},{1,5},{5... | collective-permute-start | bytes 1572872 | tf_op jit(solution)/shard_map/ppermute | solution.py:44
  37.3 0.9 %copy-start.3 = (bf16[3,256,512]{2,1,0:T(8,128)(2,1)}, bf16[3,256,512]{2,1,0:T(8,128)(2,1)S(1)}, u32[]{:S(2)}) copy-start(bf16[3,256,512]{2,1,0:T(8,128)(2,1)S(1)} %collective-permute-done.13.refs_3_.refs_5_) | copy-start | bytes 2359300
  37.3 6.1 %collective-permute-start.14 = (bf16[64,2048]{1,0:T(8,128)(2,1)}, bf16[64,2048]{1,0:T(8,128)(2,1)}, u32[]{:S(2)}, u32[]{:S(2)}) collective-permute-start(bf16[64,2048]{1,0:T(8,128)(2,1)} %get-tuple-element.23.refs_2_), channel_id=1, source_target_pairs={{0,4},{4,0},{8,12},{12,8},{16,20},{20,16},{24,28},{28,24},{1,5},{5... | collective-permute-start | bytes 786440 | tf_op jit(solution)/shard_map/ppermute | solution.py:44
  38.2 5.2 %collective-permute-start.15 = (bf16[256,512]{1,0:T(8,128)(2,1)}, bf16[256,512]{1,0:T(8,128)(2,1)}, u32[]{:S(2)}, u32[]{:S(2)}) collective-permute-start(bf16[256,512]{1,0:T(8,128)(2,1)} %get-tuple-element.24.refs_6_), channel_id=1, source_target_pairs={{0,4},{4,0},{8,12},{12,8},{16,20},{20,16},{24,28},{28,24},{1,5},{5... | collective-permute-start | bytes 786440 | tf_op jit(solution)/shard_map/ppermute | solution.py:44
  39.0 1.0 %copy-start.5 = (s32[1,4,128,128]{3,2,1,0:T(8,128)S(1)}, s32[1,4,128,128]{3,2,1,0:T(8,128)}, u32[]{:S(2)}) copy-start(s32[1,4,128,128]{3,2,1,0:T(8,128)} %tiles_ref.1) | copy-start | bytes 786436
  41.0 2.4 %copy-start.4 = (bf16[3,256,512]{2,1,0:T(8,128)(2,1)S(1)}, bf16[3,256,512]{2,1,0:T(8,128)(2,1)}, u32[]{:S(2)}) copy-start(bf16[3,256,512]{2,1,0:T(8,128)(2,1)} %copy-done.3) | copy-start | bytes 2359300
  41.0 2.4 %copy-start.10 = (bf16[3,64,2048]{2,1,0:T(8,128)(2,1)S(1)}, bf16[3,64,2048]{2,1,0:T(8,128)(2,1)}, u32[]{:S(2)}) copy-start(bf16[3,64,2048]{2,1,0:T(8,128)(2,1)} %copy-done.9) | copy-start | bytes 2359300
  41.0 2.4 %copy-start.12 = (bf16[3,256,512]{2,1,0:T(8,128)(2,1)S(1)}, bf16[3,256,512]{2,1,0:T(8,128)(2,1)}, u32[]{:S(2)}) copy-start(bf16[3,256,512]{2,1,0:T(8,128)(2,1)} %copy-done.11) | copy-start | bytes 2359300
  (1 other events, 0.7 us)

commit v6 on v5

--- a/solution.py
+++ b/solution.py
@@ -216,25 +216,35 @@
     )(*blocks, *after)
 
 
-def prepare_kernel(dense_ref, out_ref):
+def prepare_kernel(dense_ref, tiles_ref, out_ref, tiles_out):
     out_ref[...] = dense_ref[...].astype(jnp.float32).astype(jnp.bfloat16)
-
-
-def prepare(dense_weight):
+    tiles_out[...] = tiles_ref[...].astype(jnp.float32).astype(jnp.bfloat16)
+
+
+def prepare(dense_weight, tiles):
     rows, columns = dense_weight.shape
     step = rows // 4
     return pl.pallas_call(
         prepare_kernel,
         grid=(rows // step,),
-        out_shape=jax.ShapeDtypeStruct((rows, columns), jnp.bfloat16),
-        in_specs=[pl.BlockSpec((step, columns), lambda i: (i, 0))],
-        out_specs=pl.BlockSpec((step, columns), lambda i: (i, 0)),
+        out_shape=[
+            jax.ShapeDtypeStruct((rows, columns), jnp.bfloat16),
+            jax.ShapeDtypeStruct(tiles.shape, jnp.bfloat16),
+        ],
+        in_specs=[
+            pl.BlockSpec((step, columns), lambda i: (i, 0)),
+            pl.BlockSpec(tiles.shape, lambda i: (0, 0, 0, 0)),
+        ],
+        out_specs=[
+            pl.BlockSpec((step, columns), lambda i: (i, 0)),
+            pl.BlockSpec(tiles.shape, lambda i: (0, 0, 0, 0)),
+        ],
         compiler_params=params(),
         cost_estimate=pl.CostEstimate(
             flops=2 * rows * columns, bytes_accessed=6 * rows * columns, transcendentals=0
         ),
         name="dense_rows",
-    )(dense_weight)
+    )(dense_weight, tiles)
 
 
 def add_stripes(dense_ref, mine_ref, other_ref, total_ref):
@@ -254,7 +264,7 @@
 def add_blocks(targets_ref, tiles_ref, received_ref, total_ref, count_ref):
     _, parts, block_rows, _ = tiles_ref.shape
     for source in range(parts):
-        tile = tiles_ref[0, source].astype(jnp.float32).astype(jnp.bfloat16)
+        tile = tiles_ref[0, source]
         ones = jnp.ones((tile.shape[1], LANES), jnp.bfloat16)
         weight = jnp.dot(tile, ones, preferred_element_type=jnp.float32)
         for slot in range(received_ref.shape[1] // block_rows):
@@ -361,13 +371,17 @@
         pieces[which].extend(
             (ref if len(ref.shape) == 2 else ref.at[at], mask) for at, mask in enumerate(masks)
         )
-    for copy in copies:
-        copy.wait()
+    for copy, (which, _) in zip(copies, parts):
+        if which == 0:
+            copy.wait()
     place_first(pieces[0], first_ref)
     width = first_ref.shape[2]
     for at in range(first_ref.shape[0]):
         gated = jnp.dot(combined_ref[...], first_ref[at], preferred_element_type=jnp.float32)
         hidden_ref[:, pl.ds(at * width, width)] = jnp.maximum(gated, 0.0).astype(jnp.bfloat16)
+    for copy, (which, _) in zip(copies, parts):
+        if which == 1:
+            copy.wait()
     place_second(pieces[1], second_ref)
     out_ref[...] = jnp.dot(
         hidden_ref[...], second_ref[...], preferred_element_type=jnp.float32
@@ -441,7 +455,7 @@
         pieces.append(held)
     received = lax.all_to_all(pick(lists, features, block_rows), "narrow", 0, 0)
 
-    dense = prepare(dense_weight)
+    dense, tiles = prepare(dense_weight, sparse_weight)
 
     carried = halves(owners, features, swap(features, wide, 1))
     along = [tuple(orders[k % 2][hop] for k in range(stripes)) for hop in range(hops)]
@@ -470,7 +484,7 @@
         parts.append((ends[which], which, end_masks[which]))
         parts.append((swap(ends[which], wide, 1), which, crossed(end_masks[which])))
 
-    total, count = block_sums(targets, sparse_weight, received, features.shape[0])
+    total, count = block_sums(targets, tiles, received, features.shape[0])
     combined = combined_rows(dense, carried, other, total, count, features)
     return layer(combined, parts, second_weight.shape[0] * wide)
 

time: 48.6 us -> 48.1 us (0.990)
  waiting for transfers between devices: 9.75 us -> 9.13 us
    unnamed x32 -> x34, local copies, waits for them, and re-layouts: 4.63 us -> 4.49 us
  transfers between devices with their start and end apart: 17 -> 17, of which waited for: 5 -> 3; matrix products, arithmetic and copies ran while one was open for 0% -> 0% of each run, Pallas kernels for 18% -> 19%
where the time goes in v6:
time: 48.1 us; the launch traced here: 47.7 us
  starting transfers between devices  20 us (42%)
  Pallas kernels  13.9 us (29%)
  waiting for transfers between devices  9.13 us (19%)
  local copies, waits for them, and re-layouts  4.49 us (9%)
    ppermute x16, starting transfers between devices, swap(): return lax.ppermute(block, 'wide', [(i, i ^ bit) for i in range(count)])  14.6 us
    ppermute x16, waiting for transfers between devices, swap(): return lax.ppermute(block, 'wide', [(i, i ^ bit) for i in range(count)])  9.12 us
    all_to_all x1, starting transfers between devices, shards(): received = lax.all_to_all(pick(lists, features, block_rows), 'narrow', 0, 0)  5.32 us
    pallas_call x1, Pallas kernels, layer(): pl.pallas_call(functools.partial(layer_kernel, tuple(((which, masks) for...  4.79 us
    unnamed x34, local copies, waits for them, and re-layouts  4.49 us
    pallas_call x1, Pallas kernels, combined_rows(): pl.pallas_call(rows_kernel, out_shape=jax.ShapeDtypeStruct(features.shape...  2.39 us
    pallas_call x2, Pallas kernels, choose(): pl.pallas_call(functools.partial(choose_kernel, bits, stacked, len(after)...  2 us
    pallas_call x1, Pallas kernels, pick(): pl.pallas_call(functools.partial(pick_kernel, parts, cap, block_rows), ou...  1.6 us
  transfers between devices with their start and end apart: 17, of which 3 were waited for; matrix products, arithmetic and copies ran while one was open for 0% of the time, Pallas kernels for 19%

profile of v6, /device:TPU:0, one launch (start us, length us, event | category | flops | bytes accessed | tf_op | source)
XLA Modules:
  0.0 47.7 jit_solution(14694680192346210721)
XLA Ops:
  0.0 0.5 collective-permute-start
  0.5 2.5 %collective-permute-start.3 = (bf16[64,2048]{1,0:T(8,128)(2,1)}, bf16[64,2048]{1,0:T(8,128)(2,1)S(1)}, u32[]{:S(2)}, u32[]{:S(2)}) collective-permute-start(bf16[64,2048]{1,0:T(8,128)(2,1)} %refs_0_.1), channel_id=1, source_target_pairs={{0,8},{4,12},{8,0},{12,4},{16,24},{20,28},{24,16},{28,20},{1,9},{5... | collective-permute-start | bytes 786440 | tf_op jit(solution)/shard_map/ppermute | solution.py:44
  3.0 1.6 %collective-permute-start.6 = (bf16[256,512]{1,0:T(8,128)(2,1)}, bf16[256,512]{1,0:T(8,128)(2,1)}, u32[]{:S(2)}, u32[]{:S(2)}) collective-permute-start(bf16[256,512]{1,0:T(8,128)(2,1)} %refs_3_.1), channel_id=1, source_target_pairs={{0,16},{4,20},{8,24},{12,28},{16,0},{20,4},{24,8},{28,12},{1,17},{... | collective-permute-start | bytes 786440 | tf_op jit(solution)/shard_map/ppermute | solution.py:44
  4.6 0.5 collective-permute-start.4
  5.1 1.0 %copy-done = bf16[512,512]{1,0:T(8,128)(2,1)S(1)} copy-done((bf16[512,512]{1,0:T(8,128)(2,1)S(1)}, bf16[512,512]{1,0:T(8,128)(2,1)}, u32[]{:S(2)}) %copy-start) | copy-done | bytes 524312
  6.2 0.7 %copy-done.7 = s32[1,4,2]{1,2,0:T(2,128)S(1)} copy-done((s32[1,4,2]{1,2,0:T(2,128)S(1)}, s32[1,4,2]{1,2,0:T(2,128)}, u32[]{:S(2)}) %copy-start.7) | copy-done | bytes 56
  6.9 1.6 %pick_blocks.1 = bf16[4,256,512]{2,1,0:T(8,128)(2,1)} custom-call(s32[1,2,4]{2,1,0:T(2,128)S(1)} %bitcast.6, bf16[512,512]{1,0:T(8,128)(2,1)S(1)} %copy-done), custom_call_target="tpu_custom_call" | custom-call | tf_op jit(solution)/shard_map/pick_blocks/pallas_call | solution.py:75
  8.5 5.3 %all-to-all-start = ((bf16[4,256,512]{2,1,0:T(8,128)(2,1)}), bf16[4,256,512]{2,1,0:T(8,128)(2,1)S(1)}, u32[]{:S(2)}, u32[]{:S(2)}) async-start(bf16[4,256,512]{2,1,0:T(8,128)(2,1)} %pick_blocks.1), calls=%async_computation | async-start | bytes 2097152 | tf_op jit(solution)/shard_map/all_to_all | solution.py:456
  13.8 0.6 %stripe_halves.1 = (bf16[256,512]{1,0:T(8,128)(2,1)S(1)}, bf16[256,512]{1,0:T(8,128)(2,1)S(1)}) custom-call(s32[2,4]{1,0:T(2,128)S(1)} %bitcast.3, bf16[512,512]{1,0:T(8,128)(2,1)S(1)} %copy-done.1, bf16[512,512]{1,0:T(8,128)(2,1)S(1)} %collective-permute-done.other_ref), custom_call_target="tpu_custom_call" | custom-call | tf_op jit(solution)/shard_map/stripe_halves/pallas_call | solution.py:116
  14.5 1.6 %collective-permute-start.1 = (bf16[256,512]{1,0:T(8,128)(2,1)S(1)}, bf16[256,512]{1,0:T(8,128)(2,1)S(1)}, u32[]{:S(2)}, u32[]{:S(2)}) collective-permute-start(bf16[256,512]{1,0:T(8,128)(2,1)S(1)} %get-tuple-element.18.refs_0_), channel_id=1, source_target_pairs={{0,8},{4,12},{8,0},{12,4},{16,24},{20,28},{24,16},{28,20},{1,9},{5... | collective-permute-start | bytes 786440 | tf_op jit(solution)/shard_map/ppermute | solution.py:44
  16.0 0.7 %copy-done.15 = bf16[64,2048]{1,0:T(8,128)(2,1)} copy-done((bf16[64,2048]{1,0:T(8,128)(2,1)}, bf16[64,2048]{1,0:T(8,128)(2,1)S(1)}, u32[]{:S(2)}) %copy-start.15) | copy-done | bytes 262168
  16.7 1.6 %collective-permute-start.2 = (bf16[256,512]{1,0:T(8,128)(2,1)S(1)}, bf16[256,512]{1,0:T(8,128)(2,1)S(1)}, u32[]{:S(2)}, u32[]{:S(2)}) collective-permute-start(bf16[256,512]{1,0:T(8,128)(2,1)S(1)} %get-tuple-element.19.refs_1_), channel_id=1, source_target_pairs={{0,16},{4,20},{8,24},{12,28},{16,0},{20,4},{24,8},{28,12},{1,17},{... | collective-permute-start | bytes 786440 | tf_op jit(solution)/shard_map/ppermute | solution.py:44
  18.3 1.6 %copy-done.2 = s32[512,1024]{1,0:T(8,128)S(1)} copy-done((s32[512,1024]{1,0:T(8,128)S(1)}, s32[512,1024]{1,0:T(8,128)}, u32[]{:S(2)}) %copy-start.2) | copy-done | bytes 2097176
  19.9 0.2 dense_rows.1
  20.1 0.6 %collective-permute-start.10 = (bf16[256,512]{1,0:T(8,128)(2,1)}, bf16[256,512]{1,0:T(8,128)(2,1)}, u32[]{:S(2)}, u32[]{:S(2)}) collective-permute-start(bf16[256,512]{1,0:T(8,128)(2,1)} %collective-permute-done.6.refs_5_), channel_id=1, source_target_pairs={{0,8},{4,12},{8,0},{12,4},{16,24},{20,28},{24,16},{28,20},{1,9},{5... | collective-permute-start | bytes 786440 | tf_op jit(solution)/shard_map/ppermute | solution.py:44
  20.7 0.1 copy-done.16
  20.8 1.2 %join_pieces.1 = (bf16[3,64,2048]{2,1,0:T(8,128)(2,1)S(1)}, bf16[3,256,512]{2,1,0:T(8,128)(2,1)S(1)}) custom-call(bf16[64,2048]{1,0:T(8,128)(2,1)S(1)} %copy-done.13, bf16[64,2048]{1,0:T(8,128)(2,1)S(1)} %copy-done.16, bf16[64,2048]{1,0:T(8,128)(2,1)} %collective-permute-done.4.refs_2_, bf16[256,512]{1,0:T(8,128)(2,1)S(1)} %copy-done.14, ...), custom_call_target="tpu_custom_call" | custom-call | flops 2000000000 | tf_op jit(solution)/shard_map/join_pieces/pallas_call | solution.py:188
  22.1 0.5 %collective-permute-start.13 = (bf16[3,256,512]{2,1,0:T(8,128)(2,1)S(1)}, bf16[3,256,512]{2,1,0:T(8,128)(2,1)S(1)}, u32[]{:S(2)}, u32[]{:S(2)}) collective-permute-start(bf16[3,256,512]{2,1,0:T(8,128)(2,1)S(1)} %get-tuple-element.26.refs_4_), channel_id=1, source_target_pairs={{0,4},{4,0},{8,12},{12,8},{16,20},{20,16},{24,28},{28,24},{1,5},{5... | collective-permute-start | bytes 2359304 | tf_op jit(solution)/shard_map/ppermute | solution.py:44
  22.6 2.0 %collective-permute-start.9 = (bf16[64,2048]{1,0:T(8,128)(2,1)S(1)}, bf16[64,2048]{1,0:T(8,128)(2,1)}, u32[]{:S(2)}, u32[]{:S(2)}) collective-permute-start(bf16[64,2048]{1,0:T(8,128)(2,1)S(1)} %copy-done.16), channel_id=1, source_target_pairs={{0,16},{4,20},{8,24},{12,28},{16,0},{20,4},{24,8},{28,12},{1,17},{... | collective-permute-start | bytes 786440 | tf_op jit(solution)/shard_map/ppermute | solution.py:44
  24.6 0.6 %stripe_choice.2 = (bf16[256,512]{1,0:T(8,128)(2,1)S(1)}, bf16[256,512]{1,0:T(8,128)(2,1)S(1)}) custom-call(s32[2,4]{1,0:T(2,128)S(1)} %bitcast.4, bf16[256,512]{1,0:T(8,128)(2,1)S(1)} %get-tuple-element.18.refs_0_, bf16[256,512]{1,0:T(8,128)(2,1)S(1)} %get-tuple-element.19.refs_1_, bf16[256,512]{1,0:T(8,128)(2,1)S(1)} %collective-permute-done.1.refs_2_, ...), custom_call_target="tpu_custom_call" | custom-call | flops 2000000000 | tf_op jit(solution)/shard_map/stripe_choice/pallas_call | solution.py:159
  25.3 0.7 %collective-permute-start.7 = (bf16[256,512]{1,0:T(8,128)(2,1)S(1)}, bf16[256,512]{1,0:T(8,128)(2,1)S(1)}, u32[]{:S(2)}, u32[]{:S(2)}) collective-permute-start(bf16[256,512]{1,0:T(8,128)(2,1)S(1)} %get-tuple-element.21.refs_0_), channel_id=1, source_target_pairs={{0,16},{4,20},{8,24},{12,28},{16,0},{20,4},{24,8},{28,12},{1,17},{... | collective-permute-start | bytes 786440 | tf_op jit(solution)/shard_map/ppermute | solution.py:44
  26.0 1.6 %collective-permute-done.10.refs_5_.refs_1_ = bf16[256,512]{1,0:T(8,128)(2,1)} collective-permute-done((bf16[256,512]{1,0:T(8,128)(2,1)}, bf16[256,512]{1,0:T(8,128)(2,1)}, u32[]{:S(2)}, u32[]{:S(2)}) %collective-permute-start.10) | collective-permute-done | bytes 262176 | tf_op jit(solution)/shard_map/ppermute | solution.py:44
  27.5 1.5 %collective-permute-start.8 = (bf16[256,512]{1,0:T(8,128)(2,1)S(1)}, bf16[256,512]{1,0:T(8,128)(2,1)S(1)}, u32[]{:S(2)}, u32[]{:S(2)}) collective-permute-start(bf16[256,512]{1,0:T(8,128)(2,1)S(1)} %get-tuple-element.22.refs_1_), channel_id=1, source_target_pairs={{0,8},{4,12},{8,0},{12,4},{16,24},{20,28},{24,16},{28,20},{1,9},{5... | collective-permute-start | bytes 786440 | tf_op jit(solution)/shard_map/ppermute | solution.py:44
  29.0 2.9 %collective-permute-done.9.refs_4_.refs_0_ = bf16[64,2048]{1,0:T(8,128)(2,1)} collective-permute-done((bf16[64,2048]{1,0:T(8,128)(2,1)S(1)}, bf16[64,2048]{1,0:T(8,128)(2,1)}, u32[]{:S(2)}, u32[]{:S(2)}) %collective-permute-start.9) | collective-permute-done | bytes 262176 | tf_op jit(solution)/shard_map/ppermute | solution.py:44
  31.9 4.6 %collective-permute-done.7.refs_2_ = bf16[256,512]{1,0:T(8,128)(2,1)S(1)} collective-permute-done((bf16[256,512]{1,0:T(8,128)(2,1)S(1)}, bf16[256,512]{1,0:T(8,128)(2,1)S(1)}, u32[]{:S(2)}, u32[]{:S(2)}) %collective-permute-start.7) | collective-permute-done | bytes 262176 | tf_op jit(solution)/shard_map/ppermute | solution.py:44
  36.5 1.4 %stripe_choice.3.mine_ref = bf16[2,256,512]{2,1,0:T(8,128)(2,1)} custom-call(s32[2,4]{1,0:T(2,128)S(1)} %bitcast.5, bf16[256,512]{1,0:T(8,128)(2,1)S(1)} %get-tuple-element.21.refs_0_, bf16[256,512]{1,0:T(8,128)(2,1)S(1)} %get-tuple-element.22.refs_1_, bf16[256,512]{1,0:T(8,128)(2,1)S(1)} %collective-permute-done.7.refs_2_, ...), custom_call_target="tpu_custom_call" | custom-call | flops 2000000000 | tf_op jit(solution)/shard_map/stripe_choice/pallas_call | solution.py:159
  38.1 0.5 %collective-permute-start.14 = (bf16[64,2048]{1,0:T(8,128)(2,1)}, bf16[64,2048]{1,0:T(8,128)(2,1)}, u32[]{:S(2)}, u32[]{:S(2)}) collective-permute-start(bf16[64,2048]{1,0:T(8,128)(2,1)} %get-tuple-element.27.refs_2_), channel_id=1, source_target_pairs={{0,4},{4,0},{8,12},{12,8},{16,20},{20,16},{24,28},{28,24},{1,5},{5... | collective-permute-start | bytes 786440 | tf_op jit(solution)/shard_map/ppermute | solution.py:44
  38.6 0.3 copy-done.3
  38.9 0.5 %collective-permute-start.15 = (bf16[256,512]{1,0:T(8,128)(2,1)}, bf16[256,512]{1,0:T(8,128)(2,1)}, u32[]{:S(2)}, u32[]{:S(2)}) collective-permute-start(bf16[256,512]{1,0:T(8,128)(2,1)} %get-tuple-element.28.refs_6_), channel_id=1, source_target_pairs={{0,4},{4,0},{8,12},{12,8},{16,20},{20,16},{24,28},{28,24},{1,5},{5... | collective-permute-start | bytes 786440 | tf_op jit(solution)/shard_map/ppermute | solution.py:44
  39.4 1.0 %block_sums.1 = (f32[512,512]{1,0:T(8,128)S(1)}, f32[512,128]{1,0:T(8,128)S(1)}) custom-call(s32[1,2,4]{2,1,0:T(2,128)S(1)} %bitcast.7, bf16[1,4,128,128]{3,2,1,0:T(8,128)(2,1)S(1)} %get-tuple-element.23.tiles_ref, bf16[4,256,512]{2,1,0:T(8,128)(2,1)S(1)} %all-to-all-done.received_ref), custom_call_target="tpu_custom_call" | custom-call | bytes 2000000 | tf_op jit(solution)/shard_map/block_sums/pallas_call | solution.py:314
  40.5 2.4 %combined_rows.1.combined_ref = bf16[512,512]{1,0:T(8,128)(2,1)S(1)} custom-call(bf16[512,1024]{1,0:T(8,128)(2,1)S(1)} %get-tuple-element.17.refs_4_.dense_ref, bf16[2,256,512]{2,1,0:T(8,128)(2,1)} %stripe_choice.3.mine_ref, bf16[2,256,512]{2,1,0:T(8,128)(2,1)} %collective-permute-done.11.other_ref, f32[512,512]{1,0:T(8,128)S(1)} %get-tuple-element.24.total_ref, ...), custom_call_target="tpu_custom_call" | custom-call | bytes 4000000 | tf_op jit(solution)/shard_map/combined_rows/pallas_call | solution.py:342
  42.9 4.8 %layer.1 = bf16[512,512]{1,0:T(8,128)(2,1)} custom-call(bf16[512,512]{1,0:T(8,128)(2,1)S(1)} %combined_rows.1.combined_ref, bf16[3,64,2048]{2,1,0:T(8,128)(2,1)S(1)} %copy-done.10, bf16[3,64,2048]{2,1,0:T(8,128)(2,1)S(1)} %collective-permute-done.12.refs_2_.refs_1_, bf16[64,2048]{1,0:T(8,128)(2,1)} %get-tuple-element.27.refs_2_, ...), custom_call_target="tpu_custom_call" | custom-call | flops 99999997952 | bytes 4000000 | tf_op jit(solution)/shard_map/layer/pallas_call | solution.py:394
  (46 shorter events, 0.3 us)
Async XLA Ops:
  0.0 13.8 %copy-start.6 = (s32[4,2]{0,1:T(2,128)S(1)}, s32[4,2]{0,1:T(2,128)}, u32[]{:S(2)}) copy-start(s32[4,2]{0,1:T(2,128)} %param.9) | copy-start | bytes 100
  0.0 13.8 %collective-permute-start = (bf16[512,512]{1,0:T(8,128)(2,1)}, bf16[512,512]{1,0:T(8,128)(2,1)S(1)}, u32[]{:S(2)}, u32[]{:S(2)}) collective-permute-start(bf16[512,512]{1,0:T(8,128)(2,1)} %features_ref.3), channel_id=1, source_target_pairs={{0,4},{4,0},{8,12},{12,8},{16,20},{20,16},{24,28},{28,24},{1,5},{5... | collective-permute-start | bytes 1572872 | tf_op jit(solution)/shard_map/ppermute | solution.py:44
  0.5 15.6 %collective-permute-start.3 = (bf16[64,2048]{1,0:T(8,128)(2,1)}, bf16[64,2048]{1,0:T(8,128)(2,1)S(1)}, u32[]{:S(2)}, u32[]{:S(2)}) collective-permute-start(bf16[64,2048]{1,0:T(8,128)(2,1)} %refs_0_.1), channel_id=1, source_target_pairs={{0,8},{4,12},{8,0},{12,4},{16,24},{20,28},{24,16},{28,20},{1,9},{5... | collective-permute-start | bytes 786440 | tf_op jit(solution)/shard_map/ppermute | solution.py:44
  3.0 17.1 %collective-permute-start.6 = (bf16[256,512]{1,0:T(8,128)(2,1)}, bf16[256,512]{1,0:T(8,128)(2,1)}, u32[]{:S(2)}, u32[]{:S(2)}) collective-permute-start(bf16[256,512]{1,0:T(8,128)(2,1)} %refs_3_.1), channel_id=1, source_target_pairs={{0,16},{4,20},{8,24},{12,28},{16,0},{20,4},{24,8},{28,12},{1,17},{... | collective-permute-start | bytes 786440 | tf_op jit(solution)/shard_map/ppermute | solution.py:44
  4.6 16.1 %collective-permute-start.4 = (bf16[64,2048]{1,0:T(8,128)(2,1)}, bf16[64,2048]{1,0:T(8,128)(2,1)}, u32[]{:S(2)}, u32[]{:S(2)}) collective-permute-start(bf16[64,2048]{1,0:T(8,128)(2,1)} %refs_0_.1), channel_id=1, source_target_pairs={{0,16},{4,20},{8,24},{12,28},{16,0},{20,4},{24,8},{28,12},{1,17},{... | collective-permute-start | bytes 786440 | tf_op jit(solution)/shard_map/ppermute | solution.py:44
  5.0 15.7 %collective-permute-start.5 = (bf16[256,512]{1,0:T(8,128)(2,1)}, bf16[256,512]{1,0:T(8,128)(2,1)}, u32[]{:S(2)}, u32[]{:S(2)}) collective-permute-start(bf16[256,512]{1,0:T(8,128)(2,1)} %refs_3_.1), channel_id=1, source_target_pairs={{0,8},{4,12},{8,0},{12,4},{16,24},{20,28},{24,16},{28,20},{1,9},{5... | collective-permute-start | bytes 786440 | tf_op jit(solution)/shard_map/ppermute | solution.py:44
  5.1 1.0 %copy-start = (bf16[512,512]{1,0:T(8,128)(2,1)S(1)}, bf16[512,512]{1,0:T(8,128)(2,1)}, u32[]{:S(2)}) copy-start(bf16[512,512]{1,0:T(8,128)(2,1)} %features_ref.3) | copy-start | bytes 1572868
  6.8 7.0 %copy-start.1 = (bf16[512,512]{1,0:T(8,128)(2,1)S(1)}, bf16[512,512]{1,0:T(8,128)(2,1)}, u32[]{:S(2)}) copy-start(bf16[512,512]{1,0:T(8,128)(2,1)} %features_ref.3) | copy-start | bytes 1572868
  6.9 11.4 %copy-start.5 = (s32[1,4,128,128]{3,2,1,0:T(8,128)S(1)}, s32[1,4,128,128]{3,2,1,0:T(8,128)}, u32[]{:S(2)}) copy-start(s32[1,4,128,128]{3,2,1,0:T(8,128)} %tiles_ref.1) | copy-start | bytes 786436
  8.5 30.9 %all-to-all-start = ((bf16[4,256,512]{2,1,0:T(8,128)(2,1)}), bf16[4,256,512]{2,1,0:T(8,128)(2,1)S(1)}, u32[]{:S(2)}, u32[]{:S(2)}) async-start(bf16[4,256,512]{2,1,0:T(8,128)(2,1)} %pick_blocks.1), calls=%async_computation | async-start | bytes 2097152 | tf_op jit(solution)/shard_map/all_to_all | solution.py:456
  13.8 6.9 %copy-start.13 = (bf16[64,2048]{1,0:T(8,128)(2,1)S(1)}, bf16[64,2048]{1,0:T(8,128)(2,1)}, u32[]{:S(2)}) copy-start(bf16[64,2048]{1,0:T(8,128)(2,1)} %refs_0_.1) | copy-start | bytes 786436
  13.8 6.9 %copy-start.14 = (bf16[256,512]{1,0:T(8,128)(2,1)S(1)}, bf16[256,512]{1,0:T(8,128)(2,1)}, u32[]{:S(2)}) copy-start(bf16[256,512]{1,0:T(8,128)(2,1)} %refs_3_.1) | copy-start | bytes 786436
  14.5 8.2 %collective-permute-start.1 = (bf16[256,512]{1,0:T(8,128)(2,1)S(1)}, bf16[256,512]{1,0:T(8,128)(2,1)S(1)}, u32[]{:S(2)}, u32[]{:S(2)}) collective-permute-start(bf16[256,512]{1,0:T(8,128)(2,1)S(1)} %get-tuple-element.18.refs_0_), channel_id=1, source_target_pairs={{0,8},{4,12},{8,0},{12,4},{16,24},{20,28},{24,16},{28,20},{1,9},{5... | collective-permute-start | bytes 786440 | tf_op jit(solution)/shard_map/ppermute | solution.py:44
  16.7 7.9 %collective-permute-start.2 = (bf16[256,512]{1,0:T(8,128)(2,1)S(1)}, bf16[256,512]{1,0:T(8,128)(2,1)S(1)}, u32[]{:S(2)}, u32[]{:S(2)}) collective-permute-start(bf16[256,512]{1,0:T(8,128)(2,1)S(1)} %get-tuple-element.19.refs_1_), channel_id=1, source_target_pairs={{0,16},{4,20},{8,24},{12,28},{16,0},{20,4},{24,8},{28,12},{1,17},{... | collective-permute-start | bytes 786440 | tf_op jit(solution)/shard_map/ppermute | solution.py:44
  18.3 1.6 %copy-start.2 = (s32[512,1024]{1,0:T(8,128)S(1)}, s32[512,1024]{1,0:T(8,128)}, u32[]{:S(2)}) copy-start(s32[512,1024]{1,0:T(8,128)} %dense_ref.1) | copy-start | bytes 6291460
  19.9 0.9 %copy-start.16 = (bf16[64,2048]{1,0:T(8,128)(2,1)S(1)}, bf16[64,2048]{1,0:T(8,128)(2,1)}, u32[]{:S(2)}) copy-start(bf16[64,2048]{1,0:T(8,128)(2,1)} %copy-done.15) | copy-start | bytes 786436
  20.1 7.4 %collective-permute-start.10 = (bf16[256,512]{1,0:T(8,128)(2,1)}, bf16[256,512]{1,0:T(8,128)(2,1)}, u32[]{:S(2)}, u32[]{:S(2)}) collective-permute-start(bf16[256,512]{1,0:T(8,128)(2,1)} %collective-permute-done.6.refs_5_), channel_id=1, source_target_pairs={{0,8},{4,12},{8,0},{12,4},{16,24},{20,28},{24,16},{28,20},{1,9},{5... | collective-permute-start | bytes 786440 | tf_op jit(solution)/shard_map/ppermute | solution.py:44
  22.0 3.2 %copy-start.9 = (bf16[3,64,2048]{2,1,0:T(8,128)(2,1)}, bf16[3,64,2048]{2,1,0:T(8,128)(2,1)S(1)}, u32[]{:S(2)}) copy-start(bf16[3,64,2048]{2,1,0:T(8,128)(2,1)S(1)} %get-tuple-element.20.refs_5_.refs_0_) | copy-start | bytes 2359300
  22.0 3.2 %copy-start.11 = (bf16[3,256,512]{2,1,0:T(8,128)(2,1)}, bf16[3,256,512]{2,1,0:T(8,128)(2,1)S(1)}, u32[]{:S(2)}) copy-start(bf16[3,256,512]{2,1,0:T(8,128)(2,1)S(1)} %get-tuple-element.26.refs_4_) | copy-start | bytes 2359300
  22.1 16.0 %collective-permute-start.12 = (bf16[3,64,2048]{2,1,0:T(8,128)(2,1)S(1)}, bf16[3,64,2048]{2,1,0:T(8,128)(2,1)S(1)}, u32[]{:S(2)}, u32[]{:S(2)}) collective-permute-start(bf16[3,64,2048]{2,1,0:T(8,128)(2,1)S(1)} %get-tuple-element.20.refs_5_.refs_0_), channel_id=1, source_target_pairs={{0,4},{4,0},{8,12},{12,8},{16,20},{20,16},{24,28},{28,24},{1,5},{5... | collective-permute-start | bytes 2359304 | tf_op jit(solution)/shard_map/ppermute | solution.py:44
  22.1 15.9 %collective-permute-start.13 = (bf16[3,256,512]{2,1,0:T(8,128)(2,1)S(1)}, bf16[3,256,512]{2,1,0:T(8,128)(2,1)S(1)}, u32[]{:S(2)}, u32[]{:S(2)}) collective-permute-start(bf16[3,256,512]{2,1,0:T(8,128)(2,1)S(1)} %get-tuple-element.26.refs_4_), channel_id=1, source_target_pairs={{0,4},{4,0},{8,12},{12,8},{16,20},{20,16},{24,28},{28,24},{1,5},{5... | collective-permute-start | bytes 2359304 | tf_op jit(solution)/shard_map/ppermute | solution.py:44
  22.6 9.3 %collective-permute-start.9 = (bf16[64,2048]{1,0:T(8,128)(2,1)S(1)}, bf16[64,2048]{1,0:T(8,128)(2,1)}, u32[]{:S(2)}, u32[]{:S(2)}) collective-permute-start(bf16[64,2048]{1,0:T(8,128)(2,1)S(1)} %copy-done.16), channel_id=1, source_target_pairs={{0,16},{4,20},{8,24},{12,28},{16,0},{20,4},{24,8},{28,12},{1,17},{... | collective-permute-start | bytes 786440 | tf_op jit(solution)/shard_map/ppermute | solution.py:44
  25.3 11.3 %collective-permute-start.7 = (bf16[256,512]{1,0:T(8,128)(2,1)S(1)}, bf16[256,512]{1,0:T(8,128)(2,1)S(1)}, u32[]{:S(2)}, u32[]{:S(2)}) collective-permute-start(bf16[256,512]{1,0:T(8,128)(2,1)S(1)} %get-tuple-element.21.refs_0_), channel_id=1, source_target_pairs={{0,16},{4,20},{8,24},{12,28},{16,0},{20,4},{24,8},{28,12},{1,17},{... | collective-permute-start | bytes 786440 | tf_op jit(solution)/shard_map/ppermute | solution.py:44
  27.5 9.0 %collective-permute-start.8 = (bf16[256,512]{1,0:T(8,128)(2,1)S(1)}, bf16[256,512]{1,0:T(8,128)(2,1)S(1)}, u32[]{:S(2)}, u32[]{:S(2)}) collective-permute-start(bf16[256,512]{1,0:T(8,128)(2,1)S(1)} %get-tuple-element.22.refs_1_), channel_id=1, source_target_pairs={{0,8},{4,12},{8,0},{12,4},{16,24},{20,28},{24,16},{28,20},{1,9},{5... | collective-permute-start | bytes 786440 | tf_op jit(solution)/shard_map/ppermute | solution.py:44
  37.9 1.5 %copy-start.8 = (s32[1,4,2]{1,2,0:T(2,128)S(1)}, s32[1,4,2]{1,2,0:T(2,128)}, u32[]{:S(2)}) copy-start(s32[1,4,2]{1,2,0:T(2,128)} %param.13) | copy-start | bytes 100
  37.9 2.5 %collective-permute-start.11 = (bf16[2,256,512]{2,1,0:T(8,128)(2,1)}, bf16[2,256,512]{2,1,0:T(8,128)(2,1)}, u32[]{:S(2)}, u32[]{:S(2)}) collective-permute-start(bf16[2,256,512]{2,1,0:T(8,128)(2,1)} %stripe_choice.3.mine_ref), channel_id=1, source_target_pairs={{0,4},{4,0},{8,12},{12,8},{16,20},{20,16},{24,28},{28,24},{1,5},{5... | collective-permute-start | bytes 1572872 | tf_op jit(solution)/shard_map/ppermute | solution.py:44
  38.0 0.9 %copy-start.3 = (bf16[3,256,512]{2,1,0:T(8,128)(2,1)}, bf16[3,256,512]{2,1,0:T(8,128)(2,1)S(1)}, u32[]{:S(2)}) copy-start(bf16[3,256,512]{2,1,0:T(8,128)(2,1)S(1)} %collective-permute-done.13.refs_3_.refs_5_) | copy-start | bytes 2359300
  38.1 4.8 %collective-permute-start.14 = (bf16[64,2048]{1,0:T(8,128)(2,1)}, bf16[64,2048]{1,0:T(8,128)(2,1)}, u32[]{:S(2)}, u32[]{:S(2)}) collective-permute-start(bf16[64,2048]{1,0:T(8,128)(2,1)} %get-tuple-element.27.refs_2_), channel_id=1, source_target_pairs={{0,4},{4,0},{8,12},{12,8},{16,20},{20,16},{24,28},{28,24},{1,5},{5... | collective-permute-start | bytes 786440 | tf_op jit(solution)/shard_map/ppermute | solution.py:44
  38.9 4.0 %collective-permute-start.15 = (bf16[256,512]{1,0:T(8,128)(2,1)}, bf16[256,512]{1,0:T(8,128)(2,1)}, u32[]{:S(2)}, u32[]{:S(2)}) collective-permute-start(bf16[256,512]{1,0:T(8,128)(2,1)} %get-tuple-element.28.refs_6_), channel_id=1, source_target_pairs={{0,4},{4,0},{8,12},{12,8},{16,20},{20,16},{24,28},{28,24},{1,5},{5... | collective-permute-start | bytes 786440 | tf_op jit(solution)/shard_map/ppermute | solution.py:44
  40.5 2.4 %copy-start.4 = (bf16[3,256,512]{2,1,0:T(8,128)(2,1)S(1)}, bf16[3,256,512]{2,1,0:T(8,128)(2,1)}, u32[]{:S(2)}) copy-start(bf16[3,256,512]{2,1,0:T(8,128)(2,1)} %copy-done.3) | copy-start | bytes 2359300
  40.5 2.4 %copy-start.10 = (bf16[3,64,2048]{2,1,0:T(8,128)(2,1)S(1)}, bf16[3,64,2048]{2,1,0:T(8,128)(2,1)}, u32[]{:S(2)}) copy-start(bf16[3,64,2048]{2,1,0:T(8,128)(2,1)} %copy-done.9) | copy-start | bytes 2359300
  40.5 2.4 %copy-start.12 = (bf16[3,256,512]{2,1,0:T(8,128)(2,1)S(1)}, bf16[3,256,512]{2,1,0:T(8,128)(2,1)}, u32[]{:S(2)}) copy-start(bf16[3,256,512]{2,1,0:T(8,128)(2,1)} %copy-done.11) | copy-start | bytes 2359300
  (2 other events, 1.4 us)
